TPU v7x, 256 devices: a whole 4x4x8 slice. The times are simulated.
256 devices in a mesh: rep: 8 (over y, x_lo), blk: 32 (over x_hi, z, core).
Axes of the slice: x: 4 (x_hi: 2, x_lo: 2; x = x_hi * 2 + x_lo), y: 4, z: 8, core: 2. Of those that a mesh axis runs over, the one named last changes fastest.
Arguments:
- features: float32 [32, 1024, 128], P('blk', 'rep'), may hold values from -6 to 6
- weight: float32 [128, 256], replicated, may hold values from -0.5 to 0.5
- cotangent: float32 [32, 1024, 256], P('blk', 'rep'), may hold values from -6 to 6
- tile_vals: float32 [32, 8, 4, 32, 128, 128], P('blk', 'rep'), may hold values from 0.002 to 0.03
- tile_rows: int32 [32, 8, 4, 32], P('blk', 'rep'), may hold values from 0 to 7, as said below
- tile_cols: int32 [32, 8, 4, 32], P('blk', 'rep'), may hold values from 0 to 7
- tile_count: int32 [32, 8, 4], P('blk', 'rep'), may hold values from 4 to 32, as said below
Outputs:
- hidden: float32 [32, 1024, 256], P('blk', 'rep')
- feature_grad: float32 [32, 1024, 128], P('blk', 'rep')
Inputs may be any that keep to these rules, and one draw needn't show every extreme that they name: `tile_rows`: the 32 slots of one device and section name distinct tile positions (row, column). `tile_count`: every device has 32 live slots at some section.
All inputs are finite; a program needn't handle non-finite values.
Results may differ from a plain program's by a relative error of at most 0.0003.
Values sent between devices are 32-bit elements; how exact they have to be, the bound alone decides.
No kernel may reach another device: no remote copies, remote signals or barrier semaphores. Data moves between devices by JAX's collectives and lax.ppermute only.
A program may use at most 64 MiB of HBM per device.

v0:
```python
import functools

import jax
import jax.numpy as jnp
from jax import lax
from jax.experimental import pallas as pl
from jax.experimental.pallas import tpu as pltpu
from jax.sharding import PartitionSpec as P

F32 = jnp.float32
BF16 = jnp.bfloat16
HIGHEST = lax.Precision.HIGHEST
SIDE = 128
CHUNK = 8


def halves(value):
    high = value.astype(BF16)
    return high, (value - high.astype(F32)).astype(BF16)


def store_split(split, block, value):
    high, low = halves(value)
    split[block, :SIDE, :SIDE] = high
    split[block, SIDE:, :SIDE] = high
    split[block, :SIDE, SIDE:] = low
    split[block, SIDE:, SIDE:] = low


def clear(total):
    total[...] = jnp.zeros_like(total)


def forward_body(n_in, nblocks, has_start, choose, place, rows, cols, count, *refs):
    panels = refs[:n_in]
    tiles = refs[n_in]
    start = refs[n_in + 1] if has_start else None
    out, split, total = refs[-3:]
    part, chunk = pl.program_id(0), pl.program_id(1)
    section = place[part]

    @pl.when((part == 0) & (chunk == 0))
    def _():
        clear(total)

    for index in range(n_in - int(choose)):
        @pl.when((part == index) & (chunk == 0))
        def _(index=index):
            for block in range(nblocks):
                at = pl.ds(block * SIDE, SIDE)
                value = panels[index][at, :]
                if choose and index == n_in - 2:
                    value = jnp.where(place[3] == 0, value, panels[index + 1][at, :])
                store_split(split, block, value)

    for slot in range(CHUNK):
        number = chunk * CHUNK + slot
        row = jnp.where(number < count[section], rows[section, number], nblocks)
        col = cols[section, number] ^ place[2]
        left = jnp.concatenate(halves(tiles[0, slot]), axis=1)
        product = jnp.dot(left, split[col], preferred_element_type=F32)
        at = pl.ds(pl.multiple_of(row * SIDE, SIDE), SIDE)
        total[at, :] += product

    @pl.when((part == pl.num_programs(0) - 1) & (chunk == pl.num_programs(1) - 1))
    def _():
        live = pl.ds(0, nblocks * SIDE)
        value = total[live, :SIDE] + total[live, SIDE:]
        out[...] = value + start[...] if has_start else value


def forward_tiles(place, rows, cols, count, panels, tiles, start, choose):
    slots, nodes, features = tiles.shape[1], panels[0].shape[0], panels[0].shape[1]
    nblocks = nodes // SIDE
    parts = len(panels) - int(choose)
    whole = pl.BlockSpec((nodes, features), lambda i, j, *_: (0, 0))
    extra = [] if start is None else [start]
    return pl.pallas_call(
        functools.partial(forward_body, len(panels), nblocks, start is not None, choose),
        grid_spec=pltpu.PrefetchScalarGridSpec(
            num_scalar_prefetch=4,
            grid=(parts, slots // CHUNK),
            in_specs=[whole] * len(panels)
            + [pl.BlockSpec((1, CHUNK, SIDE, SIDE), lambda i, j, place, *_: (place[i], j, 0, 0))]
            + [whole] * len(extra),
            out_specs=whole,
            scratch_shapes=[
                pltpu.VMEM((nblocks, 2 * SIDE, 2 * SIDE), BF16),
                pltpu.VMEM((nodes + SIDE, 2 * features), F32),
            ],
        ),
        out_shape=jax.ShapeDtypeStruct((nodes, features), F32),
        compiler_params=pltpu.CompilerParams(vmem_limit_bytes=24 << 20),
        cost_estimate=pl.CostEstimate(
            flops=12 * parts * slots * SIDE * SIDE * features,
            bytes_accessed=4 * parts * slots * SIDE * SIDE,
            transcendentals=0,
        ),
    )(place, rows, cols, count, *panels, tiles, *extra)


def backward_body(parts, nblocks, place, rows, cols, count, panel, tiles, *refs):
    outs = refs[:parts]
    split, total = refs[parts:]
    part, chunk = pl.program_id(0), pl.program_id(1)
    section = place[part]

    @pl.when((part == 0) & (chunk == 0))
    def _():
        for block in range(nblocks):
            store_split(split, block, panel[pl.ds(block * SIDE, SIDE), :])

    @pl.when(chunk == 0)
    def _():
        clear(total)

    for slot in range(CHUNK):
        number = chunk * CHUNK + slot
        row = rows[section, number]
        col = jnp.where(number < count[section], cols[section, number] ^ place[2], nblocks)
        left = jnp.concatenate(halves(tiles[0, slot].T), axis=1)
        product = jnp.dot(left, split[row], preferred_element_type=F32)
        at = pl.ds(pl.multiple_of(col * SIDE, SIDE), SIDE)
        total[at, :] += product

    for index in range(parts):
        @pl.when((part == index) & (chunk == pl.num_programs(1) - 1))
        def _(index=index):
            live = pl.ds(0, nblocks * SIDE)
            outs[index][...] = total[live, :SIDE] + total[live, SIDE:]


def backward_tiles(place, rows, cols, count, panel, tiles, parts):
    slots, nodes, features = tiles.shape[1], panel.shape[0], panel.shape[1]
    nblocks = nodes // SIDE
    whole = pl.BlockSpec((nodes, features), lambda i, j, *_: (0, 0))
    return pl.pallas_call(
        functools.partial(backward_body, parts, nblocks),
        grid_spec=pltpu.PrefetchScalarGridSpec(
            num_scalar_prefetch=4,
            grid=(parts, slots // CHUNK),
            in_specs=[
                whole,
                pl.BlockSpec((1, CHUNK, SIDE, SIDE), lambda i, j, place, *_: (place[i], j, 0, 0)),
            ],
            out_specs=[whole] * parts,
            scratch_shapes=[
                pltpu.VMEM((nblocks, 2 * SIDE, 2 * SIDE), BF16),
                pltpu.VMEM((nodes + SIDE, 2 * features), F32),
            ],
        ),
        out_shape=[jax.ShapeDtypeStruct((nodes, features), F32)] * parts,
        compiler_params=pltpu.CompilerParams(vmem_limit_bytes=24 << 20),
        cost_estimate=pl.CostEstimate(
            flops=12 * parts * slots * SIDE * SIDE * features,
            bytes_accessed=4 * parts * slots * SIDE * SIDE,
            transcendentals=0,
        ),
    )(place, rows, cols, count, panel, tiles)


def dense_body(partials, weight, cotangent, hidden, spread):
    propagated = partials[0]
    for index in range(1, partials.shape[0]):
        propagated = propagated + partials[index]
    preact = jnp.dot(propagated, weight[...], precision=HIGHEST, preferred_element_type=F32)
    gate = 1.0 / (1.0 + jnp.exp(-preact))
    hidden[...] = preact * gate
    grad_pre = cotangent[...] * gate * (1.0 + preact * (1.0 - gate))
    grad = lax.dot_general(
        grad_pre, weight[...], (((1,), (1,)), ((), ())),
        precision=HIGHEST, preferred_element_type=F32,
    )
    for index in range(spread.shape[0]):
        spread[index] = grad


def dense(partials, weight, cotangent):
    return pl.pallas_call(
        dense_body,
        out_shape=[
            jax.ShapeDtypeStruct(cotangent.shape, F32),
            jax.ShapeDtypeStruct(partials.shape, F32),
        ],
    )(partials, weight, cotangent)


def shards(features, weight, cotangent, tile_vals, tile_rows, tile_cols, tile_count):
    replicas, groups = lax.axis_size("rep"), lax.axis_size("blk")
    sections = groups // replicas
    rep = lax.axis_index("rep")
    core = lax.axis_index("blk") % 2
    tiles, rows, cols, count = tile_vals[0, 0], tile_rows[0, 0], tile_cols[0, 0], tile_count[0, 0]
    near = jnp.stack([jnp.int32(2), 3 - 2 * core, rep, core]).astype(jnp.int32)
    far = jnp.stack([jnp.int32(0), 1 + 2 * core, rep, core]).astype(jnp.int32)
    fars = jnp.stack([1 + 2 * core, jnp.int32(0), rep, core]).astype(jnp.int32)

    def device(group, replica):
        return replica * groups + group % groups

    def joint(block, source):
        return lax.ppermute(
            block, ("rep", "blk"),
            [(device(*source(g, r)), device(g, r)) for r in range(replicas) for g in range(groups)],
        )

    def back(block, target):
        return lax.ppermute(
            block, ("rep", "blk"),
            [(device(g, r), device(*target(g, r))) for r in range(replicas) for g in range(groups)],
        )

    def along(block, distance, ids):
        return lax.ppermute(block, "blk", [(g, (g + distance) % groups) for g in ids])

    everyone, evens, odds = range(groups), range(0, groups, 2), range(1, groups, 2)
    twin = [(r ^ 1, r) for r in range(replicas)]
    swap = [(g ^ 1, g) for g in range(groups)]

    own = features[0]
    pair = jnp.concatenate([own, lax.ppermute(own, "rep", twin)])
    base = jnp.concatenate(
        [
            joint(pair, lambda g, r, k=k: (g + sections * r + 2, r ^ (2 * k)))
            for k in range(replicas // 2)
        ]
    )
    lower = along(base, 2, everyone)
    upper = along(base, -1, evens)
    beside = lax.ppermute(base, "blk", swap)
    partial_sum = forward_tiles(near, rows, cols, count, [base, beside], tiles, None, False)
    lower_beside = along(lower, -1, odds)
    partial_sum = forward_tiles(
        far, rows, cols, count, [lower, lower_beside, upper], tiles, partial_sum, True
    )
    partials = lax.all_to_all(
        partial_sum.reshape(replicas, -1, own.shape[-1]), "rep", 0, 0, tiled=True
    )
    hidden, spread = dense(partials, weight, cotangent[0])
    grad_panel = lax.all_to_all(spread, "rep", 0, 0, tiled=True).reshape(base.shape)
    (outer,) = backward_tiles(fars, rows, cols, count, grad_panel, tiles, 1)
    outer_in = along(outer, 1, evens)
    to_lower = along(outer, 1, odds)
    (lowest,) = backward_tiles(far, rows, cols, count, grad_panel, tiles, 1)
    from_upper = along(lowest + outer_in, -2, everyone)
    mine, other = backward_tiles(near, rows, cols, count, grad_panel, tiles, 2)
    total = mine + lax.ppermute(other, "blk", swap) + from_upper + to_lower
    parts = total.reshape(replicas // 2, -1, own.shape[-1])
    pair_sum = sum(
        back(parts[k], lambda g, r, k=k: (g + sections * r + 2, r ^ (2 * k)))
        for k in range(replicas // 2)
    )
    kept, sent = jnp.split(pair_sum, 2)
    feature_grad = kept + lax.ppermute(sent, "rep", twin)
    return hidden[None], feature_grad[None]


def solution(mesh):
    placed = (
        P("blk", "rep", None),
        P(),
        P("blk", "rep", None),
        P("blk", "rep", None, None, None, None),
        P("blk", "rep", None, None),
        P("blk", "rep", None, None),
        P("blk", "rep", None),
    )
    return jax.shard_map(
        shards,
        mesh=mesh,
        in_specs=placed,
        out_specs=(P("blk", "rep", None), P("blk", "rep", None)),
        check_vma=False,
    )
```

profile of v0, /device:TPU:26, one launch (start us, length us, event | category | flops | bytes accessed | tf_op | source)
XLA Modules:
  0.0 182.8 jit_solution(14851911608165066490)
XLA Ops:
  1.3 3.9 %collective-permute-done = f32[128,128]{1,0:T(8,128)S(1)} collective-permute-done((f32[128,128]{1,0:T(8,128)}, f32[128,128]{1,0:T(8,128)S(1)}, u32[]{:S(2)}, u32[]{:S(2)}) %collective-permute-start) | collective-permute-done | bytes 65568 | tf_op jit(solution)/shard_map/ppermute | solution.py:221
  8.1 6.7 %collective-permute-start.2 = (f32[256,128]{1,0:T(8,128)S(1)}, f32[256,128]{1,0:T(8,128)S(1)}, u32[]{:S(2)}, u32[]{:S(2)}) collective-permute-start(f32[256,128]{1,0:T(8,128)S(1)} %pad_maximum_fusion), channel_id=1, source_target_pairs={{66,0},{67,1},{68,2},{69,3},{70,4},{71,5},{72,6},{73,7},{74,8},{75... | collective-permute-start | bytes 393224 | tf_op jit(solution)/shard_map/ppermute | solution.py:202
  14.7 3.1 %collective-permute-start.3 = (f32[256,128]{1,0:T(8,128)S(1)}, f32[256,128]{1,0:T(8,128)S(1)}, u32[]{:S(2)}, u32[]{:S(2)}) collective-permute-start(f32[256,128]{1,0:T(8,128)S(1)} %pad_maximum_fusion), channel_id=1, source_target_pairs={{130,0},{131,1},{132,2},{133,3},{134,4},{135,5},{136,6},{137,7},{1... | collective-permute-start | bytes 393224 | tf_op jit(solution)/shard_map/ppermute | solution.py:202
  17.9 5.6 %collective-permute-start.4 = (f32[256,128]{1,0:T(8,128)S(1)}, f32[256,128]{1,0:T(8,128)S(1)}, u32[]{:S(2)}, u32[]{:S(2)}) collective-permute-start(f32[256,128]{1,0:T(8,128)S(1)} %pad_maximum_fusion), channel_id=1, source_target_pairs={{194,0},{195,1},{196,2},{197,3},{198,4},{199,5},{200,6},{201,7},{2... | collective-permute-start | bytes 393224 | tf_op jit(solution)/shard_map/ppermute | solution.py:202
  23.5 3.4 %collective-permute-done.3 = f32[256,128]{1,0:T(8,128)S(1)} collective-permute-done((f32[256,128]{1,0:T(8,128)S(1)}, f32[256,128]{1,0:T(8,128)S(1)}, u32[]{:S(2)}, u32[]{:S(2)}) %collective-permute-start.3) | collective-permute-done | bytes 131104 | tf_op jit(solution)/shard_map/ppermute | solution.py:202
  26.9 2.8 %collective-permute-done.4 = f32[256,128]{1,0:T(8,128)S(1)} collective-permute-done((f32[256,128]{1,0:T(8,128)S(1)}, f32[256,128]{1,0:T(8,128)S(1)}, u32[]{:S(2)}, u32[]{:S(2)}) %collective-permute-start.4) | collective-permute-done | bytes 131104 | tf_op jit(solution)/shard_map/ppermute | solution.py:202
  29.9 7.6 %collective-permute-start.7 = (f32[1024,128]{1,0:T(8,128)S(1)}, f32[1024,128]{1,0:T(8,128)S(1)}, u32[]{:S(2)}, u32[]{:S(2)}) collective-permute-start(f32[1024,128]{1,0:T(8,128)S(1)} %constant_dynamic-update-slice_fusion.refs_0_), channel_id=1, source_target_pairs={{0,31},{2,1},{4,3},{6,5},{8,7},{10,9},{12,11},{14,13},{16,15},{18,... | collective-permute-start | bytes 1572872 | tf_op jit(solution)/shard_map/ppermute | solution.py:214
  37.5 9.1 %collective-permute-done.5.refs_0_ = f32[1024,128]{1,0:T(8,128)S(1)} collective-permute-done((f32[1024,128]{1,0:T(8,128)S(1)}, f32[1024,128]{1,0:T(8,128)S(1)}, u32[]{:S(2)}, u32[]{:S(2)}) %collective-permute-start.5) | collective-permute-done | bytes 524320 | tf_op jit(solution)/shard_map/ppermute | solution.py:214
  48.1 3.4 %copy-done = f32[1,1,4,32,128,128]{5,4,3,2,1,0:T(8,128)S(1)} copy-done((f32[1,1,4,32,128,128]{5,4,3,2,1,0:T(8,128)S(1)}, f32[1,1,4,32,128,128]{5,4,3,2,1,0:T(8,128)}, u32[]{:S(2)}) %copy-start) | copy-done | bytes 8388632
  53.5 3.9 %shard_map.86.refs_4_ = f32[1024,128]{1,0:T(8,128)S(1)} custom-call(s32[4]{0:T(128)S(1)} %add_add_fusion.3.place, s32[4,32]{1,0:T(4,128)S(1)} %bitcast.24, s32[4,32]{1,0:T(4,128)S(1)} %bitcast.29, s32[4]{0:T(128)S(1)} %bitcast.34, f32[1024,128]{1,0:T(8,128)S(1)} %constant_dynamic-update-slice_fusion.refs_0_, f32[1024,128]{1,0:T(8,128)S(1)} %collective-permute-done.8.refs_1_, ...), custom_call_target="tpu_custom_call" | custom-call | flops 1610612736 | bytes 4194304 | tf_op jit(solution)/shard_map/pallas_call | solution.py:78
  57.4 3.8 %shard_map.87 = f32[1024,128]{1,0:T(8,128)S(1)} custom-call(s32[4]{0:T(128)S(1)} %add_add_fusion.2.place, s32[4,32]{1,0:T(4,128)S(1)} %bitcast.25, s32[4,32]{1,0:T(4,128)S(1)} %bitcast.30, s32[4]{0:T(128)S(1)} %bitcast.35, f32[1024,128]{1,0:T(8,128)S(1)} %collective-permute-done.5.refs_0_, f32[1024,128]{1,0:T(8,128)S(1)} %collective-permute-done.6.refs_1_, ...), custom_call_target="tpu_custom_call" | custom-call | flops 1610612736 | bytes 4194304 | tf_op jit(solution)/shard_map/pallas_call | solution.py:78
  61.2 17.7 %all_to_all.10.partials = f32[8,128,128]{2,1,0:T(8,128)} all-to-all(f32[8,128,128]{2,1,0:T(8,128)S(1)} %bitcast.23), channel_id=1, replica_groups=mesh['rep'=8,'blk'=32] {'rep'}, dimensions={0} | all-to-all | bytes 1048576 | tf_op jit(solution)/shard_map/all_to_all | solution.py:236
  81.5 6.1 %all-to-all-start.1 = ((f32[8,128,128]{2,1,0:T(8,128)}), f32[8,128,128]{2,1,0:T(8,128)S(1)}, u32[]{:S(2)}, u32[]{:S(2)}) async-start(f32[8,128,128]{2,1,0:T(8,128)} %get-tuple-element.7), calls=%async_computation.1 | async-start | bytes 1048576 | tf_op jit(solution)/shard_map/all_to_all | solution.py:240
  87.7 7.8 %all-to-all-done.1 = f32[8,128,128]{2,1,0:T(8,128)S(1)} async-done(((f32[8,128,128]{2,1,0:T(8,128)}), f32[8,128,128]{2,1,0:T(8,128)S(1)}, u32[]{:S(2)}, u32[]{:S(2)}) %all-to-all-start.1) | async-done | bytes 524320 | tf_op jit(solution)/shard_map/all_to_all | solution.py:240
  95.5 3.4 %copy-done.2 = f32[1,1,4,32,128,128]{5,4,3,2,1,0:T(8,128)S(1)} copy-done((f32[1,1,4,32,128,128]{5,4,3,2,1,0:T(8,128)S(1)}, f32[1,1,4,32,128,128]{5,4,3,2,1,0:T(8,128)}, u32[]{:S(2)}) %copy-start.2) | copy-done | bytes 8388632
  104.4 3.4 %copy-done.3 = f32[1,1,4,32,128,128]{5,4,3,2,1,0:T(8,128)S(1)} copy-done((f32[1,1,4,32,128,128]{5,4,3,2,1,0:T(8,128)S(1)}, f32[1,1,4,32,128,128]{5,4,3,2,1,0:T(8,128)}, u32[]{:S(2)}) %copy-start.3) | copy-done | bytes 8388632
  107.8 4.2 %shard_map.89 = (f32[1024,128]{1,0:T(8,128)S(1)}, f32[1024,128]{1,0:T(8,128)S(1)}) custom-call(s32[4]{0:T(128)S(1)} %add_add_fusion.3.place, s32[4,32]{1,0:T(4,128)S(1)} %bitcast.27, s32[4,32]{1,0:T(4,128)S(1)} %bitcast.32, s32[4]{0:T(128)S(1)} %bitcast.37, f32[1024,128]{1,0:T(8,128)S(1)} %bitcast.21, f32[4,32,128,128]{3,2,1,0:T(8,128)S(1)} %bitcast.18), custom_call_target="tpu_custom_call" | custom-call | flops 1610612736 | bytes 4194304 | tf_op jit(solution)/shard_map/pallas_call | solution.py:137
  112.1 3.4 %copy-done.4 = f32[1,1,4,32,128,128]{5,4,3,2,1,0:T(8,128)S(1)} copy-done((f32[1,1,4,32,128,128]{5,4,3,2,1,0:T(8,128)S(1)}, f32[1,1,4,32,128,128]{5,4,3,2,1,0:T(8,128)}, u32[]{:S(2)}) %copy-start.4) | copy-done | bytes 8388632
  118.0 6.4 %collective-permute-start.11 = (f32[1024,128]{1,0:T(8,128)S(1)}, f32[1024,128]{1,0:T(8,128)S(1)}, u32[]{:S(2)}, u32[]{:S(2)}) collective-permute-start(f32[1024,128]{1,0:T(8,128)S(1)} %add.35), channel_id=1, source_target_pairs={{0,30},{1,31},{2,0},{3,1},{4,2},{5,3},{6,4},{7,5},{8,6},{9,7},{10,... | collective-permute-start | bytes 1572872 | tf_op jit(solution)/shard_map/ppermute | solution.py:214
  124.4 11.4 %collective-permute-done.11 = f32[1024,128]{1,0:T(8,128)S(1)} collective-permute-done((f32[1024,128]{1,0:T(8,128)S(1)}, f32[1024,128]{1,0:T(8,128)S(1)}, u32[]{:S(2)}, u32[]{:S(2)}) %collective-permute-start.11) | collective-permute-done | bytes 524320 | tf_op jit(solution)/shard_map/ppermute | solution.py:214
  136.0 6.4 %collective-permute-start.13 = (f32[256,128]{1,0:T(8,128)S(1)}, f32[256,128]{1,0:T(8,128)S(1)}, u32[]{:S(2)}, u32[]{:S(2)}) collective-permute-start(f32[256,128]{1,0:T(8,128)S(1)} %get-tuple-element.13), channel_id=1, source_target_pairs={{0,2},{1,3},{2,4},{3,5},{4,6},{5,7},{6,8},{7,9},{8,10},{9,11},{10,... | collective-permute-start | bytes 393224 | tf_op jit(solution)/shard_map/ppermute | solution.py:208
  146.3 10.4 %collective-permute-done.14 = f32[256,128]{1,0:T(8,128)S(1)} collective-permute-done((f32[256,128]{1,0:T(8,128)S(1)}, f32[256,128]{1,0:T(8,128)S(1)}, u32[]{:S(2)}, u32[]{:S(2)}) %collective-permute-start.14) | collective-permute-done | bytes 131104 | tf_op jit(solution)/shard_map/ppermute | solution.py:208
  156.7 21.1 %collective-permute-done.16 = f32[256,128]{1,0:T(8,128)S(1)} collective-permute-done((f32[256,128]{1,0:T(8,128)S(1)}, f32[256,128]{1,0:T(8,128)S(1)}, u32[]{:S(2)}, u32[]{:S(2)}) %collective-permute-start.16) | collective-permute-done | bytes 131104 | tf_op jit(solution)/shard_map/ppermute | solution.py:208
  177.9 4.3 %collective-permute-done.17 = f32[128,128]{1,0:T(8,128)S(1)} collective-permute-done((f32[128,128]{1,0:T(8,128)S(1)}, f32[128,128]{1,0:T(8,128)S(1)}, u32[]{:S(2)}, u32[]{:S(2)}) %collective-permute-start.17) | collective-permute-done | bytes 65568 | tf_op jit(solution)/shard_map/ppermute | solution.py:254
  (57 shorter events, 22.9 us)
Async XLA Ops:
  0.6 56.8 %copy-start.6 = (s32[1,1,4,32]{3,2,1,0:T(4,128)S(1)}, s32[1,1,4,32]{3,2,1,0:T(4,128)}, u32[]{:S(2)}) copy-start(s32[1,1,4,32]{3,2,1,0:T(4,128)} %param.11) | copy-start | bytes 1540
  0.6 56.8 %copy-start.8 = (s32[1,1,4,32]{3,2,1,0:T(4,128)S(1)}, s32[1,1,4,32]{3,2,1,0:T(4,128)}, u32[]{:S(2)}) copy-start(s32[1,1,4,32]{3,2,1,0:T(4,128)} %param.12) | copy-start | bytes 1540
  0.7 4.6 %collective-permute-start = (f32[128,128]{1,0:T(8,128)}, f32[128,128]{1,0:T(8,128)S(1)}, u32[]{:S(2)}, u32[]{:S(2)}) collective-permute-start(f32[128,128]{1,0:T(8,128)} %bitcast.40), channel_id=1, source_target_pairs={{32,0},{0,32},{96,64},{64,96},{160,128},{128,160},{224,192},{192,2... | collective-permute-start | bytes 196616 | tf_op jit(solution)/shard_map/ppermute | solution.py:221
  6.1 17.4 %collective-permute-start.1 = (f32[256,128]{1,0:T(8,128)S(1)}, f32[256,128]{1,0:T(8,128)S(1)}, u32[]{:S(2)}, u32[]{:S(2)}) collective-permute-start(f32[256,128]{1,0:T(8,128)S(1)} %pad_maximum_fusion), channel_id=1, source_target_pairs={{2,0},{3,1},{4,2},{5,3},{6,4},{7,5},{8,6},{9,7},{10,8},{11,9},{12,... | collective-permute-start | bytes 393224 | tf_op jit(solution)/shard_map/ppermute | solution.py:202
  8.1 15.4 %collective-permute-start.2 = (f32[256,128]{1,0:T(8,128)S(1)}, f32[256,128]{1,0:T(8,128)S(1)}, u32[]{:S(2)}, u32[]{:S(2)}) collective-permute-start(f32[256,128]{1,0:T(8,128)S(1)} %pad_maximum_fusion), channel_id=1, source_target_pairs={{66,0},{67,1},{68,2},{69,3},{70,4},{71,5},{72,6},{73,7},{74,8},{75... | collective-permute-start | bytes 393224 | tf_op jit(solution)/shard_map/ppermute | solution.py:202
  14.7 12.2 %collective-permute-start.3 = (f32[256,128]{1,0:T(8,128)S(1)}, f32[256,128]{1,0:T(8,128)S(1)}, u32[]{:S(2)}, u32[]{:S(2)}) collective-permute-start(f32[256,128]{1,0:T(8,128)S(1)} %pad_maximum_fusion), channel_id=1, source_target_pairs={{130,0},{131,1},{132,2},{133,3},{134,4},{135,5},{136,6},{137,7},{1... | collective-permute-start | bytes 393224 | tf_op jit(solution)/shard_map/ppermute | solution.py:202
  17.9 11.9 %collective-permute-start.4 = (f32[256,128]{1,0:T(8,128)S(1)}, f32[256,128]{1,0:T(8,128)S(1)}, u32[]{:S(2)}, u32[]{:S(2)}) collective-permute-start(f32[256,128]{1,0:T(8,128)S(1)} %pad_maximum_fusion), channel_id=1, source_target_pairs={{194,0},{195,1},{196,2},{197,3},{198,4},{199,5},{200,6},{201,7},{2... | collective-permute-start | bytes 393224 | tf_op jit(solution)/shard_map/ppermute | solution.py:202
  29.7 16.9 %collective-permute-start.5 = (f32[1024,128]{1,0:T(8,128)S(1)}, f32[1024,128]{1,0:T(8,128)S(1)}, u32[]{:S(2)}, u32[]{:S(2)}) collective-permute-start(f32[1024,128]{1,0:T(8,128)S(1)} %constant_dynamic-update-slice_fusion.refs_0_), channel_id=1, source_target_pairs={{0,2},{1,3},{2,4},{3,5},{4,6},{5,7},{6,8},{7,9},{8,10},{9,11},{10,... | collective-permute-start | bytes 1572872 | tf_op jit(solution)/shard_map/ppermute | solution.py:214
  29.8 18.3 %collective-permute-start.8 = (f32[1024,128]{1,0:T(8,128)S(1)}, f32[1024,128]{1,0:T(8,128)S(1)}, u32[]{:S(2)}, u32[]{:S(2)}) collective-permute-start(f32[1024,128]{1,0:T(8,128)S(1)} %constant_dynamic-update-slice_fusion.refs_0_), channel_id=1, source_target_pairs={{1,0},{0,1},{3,2},{2,3},{5,4},{4,5},{7,6},{6,7},{9,8},{8,9},{11,10... | collective-permute-start | bytes 1572872 | tf_op jit(solution)/shard_map/ppermute | solution.py:230
  29.9 27.4 %collective-permute-start.7 = (f32[1024,128]{1,0:T(8,128)S(1)}, f32[1024,128]{1,0:T(8,128)S(1)}, u32[]{:S(2)}, u32[]{:S(2)}) collective-permute-start(f32[1024,128]{1,0:T(8,128)S(1)} %constant_dynamic-update-slice_fusion.refs_0_), channel_id=1, source_target_pairs={{0,31},{2,1},{4,3},{6,5},{8,7},{10,9},{12,11},{14,13},{16,15},{18,... | collective-permute-start | bytes 1572872 | tf_op jit(solution)/shard_map/ppermute | solution.py:214
  46.6 10.8 %collective-permute-start.6 = (f32[1024,128]{1,0:T(8,128)S(1)}, f32[1024,128]{1,0:T(8,128)S(1)}, u32[]{:S(2)}, u32[]{:S(2)}) collective-permute-start(f32[1024,128]{1,0:T(8,128)S(1)} %collective-permute-done.5.refs_0_), channel_id=1, source_target_pairs={{1,0},{3,2},{5,4},{7,6},{9,8},{11,10},{13,12},{15,14},{17,16},{19,... | collective-permute-start | bytes 1572872 | tf_op jit(solution)/shard_map/ppermute | solution.py:214
  48.1 3.4 %copy-start = (f32[1,1,4,32,128,128]{5,4,3,2,1,0:T(8,128)S(1)}, f32[1,1,4,32,128,128]{5,4,3,2,1,0:T(8,128)}, u32[]{:S(2)}) copy-start(f32[1,1,4,32,128,128]{5,4,3,2,1,0:T(8,128)} %param.10) | copy-start | bytes 25165828
  53.5 3.9 %copy-start.1 = (f32[1,1,4,32,128,128]{5,4,3,2,1,0:T(8,128)S(1)}, f32[1,1,4,32,128,128]{5,4,3,2,1,0:T(8,128)}, u32[]{:S(2)}) copy-start(f32[1,1,4,32,128,128]{5,4,3,2,1,0:T(8,128)} %param.10) | copy-start | bytes 25165828
  57.4 38.1 %copy-start.10 = (s32[1,1,4]{2,1,0:T(1,128)S(1)}, s32[1,1,4]{2,1,0:T(1,128)}, u32[]{:S(2)}) copy-start(s32[1,1,4]{2,1,0:T(1,128)} %param.13) | copy-start | bytes 52
  81.5 14.0 %all-to-all-start.1 = ((f32[8,128,128]{2,1,0:T(8,128)}), f32[8,128,128]{2,1,0:T(8,128)S(1)}, u32[]{:S(2)}, u32[]{:S(2)}) async-start(f32[8,128,128]{2,1,0:T(8,128)} %get-tuple-element.7), calls=%async_computation.1 | async-start | bytes 1048576 | tf_op jit(solution)/shard_map/all_to_all | solution.py:240
  101.3 16.7 %collective-permute-start.10 = (f32[1024,128]{1,0:T(8,128)S(1)}, f32[1024,128]{1,0:T(8,128)S(1)}, u32[]{:S(2)}, u32[]{:S(2)}) collective-permute-start(f32[1024,128]{1,0:T(8,128)S(1)} %shard_map.91), channel_id=1, source_target_pairs={{0,1},{2,3},{4,5},{6,7},{8,9},{10,11},{12,13},{14,15},{16,17},{18,... | collective-permute-start | bytes 1572872 | tf_op jit(solution)/shard_map/ppermute | solution.py:214
  103.1 21.3 %collective-permute-start.12 = (f32[1024,128]{1,0:T(8,128)S(1)}, f32[1024,128]{1,0:T(8,128)S(1)}, u32[]{:S(2)}, u32[]{:S(2)}) collective-permute-start(f32[1024,128]{1,0:T(8,128)S(1)} %shard_map.91), channel_id=1, source_target_pairs={{1,2},{3,4},{5,6},{7,8},{9,10},{11,12},{13,14},{15,16},{17,18},{19... | collective-permute-start | bytes 1572872 | tf_op jit(solution)/shard_map/ppermute | solution.py:214
  112.0 12.5 %collective-permute-start.9 = (f32[1024,128]{1,0:T(8,128)S(1)}, f32[1024,128]{1,0:T(8,128)S(1)}, u32[]{:S(2)}, u32[]{:S(2)}) collective-permute-start(f32[1024,128]{1,0:T(8,128)S(1)} %get-tuple-element.9), channel_id=1, source_target_pairs={{1,0},{0,1},{3,2},{2,3},{5,4},{4,5},{7,6},{6,7},{9,8},{8,9},{11,10... | collective-permute-start | bytes 1572872 | tf_op jit(solution)/shard_map/ppermute | solution.py:247
  118.0 17.8 %collective-permute-start.11 = (f32[1024,128]{1,0:T(8,128)S(1)}, f32[1024,128]{1,0:T(8,128)S(1)}, u32[]{:S(2)}, u32[]{:S(2)}) collective-permute-start(f32[1024,128]{1,0:T(8,128)S(1)} %add.35), channel_id=1, source_target_pairs={{0,30},{1,31},{2,0},{3,1},{4,2},{5,3},{6,4},{7,5},{8,6},{9,7},{10,... | collective-permute-start | bytes 1572872 | tf_op jit(solution)/shard_map/ppermute | solution.py:214
  136.0 10.3 %collective-permute-start.13 = (f32[256,128]{1,0:T(8,128)S(1)}, f32[256,128]{1,0:T(8,128)S(1)}, u32[]{:S(2)}, u32[]{:S(2)}) collective-permute-start(f32[256,128]{1,0:T(8,128)S(1)} %get-tuple-element.13), channel_id=1, source_target_pairs={{0,2},{1,3},{2,4},{3,5},{4,6},{5,7},{6,8},{7,9},{8,10},{9,11},{10,... | collective-permute-start | bytes 393224 | tf_op jit(solution)/shard_map/ppermute | solution.py:208
  142.3 14.3 %collective-permute-start.14 = (f32[256,128]{1,0:T(8,128)S(1)}, f32[256,128]{1,0:T(8,128)S(1)}, u32[]{:S(2)}, u32[]{:S(2)}) collective-permute-start(f32[256,128]{1,0:T(8,128)S(1)} %get-tuple-element.10), channel_id=1, source_target_pairs={{0,66},{1,67},{2,68},{3,69},{4,70},{5,71},{6,72},{7,73},{8,74},{9,... | collective-permute-start | bytes 393224 | tf_op jit(solution)/shard_map/ppermute | solution.py:208
  142.3 14.3 %collective-permute-start.15 = (f32[256,128]{1,0:T(8,128)S(1)}, f32[256,128]{1,0:T(8,128)S(1)}, u32[]{:S(2)}, u32[]{:S(2)}) collective-permute-start(f32[256,128]{1,0:T(8,128)S(1)} %get-tuple-element.12), channel_id=1, source_target_pairs={{0,130},{1,131},{2,132},{3,133},{4,134},{5,135},{6,136},{7,137},{8... | collective-permute-start | bytes 393224 | tf_op jit(solution)/shard_map/ppermute | solution.py:208
  144.7 33.1 %collective-permute-start.16 = (f32[256,128]{1,0:T(8,128)S(1)}, f32[256,128]{1,0:T(8,128)S(1)}, u32[]{:S(2)}, u32[]{:S(2)}) collective-permute-start(f32[256,128]{1,0:T(8,128)S(1)} %get-tuple-element.11), channel_id=1, source_target_pairs={{0,194},{1,195},{2,196},{3,197},{4,198},{5,199},{6,200},{7,201},{8... | collective-permute-start | bytes 393224 | tf_op jit(solution)/shard_map/ppermute | solution.py:208
  177.8 4.4 %collective-permute-start.17 = (f32[128,128]{1,0:T(8,128)S(1)}, f32[128,128]{1,0:T(8,128)S(1)}, u32[]{:S(2)}, u32[]{:S(2)}) collective-permute-start(f32[128,128]{1,0:T(8,128)S(1)} %split.9), channel_id=1, source_target_pairs={{32,0},{0,32},{96,64},{64,96},{160,128},{128,160},{224,192},{192,2... | collective-permute-start | bytes 196616 | tf_op jit(solution)/shard_map/ppermute | solution.py:254
  (6 other events, 12.2 us)
where the time goes:
time: 183 us
  waiting for transfers between devices  74.5 us (41%)
  starting transfers between devices  52.9 us (29%)
  Pallas kernels  19.3 us (11%)
  blocking collectives  17.7 us (10%)
  local copies, waits for them, and re-layouts  15.6 us (9%)
  other arithmetic  1.93 us (1%)
    ppermute x4, waiting for transfers between devices, back(): lax.ppermute(block, ('rep', 'blk'), [(device(g, r), device(*target(g, r))...  31.8 us
    ppermute x6, waiting for transfers between devices, along(): lax.ppermute(block, 'blk', [(g, (g + distance) % groups) for g in ids])  20.5 us
    ppermute x6, starting transfers between devices, along(): lax.ppermute(block, 'blk', [(g, (g + distance) % groups) for g in ids])  18.4 us
    all_to_all x1, blocking collectives, shards(): lax.all_to_all(partial_sum.reshape(replicas, -1, own.shape[-1]), 'rep', 0...  17.7 us
    ppermute x4, starting transfers between devices, joint(): lax.ppermute(block, ('rep', 'blk'), [(device(*source(g, r)), device(g, r)...  17.4 us
    unnamed x25, local copies, waits for them, and re-layouts  15.6 us
    ppermute x4, starting transfers between devices, back(): lax.ppermute(block, ('rep', 'blk'), [(device(g, r), device(*target(g, r))...  9.97 us
    pallas_call x3, Pallas kernels, backward_tiles(): pl.pallas_call(functools.partial(backward_body, parts, nblocks), grid_spe...  9.06 us
  transfers between devices with their start and end apart: 19, of which 10 were waited for; matrix products, arithmetic and copies ran while one was open for 0% of the time, Pallas kernels for 6%

commit v1 on v0

v1 whole, which is shorter than its diff:
```python
import functools

import jax
import jax.numpy as jnp
from jax import lax
from jax.experimental import pallas as pl
from jax.experimental.pallas import tpu as pltpu
from jax.sharding import PartitionSpec as P

F32 = jnp.float32
BF16 = jnp.bfloat16
HIGHEST = lax.Precision.HIGHEST
SIDE = 128
CHUNK = 8
NEAR, FAR, OUTER, LOWEST, CORE = 0, 2, 3, 2, 4


def halves(value):
    high = value.astype(BF16)
    return high, (value - high.astype(F32)).astype(BF16)


def store_split(split, block, value):
    high, low = halves(value)
    split[block, :SIDE, :SIDE] = high
    split[block, SIDE:, :SIDE] = high
    split[block, :SIDE, SIDE:] = low
    split[block, SIDE:, SIDE:] = low


def tile_copies(parts, first, info, tiles, held, sems):
    chunks = held.shape[1] // CHUNK

    def copy(part, chunk):
        at = pl.ds(pl.multiple_of(chunk * CHUNK, CHUNK), CHUNK)
        return pltpu.make_async_copy(
            tiles.at[info[0, first + part], at], held.at[part, at], sems.at[part, chunk]
        )

    for part in range(parts):
        for chunk in range(chunks):
            copy(part, chunk).start()
    return copy, chunks


def multiply(part, section, copy, chunks, info, source, target, transposed, held, split, total):
    @pl.loop(0, chunks)
    def _(chunk):
        copy(part, chunk).wait()
        for slot in range(CHUNK):
            number = chunk * CHUNK + slot
            tile = held[part, number]
            left = jnp.concatenate(halves(tile.T if transposed else tile), axis=1)
            right = split[info[source + section, number]]
            product = jnp.dot(left, right, preferred_element_type=F32)
            row = info[target + section, number] * SIDE
            total[pl.ds(pl.multiple_of(row, SIDE), SIDE), :] += product


def folded(total, nodes):
    live = pl.ds(0, nodes)
    return total[live, :SIDE] + total[live, SIDE:]


def forward_body(n_in, has_start, choose, first, info, *refs):
    panels, tiles = refs[:n_in], refs[n_in]
    out, split, total, held, sems = refs[-5:]
    nodes, parts = out.shape[0], n_in - int(choose)
    sections = info.shape[0] // 4
    copy, chunks = tile_copies(parts, first, info, tiles, held, sems)
    total[...] = jnp.zeros_like(total)
    for part in range(parts):
        for block in range(nodes // SIDE):
            at = pl.ds(block * SIDE, SIDE)
            value = panels[part][at, :]
            if choose and part == parts - 1:
                value = jnp.where(info[0, CORE] == 0, value, panels[parts][at, :])
            store_split(split, block, value)
        multiply(
            part, info[0, first + part], copy, chunks, info, 1 + sections, 1, False,
            held, split, total,
        )
    value = folded(total, nodes)
    out[...] = value + refs[n_in + 1][...] if has_start else value


def backward_body(parts, first, info, panel, tiles, *refs):
    outs = refs[:parts]
    split, total, held, sems = refs[parts:]
    nodes = panel.shape[0]
    sections = info.shape[0] // 4
    copy, chunks = tile_copies(parts, first, info, tiles, held, sems)
    for block in range(nodes // SIDE):
        store_split(split, block, panel[pl.ds(block * SIDE, SIDE), :])
    for part in range(parts):
        total[...] = jnp.zeros_like(total)
        multiply(
            part, info[0, first + part], copy, chunks, info, 1 + 2 * sections, 1 + 3 * sections,
            True, held, split, total,
        )
        outs[part][...] = folded(total, nodes)


def tile_call(body, parts, info, panels, tiles, extra, n_out, cost):
    slots, (nodes, features) = tiles.shape[1], panels[0].shape
    whole = pl.BlockSpec(memory_space=pltpu.VMEM)
    return pl.pallas_call(
        body,
        in_specs=[pl.BlockSpec(memory_space=pltpu.SMEM)]
        + [whole] * len(panels)
        + [pl.BlockSpec(memory_space=pltpu.HBM)]
        + [whole] * len(extra),
        out_specs=[whole] * n_out,
        scratch_shapes=[
            pltpu.VMEM((nodes // SIDE, 2 * SIDE, 2 * SIDE), BF16),
            pltpu.VMEM((nodes + SIDE, 2 * features), F32),
            pltpu.VMEM((parts, slots, SIDE, SIDE), F32),
            pltpu.SemaphoreType.DMA((parts, slots // CHUNK)),
        ],
        out_shape=[jax.ShapeDtypeStruct((nodes, features), F32)] * n_out,
        compiler_params=pltpu.CompilerParams(vmem_limit_bytes=50 << 20),
        cost_estimate=pl.CostEstimate(
            flops=cost * parts * slots * SIDE * SIDE * features,
            bytes_accessed=4 * parts * slots * SIDE * SIDE,
            transcendentals=0,
        ),
    )(info, *panels, tiles, *extra)


def forward_tiles(first, info, panels, tiles, start, choose):
    extra = [] if start is None else [start]
    body = functools.partial(forward_body, len(panels), start is not None, choose, first)
    return tile_call(body, len(panels) - int(choose), info, panels, tiles, extra, 1, 32)[0]


def backward_tiles(first, info, panel, tiles, parts, cost=32):
    body = functools.partial(backward_body, parts, first)
    return tile_call(body, parts, info, [panel], tiles, [], parts, cost)


def dense_body(partials, weight, cotangent, hidden, spread):
    propagated = partials[0]
    for index in range(1, partials.shape[0]):
        propagated = propagated + partials[index]
    preact = jnp.dot(propagated, weight[...], precision=HIGHEST, preferred_element_type=F32)
    gate = 1.0 / (1.0 + jnp.exp(-preact))
    hidden[...] = preact * gate
    grad_pre = cotangent[...] * gate * (1.0 + preact * (1.0 - gate))
    grad = lax.dot_general(
        grad_pre, weight[...], (((1,), (1,)), ((), ())),
        precision=HIGHEST, preferred_element_type=F32,
    )
    for index in range(spread.shape[0]):
        spread[index] = grad


def dense(partials, weight, cotangent):
    return pl.pallas_call(
        dense_body,
        out_shape=[
            jax.ShapeDtypeStruct(cotangent.shape, F32),
            jax.ShapeDtypeStruct(partials.shape, F32),
        ],
    )(partials, weight, cotangent)


def shards(features, weight, cotangent, tile_vals, tile_rows, tile_cols, tile_count):
    replicas, groups = lax.axis_size("rep"), lax.axis_size("blk")
    sections = groups // replicas
    rep = lax.axis_index("rep")
    core = lax.axis_index("blk") % 2
    tiles, rows, cols, count = tile_vals[0, 0], tile_rows[0, 0], tile_cols[0, 0], tile_count[0, 0]
    slots = rows.shape[-1]
    live = lax.broadcasted_iota(jnp.int32, rows.shape, 1) < count[:, None]
    lane = lax.broadcasted_iota(jnp.int32, (1, slots), 1)
    plan = jnp.where(lane == 0, 2, 0)
    plan = jnp.where(lane == 1, 3 - 2 * core, plan)
    plan = jnp.where(lane == 3, 1 + 2 * core, plan)
    plan = jnp.where(lane == CORE, core, plan)
    spare = replicas
    info = jnp.concatenate(
        [plan, jnp.where(live, rows, spare), cols ^ rep, rows, jnp.where(live, cols ^ rep, spare)]
    )

    def device(group, replica):
        return replica * groups + group % groups

    def joint(block, source):
        return lax.ppermute(
            block, ("rep", "blk"),
            [(device(*source(g, r)), device(g, r)) for r in range(replicas) for g in range(groups)],
        )

    def back(block, target):
        return lax.ppermute(
            block, ("rep", "blk"),
            [(device(g, r), device(*target(g, r))) for r in range(replicas) for g in range(groups)],
        )

    def along(block, distance, ids):
        return lax.ppermute(block, "blk", [(g, (g + distance) % groups) for g in ids])

    everyone, evens, odds = range(groups), range(0, groups, 2), range(1, groups, 2)
    twin = [(r ^ 1, r) for r in range(replicas)]
    swap = [(g ^ 1, g) for g in range(groups)]

    own = features[0]
    nodes = own.shape[0]
    pair = lax.dynamic_update_slice(
        jnp.concatenate([own, own]), lax.ppermute(own, "rep", twin), (nodes, 0)
    )
    base = jnp.concatenate(
        [
            joint(pair, lambda g, r, k=k: (g + sections * r + 2, r ^ (2 * k)))
            for k in range(replicas // 2)
        ]
    )
    lower = along(base, 2, everyone)
    upper = along(base, -1, evens)
    beside = lax.ppermute(base, "blk", swap)
    partial_sum = forward_tiles(NEAR, info, [base, beside], tiles, None, False)
    lower, partial_sum = lax.optimization_barrier((lower, partial_sum))
    lower_beside = along(lower, -1, odds)
    partial_sum = forward_tiles(
        FAR, info, [lower, lower_beside, upper], tiles, partial_sum, True
    )
    partials = lax.all_to_all(
        partial_sum.reshape(replicas, -1, own.shape[-1]), "rep", 0, 0, tiled=True
    )
    hidden, spread = dense(partials, weight, cotangent[0])
    grad_panel = lax.all_to_all(spread, "rep", 0, 0, tiled=True).reshape(base.shape)
    (outer,) = backward_tiles(OUTER, info, grad_panel, tiles, 1)
    outer_in = along(outer, 1, evens)
    to_lower = along(outer, 1, odds)
    (lowest,) = backward_tiles(LOWEST, info, grad_panel, tiles, 1)
    combined = lowest + outer_in
    from_upper = along(combined, -2, everyone)
    late_panel, _ = lax.optimization_barrier((grad_panel, combined))
    mine, other = backward_tiles(NEAR, info, late_panel, tiles, 2)
    other, from_upper = lax.optimization_barrier((other, from_upper))
    total = mine + lax.ppermute(other, "blk", swap) + from_upper + to_lower
    parts = total.reshape(replicas // 2, -1, own.shape[-1])
    pair_sum = 0.0
    for k in range(replicas // 2):
        part = parts[k]
        if k:
            part = lax.ppermute(part, "rep", [(r, r ^ (2 * k)) for r in range(replicas)])
        pair_sum = pair_sum + back(
            part, lambda g, r, k=k: (g + sections * (r ^ (2 * k)) + 2, r)
        )
    kept, sent = jnp.split(pair_sum, 2)
    feature_grad = kept + lax.ppermute(sent, "rep", twin)
    return hidden[None], feature_grad[None]


def solution(mesh):
    placed = (
        P("blk", "rep", None),
        P(),
        P("blk", "rep", None),
        P("blk", "rep", None, None, None, None),
        P("blk", "rep", None, None),
        P("blk", "rep", None, None),
        P("blk", "rep", None),
    )
    return jax.shard_map(
        shards,
        mesh=mesh,
        in_specs=placed,
        out_specs=(P("blk", "rep", None), P("blk", "rep", None)),
        check_vma=False,
    )
```

time: 183 us -> 147 us (0.80)
  waiting for transfers between devices: 74.5 us -> 46.2 us
  local copies, waits for them, and re-layouts: 15.6 us -> 0.93 us
  blocking collectives: 17.7 us -> 31.3 us
  starting transfers between devices: 52.9 us -> 40.1 us
  Pallas kernels: 19.3 us -> 23.7 us
    unnamed x25 -> x3, local copies, waits for them, and re-layouts: 15.6 us -> 0.03 us
    ppermute x4, waiting for transfers between devices: 31.8 us -> 16.4 us  [back(): lax.ppermute(block, ('rep', 'blk'), [(device(g, r), device(*target(g, r))...]
    all_to_all x0 -> x1, blocking collectives: none -> 12.6 us  [shards(): lax.all_to_all(spread, 'rep', 0, 0, tiled=True).reshape(base.shape)]
    all_to_all x1 -> x0, waiting for transfers between devices: 7.76 us -> none  [shards(): lax.all_to_all(spread, 'rep', 0, 0, tiled=True).reshape(base.shape)]
    ppermute x6, starting transfers between devices: 18.4 us -> 11.7 us  [along(): lax.ppermute(block, 'blk', [(g, (g + distance) % groups) for g in ids])]
    all_to_all x1 -> x0, starting transfers between devices: 6.12 us -> none  [shards(): lax.all_to_all(spread, 'rep', 0, 0, tiled=True).reshape(base.shape)]
    ppermute x6, waiting for transfers between devices: 20.5 us -> 14.5 us  [along(): lax.ppermute(block, 'blk', [(g, (g + distance) % groups) for g in ids])]
    ppermute x1 -> x4, starting transfers between devices: 0.62 us -> 5.4 us  [the longest x3 4.78 us: shards(): part = lax.ppermute(part, 'rep', [(r, r ^ 2 * k) for r in range(replicas)])]
  transfers between devices with their start and end apart: 19 -> 21, of which waited for: 10 -> 12; matrix products, arithmetic and copies ran while one was open for 0% -> 2% of each run, Pallas kernels for 6% -> 9%
where the time goes in v1:
time: 147 us; the launch traced here: 146 us
  waiting for transfers between devices  46.2 us (31%)
  starting transfers between devices  40.1 us (27%)
  blocking collectives  31.3 us (21%)
  Pallas kernels  23.7 us (16%)
  other arithmetic  2.53 us (2%)
    pallas_call x5, Pallas kernels, tile_call(): pl.pallas_call(body, in_specs=[pl.BlockSpec(memory_space=pltpu.SMEM)] + [...  21 us
    all_to_all x1, blocking collectives, shards(): lax.all_to_all(partial_sum.reshape(replicas, -1, own.shape[-1]), 'rep', 0...  18.7 us
    ppermute x4, starting transfers between devices, joint(): lax.ppermute(block, ('rep', 'blk'), [(device(*source(g, r)), device(g, r)...  17.3 us
    ppermute x4, waiting for transfers between devices, back(): lax.ppermute(block, ('rep', 'blk'), [(device(g, r), device(*target(g, r))...  16.4 us
    ppermute x6, waiting for transfers between devices, along(): lax.ppermute(block, 'blk', [(g, (g + distance) % groups) for g in ids])  14.5 us
    all_to_all x1, blocking collectives, shards(): lax.all_to_all(spread, 'rep', 0, 0, tiled=True).reshape(base.shape)  12.6 us
    ppermute x6, starting transfers between devices, along(): lax.ppermute(block, 'blk', [(g, (g + distance) % groups) for g in ids])  11.7 us
    ppermute x4, waiting for transfers between devices, joint(): lax.ppermute(block, ('rep', 'blk'), [(device(*source(g, r)), device(g, r)...  6.23 us
  transfers between devices with their start and end apart: 21, of which 12 were waited for; matrix products, arithmetic and copies ran while one was open for 2% of the time, Pallas kernels for 9%

profile of v1, /device:TPU:26, one launch (start us, length us, event | category | flops | bytes accessed | tf_op | source)
XLA Modules:
  0.0 145.5 jit_solution(9697745135243784937)
XLA Ops:
  2.2 3.0 %collective-permute-done = f32[128,128]{1,0:T(8,128)S(1)} collective-permute-done((f32[128,128]{1,0:T(8,128)}, f32[128,128]{1,0:T(8,128)S(1)}, u32[]{:S(2)}, u32[]{:S(2)}) %collective-permute-start) | collective-permute-done | bytes 65568 | tf_op jit(solution)/shard_map/ppermute | solution.py:210
  5.2 1.9 %collective-permute-start.1 = (f32[256,128]{1,0:T(8,128)S(1)}, f32[256,128]{1,0:T(8,128)S(1)}, u32[]{:S(2)}, u32[]{:S(2)}) collective-permute-start(f32[256,128]{1,0:T(8,128)S(1)} %constant_dynamic-update-slice_fusion.4), channel_id=1, source_target_pairs={{2,0},{3,1},{4,2},{5,3},{6,4},{7,5},{8,6},{9,7},{10,8},{11,9},{12,... | collective-permute-start | bytes 393224 | tf_op jit(solution)/shard_map/ppermute | solution.py:189
  7.1 6.7 %collective-permute-start.2 = (f32[256,128]{1,0:T(8,128)S(1)}, f32[256,128]{1,0:T(8,128)S(1)}, u32[]{:S(2)}, u32[]{:S(2)}) collective-permute-start(f32[256,128]{1,0:T(8,128)S(1)} %constant_dynamic-update-slice_fusion.4), channel_id=1, source_target_pairs={{66,0},{67,1},{68,2},{69,3},{70,4},{71,5},{72,6},{73,7},{74,8},{75... | collective-permute-start | bytes 393224 | tf_op jit(solution)/shard_map/ppermute | solution.py:189
  13.8 3.1 %collective-permute-start.3 = (f32[256,128]{1,0:T(8,128)S(1)}, f32[256,128]{1,0:T(8,128)S(1)}, u32[]{:S(2)}, u32[]{:S(2)}) collective-permute-start(f32[256,128]{1,0:T(8,128)S(1)} %constant_dynamic-update-slice_fusion.4), channel_id=1, source_target_pairs={{130,0},{131,1},{132,2},{133,3},{134,4},{135,5},{136,6},{137,7},{1... | collective-permute-start | bytes 393224 | tf_op jit(solution)/shard_map/ppermute | solution.py:189
  16.9 5.6 %collective-permute-start.4 = (f32[256,128]{1,0:T(8,128)S(1)}, f32[256,128]{1,0:T(8,128)S(1)}, u32[]{:S(2)}, u32[]{:S(2)}) collective-permute-start(f32[256,128]{1,0:T(8,128)S(1)} %constant_dynamic-update-slice_fusion.4), channel_id=1, source_target_pairs={{194,0},{195,1},{196,2},{197,3},{198,4},{199,5},{200,6},{201,7},{2... | collective-permute-start | bytes 393224 | tf_op jit(solution)/shard_map/ppermute | solution.py:189
  22.5 3.4 %collective-permute-done.3 = f32[256,128]{1,0:T(8,128)S(1)} collective-permute-done((f32[256,128]{1,0:T(8,128)S(1)}, f32[256,128]{1,0:T(8,128)S(1)}, u32[]{:S(2)}, u32[]{:S(2)}) %collective-permute-start.3) | collective-permute-done | bytes 131104 | tf_op jit(solution)/shard_map/ppermute | solution.py:189
  26.0 2.8 %collective-permute-done.4 = f32[256,128]{1,0:T(8,128)S(1)} collective-permute-done((f32[256,128]{1,0:T(8,128)S(1)}, f32[256,128]{1,0:T(8,128)S(1)}, u32[]{:S(2)}, u32[]{:S(2)}) %collective-permute-start.4) | collective-permute-done | bytes 131104 | tf_op jit(solution)/shard_map/ppermute | solution.py:189
  30.6 7.3 %collective-permute-start.8 = (f32[1024,128]{1,0:T(8,128)S(1)}, f32[1024,128]{1,0:T(8,128)S(1)}, u32[]{:S(2)}, u32[]{:S(2)}) collective-permute-start(f32[1024,128]{1,0:T(8,128)S(1)} %constant_dynamic-update-slice_fusion.refs_0_), channel_id=1, source_target_pairs={{0,31},{2,1},{4,3},{6,5},{8,7},{10,9},{12,11},{14,13},{16,15},{18,... | collective-permute-start | bytes 1572872 | tf_op jit(solution)/shard_map/ppermute | solution.py:201
  38.0 4.7 %shard_map.86.refs_4_ = f32[1024,128]{1,0:T(8,128)S(1)} custom-call(s32[17,32]{1,0:T(8,128)S(1)} %concatenate.9.info, f32[1024,128]{1,0:T(8,128)S(1)} %constant_dynamic-update-slice_fusion.refs_0_, f32[1024,128]{1,0:T(8,128)S(1)} %collective-permute-done.6.refs_1_, f32[4,32,128,128]{3,2,1,0:T(8,128)} %bitcast.18), custom_call_target="tpu_custom_call" | custom-call | flops 4294967296 | bytes 4194304 | tf_op jit(solution)/shard_map/pallas_call | solution.py:107
  42.7 4.2 %collective-permute-done.5.refs_0_ = f32[1024,128]{1,0:T(8,128)S(1)} collective-permute-done((f32[1024,128]{1,0:T(8,128)S(1)}, f32[1024,128]{1,0:T(8,128)S(1)}, u32[]{:S(2)}, u32[]{:S(2)}) %collective-permute-start.5) | collective-permute-done | bytes 524320 | tf_op jit(solution)/shard_map/ppermute | solution.py:201
  48.2 2.5 %collective-permute-done.7.refs_1_ = f32[1024,128]{1,0:T(8,128)S(1)} collective-permute-done((f32[1024,128]{1,0:T(8,128)S(1)}, f32[1024,128]{1,0:T(8,128)S(1)}, u32[]{:S(2)}, u32[]{:S(2)}) %collective-permute-start.7) | collective-permute-done | bytes 524320 | tf_op jit(solution)/shard_map/ppermute | solution.py:201
  50.6 4.7 %shard_map.87 = f32[1024,128]{1,0:T(8,128)S(1)} custom-call(s32[17,32]{1,0:T(8,128)S(1)} %concatenate.9.info, f32[1024,128]{1,0:T(8,128)S(1)} %collective-permute-done.5.refs_0_, f32[1024,128]{1,0:T(8,128)S(1)} %collective-permute-done.7.refs_1_, f32[1024,128]{1,0:T(8,128)S(1)} %collective-permute-done.8.refs_2_, f32[4,32,128,128]{3,2,1,0:T(8,128)} %bitcast.19, ...), custom_call_target="tpu_custom_call" | custom-call | flops 4294967296 | bytes 4194304 | tf_op jit(solution)/shard_map/pallas_call | solution.py:107
  55.4 18.7 %all_to_all.10.partials = f32[8,128,128]{2,1,0:T(8,128)} all-to-all(f32[8,128,128]{2,1,0:T(8,128)S(1)} %bitcast.17), channel_id=1, replica_groups=mesh['rep'=8,'blk'=32] {'rep'}, dimensions={0} | all-to-all | bytes 1048576 | tf_op jit(solution)/shard_map/all_to_all | solution.py:227
  74.1 2.6 %shard_map.88 = (f32[128,256]{1,0:T(8,128)}, f32[8,128,128]{2,1,0:T(8,128)}) custom-call(f32[8,128,128]{2,1,0:T(8,128)} %all_to_all.10.partials, f32[128,256]{1,0:T(8,128)} %weight.1, f32[128,256]{1,0:T(8,128)} %bitcast.23), custom_call_target="tpu_custom_call" | custom-call | tf_op jit(solution)/shard_map/pallas_call | solution.py:158
  76.7 12.6 %all_to_all.11 = f32[8,128,128]{2,1,0:T(8,128)S(1)} all-to-all(f32[8,128,128]{2,1,0:T(8,128)} %get-tuple-element.14), channel_id=1, replica_groups=mesh['rep'=8,'blk'=32] {'rep'}, dimensions={0} | all-to-all | bytes 1048576 | tf_op jit(solution)/shard_map/all_to_all | solution.py:231
  89.3 3.3 %shard_map.90 = f32[1024,128]{1,0:T(8,128)S(1)} custom-call(s32[17,32]{1,0:T(8,128)S(1)} %concatenate.9.info, f32[1024,128]{1,0:T(8,128)S(1)} %bitcast.14, f32[4,32,128,128]{3,2,1,0:T(8,128)} %bitcast.20), custom_call_target="tpu_custom_call" | custom-call | flops 2147483648 | bytes 2097152 | tf_op jit(solution)/shard_map/pallas_call | solution.py:107
  94.0 3.3 %shard_map.89 = f32[1024,128]{1,0:T(8,128)S(1)} custom-call(s32[17,32]{1,0:T(8,128)S(1)} %concatenate.9.info, f32[1024,128]{1,0:T(8,128)S(1)} %bitcast.15, f32[4,32,128,128]{3,2,1,0:T(8,128)} %bitcast.21), custom_call_target="tpu_custom_call" | custom-call | flops 2147483648 | bytes 2097152 | tf_op jit(solution)/shard_map/pallas_call | solution.py:107
  99.1 5.0 %shard_map.91 = (f32[1024,128]{1,0:T(8,128)S(1)}, f32[1024,128]{1,0:T(8,128)S(1)}) custom-call(s32[17,32]{1,0:T(8,128)S(1)} %concatenate.9.info, f32[1024,128]{1,0:T(8,128)S(1)} %bitcast.16, f32[4,32,128,128]{3,2,1,0:T(8,128)} %bitcast.22), custom_call_target="tpu_custom_call" | custom-call | flops 4294967296 | bytes 4194304 | tf_op jit(solution)/shard_map/pallas_call | solution.py:107
  104.1 5.8 %collective-permute-done.10 = f32[1024,128]{1,0:T(8,128)S(1)} collective-permute-done((f32[1024,128]{1,0:T(8,128)S(1)}, f32[1024,128]{1,0:T(8,128)S(1)}, u32[]{:S(2)}, u32[]{:S(2)}) %collective-permute-start.10) | collective-permute-done | bytes 524320 | tf_op jit(solution)/shard_map/ppermute | solution.py:201
  109.8 2.1 %collective-permute-done.12 = f32[1024,128]{1,0:T(8,128)S(1)} collective-permute-done((f32[1024,128]{1,0:T(8,128)S(1)}, f32[1024,128]{1,0:T(8,128)S(1)}, u32[]{:S(2)}, u32[]{:S(2)}) %collective-permute-start.12) | collective-permute-done | bytes 524320 | tf_op jit(solution)/shard_map/ppermute | solution.py:201
  112.1 3.5 %collective-permute-start.16 = (f32[256,128]{1,0:T(8,128)S(1)}, f32[256,128]{1,0:T(8,128)S(1)}, u32[]{:S(2)}, u32[]{:S(2)}) collective-permute-start(f32[256,128]{1,0:T(8,128)S(1)} %get-tuple-element.24), channel_id=1, source_target_pairs={{0,128},{32,160},{64,192},{96,224},{128,0},{160,32},{192,64},{224,... | collective-permute-start | bytes 393224 | tf_op jit(solution)/shard_map/ppermute | solution.py:247
  116.8 3.8 %collective-permute-start.13 = (f32[256,128]{1,0:T(8,128)S(1)}, f32[256,128]{1,0:T(8,128)S(1)}, u32[]{:S(2)}, u32[]{:S(2)}) collective-permute-start(f32[256,128]{1,0:T(8,128)S(1)} %get-tuple-element.25), channel_id=1, source_target_pairs={{0,2},{1,3},{2,4},{3,5},{4,6},{5,7},{6,8},{7,9},{8,10},{9,11},{10,... | collective-permute-start | bytes 393224 | tf_op jit(solution)/shard_map/ppermute | solution.py:195
  124.1 14.9 %collective-permute-done.15 = f32[256,128]{1,0:T(8,128)S(1)} collective-permute-done((f32[256,128]{1,0:T(8,128)S(1)}, f32[256,128]{1,0:T(8,128)S(1)}, u32[]{:S(2)}, u32[]{:S(2)}) %collective-permute-start.15) | collective-permute-done | bytes 131104 | tf_op jit(solution)/shard_map/ppermute | solution.py:195
  140.6 4.3 %collective-permute-done.20 = f32[128,128]{1,0:T(8,128)S(1)} collective-permute-done((f32[128,128]{1,0:T(8,128)S(1)}, f32[128,128]{1,0:T(8,128)S(1)}, u32[]{:S(2)}, u32[]{:S(2)}) %collective-permute-start.20) | collective-permute-done | bytes 65568 | tf_op jit(solution)/shard_map/ppermute | solution.py:252
  (41 shorter events, 14.8 us)
Async XLA Ops:
  0.6 4.6 %collective-permute-start = (f32[128,128]{1,0:T(8,128)}, f32[128,128]{1,0:T(8,128)S(1)}, u32[]{:S(2)}, u32[]{:S(2)}) collective-permute-start(f32[128,128]{1,0:T(8,128)} %bitcast.24), channel_id=1, source_target_pairs={{32,0},{0,32},{96,64},{64,96},{160,128},{128,160},{224,192},{192,2... | collective-permute-start | bytes 196616 | tf_op jit(solution)/shard_map/ppermute | solution.py:210
  5.2 17.3 %collective-permute-start.1 = (f32[256,128]{1,0:T(8,128)S(1)}, f32[256,128]{1,0:T(8,128)S(1)}, u32[]{:S(2)}, u32[]{:S(2)}) collective-permute-start(f32[256,128]{1,0:T(8,128)S(1)} %constant_dynamic-update-slice_fusion.4), channel_id=1, source_target_pairs={{2,0},{3,1},{4,2},{5,3},{6,4},{7,5},{8,6},{9,7},{10,8},{11,9},{12,... | collective-permute-start | bytes 393224 | tf_op jit(solution)/shard_map/ppermute | solution.py:189
  7.1 15.4 %collective-permute-start.2 = (f32[256,128]{1,0:T(8,128)S(1)}, f32[256,128]{1,0:T(8,128)S(1)}, u32[]{:S(2)}, u32[]{:S(2)}) collective-permute-start(f32[256,128]{1,0:T(8,128)S(1)} %constant_dynamic-update-slice_fusion.4), channel_id=1, source_target_pairs={{66,0},{67,1},{68,2},{69,3},{70,4},{71,5},{72,6},{73,7},{74,8},{75... | collective-permute-start | bytes 393224 | tf_op jit(solution)/shard_map/ppermute | solution.py:189
  13.8 12.2 %collective-permute-start.3 = (f32[256,128]{1,0:T(8,128)S(1)}, f32[256,128]{1,0:T(8,128)S(1)}, u32[]{:S(2)}, u32[]{:S(2)}) collective-permute-start(f32[256,128]{1,0:T(8,128)S(1)} %constant_dynamic-update-slice_fusion.4), channel_id=1, source_target_pairs={{130,0},{131,1},{132,2},{133,3},{134,4},{135,5},{136,6},{137,7},{1... | collective-permute-start | bytes 393224 | tf_op jit(solution)/shard_map/ppermute | solution.py:189
  16.9 11.9 %collective-permute-start.4 = (f32[256,128]{1,0:T(8,128)S(1)}, f32[256,128]{1,0:T(8,128)S(1)}, u32[]{:S(2)}, u32[]{:S(2)}) collective-permute-start(f32[256,128]{1,0:T(8,128)S(1)} %constant_dynamic-update-slice_fusion.4), channel_id=1, source_target_pairs={{194,0},{195,1},{196,2},{197,3},{198,4},{199,5},{200,6},{201,7},{2... | collective-permute-start | bytes 393224 | tf_op jit(solution)/shard_map/ppermute | solution.py:189
  28.8 9.2 %collective-permute-start.6 = (f32[1024,128]{1,0:T(8,128)S(1)}, f32[1024,128]{1,0:T(8,128)S(1)}, u32[]{:S(2)}, u32[]{:S(2)}) collective-permute-start(f32[1024,128]{1,0:T(8,128)S(1)} %constant_dynamic-update-slice_fusion.refs_0_), channel_id=1, source_target_pairs={{1,0},{0,1},{3,2},{2,3},{5,4},{4,5},{7,6},{6,7},{9,8},{8,9},{11,10... | collective-permute-start | bytes 1572872 | tf_op jit(solution)/shard_map/ppermute | solution.py:220
  28.9 17.9 %collective-permute-start.5 = (f32[1024,128]{1,0:T(8,128)S(1)}, f32[1024,128]{1,0:T(8,128)S(1)}, u32[]{:S(2)}, u32[]{:S(2)}) collective-permute-start(f32[1024,128]{1,0:T(8,128)S(1)} %constant_dynamic-update-slice_fusion.refs_0_), channel_id=1, source_target_pairs={{0,2},{1,3},{2,4},{3,5},{4,6},{5,7},{6,8},{7,9},{8,10},{9,11},{10,... | collective-permute-start | bytes 1572872 | tf_op jit(solution)/shard_map/ppermute | solution.py:201
  30.6 17.5 %collective-permute-start.8 = (f32[1024,128]{1,0:T(8,128)S(1)}, f32[1024,128]{1,0:T(8,128)S(1)}, u32[]{:S(2)}, u32[]{:S(2)}) collective-permute-start(f32[1024,128]{1,0:T(8,128)S(1)} %constant_dynamic-update-slice_fusion.refs_0_), channel_id=1, source_target_pairs={{0,31},{2,1},{4,3},{6,5},{8,7},{10,9},{12,11},{14,13},{16,15},{18,... | collective-permute-start | bytes 1572872 | tf_op jit(solution)/shard_map/ppermute | solution.py:201
  46.9 3.8 %collective-permute-start.7 = (f32[1024,128]{1,0:T(8,128)S(1)}, f32[1024,128]{1,0:T(8,128)S(1)}, u32[]{:S(2)}, u32[]{:S(2)}) collective-permute-start(f32[1024,128]{1,0:T(8,128)S(1)} %collective-permute-done.5.refs_0_), channel_id=1, source_target_pairs={{1,0},{3,2},{5,4},{7,6},{9,8},{11,10},{13,12},{15,14},{17,16},{19,... | collective-permute-start | bytes 1572872 | tf_op jit(solution)/shard_map/ppermute | solution.py:201
  92.6 4.7 %collective-permute-start.9 = (f32[1024,128]{1,0:T(8,128)S(1)}, f32[1024,128]{1,0:T(8,128)S(1)}, u32[]{:S(2)}, u32[]{:S(2)}) collective-permute-start(f32[1024,128]{1,0:T(8,128)S(1)} %shard_map.90), channel_id=1, source_target_pairs={{0,1},{2,3},{4,5},{6,7},{8,9},{10,11},{12,13},{14,15},{16,17},{18,... | collective-permute-start | bytes 1572872 | tf_op jit(solution)/shard_map/ppermute | solution.py:201
  97.4 12.4 %collective-permute-start.10 = (f32[1024,128]{1,0:T(8,128)S(1)}, f32[1024,128]{1,0:T(8,128)S(1)}, u32[]{:S(2)}, u32[]{:S(2)}) collective-permute-start(f32[1024,128]{1,0:T(8,128)S(1)} %add.33), channel_id=1, source_target_pairs={{0,30},{1,31},{2,0},{3,1},{4,2},{5,3},{6,4},{7,5},{8,6},{9,7},{10,... | collective-permute-start | bytes 1572872 | tf_op jit(solution)/shard_map/ppermute | solution.py:201
  97.8 14.1 %collective-permute-start.12 = (f32[1024,128]{1,0:T(8,128)S(1)}, f32[1024,128]{1,0:T(8,128)S(1)}, u32[]{:S(2)}, u32[]{:S(2)}) collective-permute-start(f32[1024,128]{1,0:T(8,128)S(1)} %shard_map.90), channel_id=1, source_target_pairs={{1,2},{3,4},{5,6},{7,8},{9,10},{11,12},{13,14},{15,16},{17,18},{19... | collective-permute-start | bytes 1572872 | tf_op jit(solution)/shard_map/ppermute | solution.py:201
  109.8 2.1 %collective-permute-start.11 = (f32[1024,128]{1,0:T(8,128)S(1)}, f32[1024,128]{1,0:T(8,128)S(1)}, u32[]{:S(2)}, u32[]{:S(2)}) collective-permute-start(f32[1024,128]{1,0:T(8,128)S(1)} %get-tuple-element.18), channel_id=1, source_target_pairs={{1,0},{0,1},{3,2},{2,3},{5,4},{4,5},{7,6},{6,7},{9,8},{8,9},{11,10... | collective-permute-start | bytes 1572872 | tf_op jit(solution)/shard_map/ppermute | solution.py:241
  112.0 8.6 %collective-permute-start.14 = (f32[256,128]{1,0:T(8,128)S(1)}, f32[256,128]{1,0:T(8,128)S(1)}, u32[]{:S(2)}, u32[]{:S(2)}) collective-permute-start(f32[256,128]{1,0:T(8,128)S(1)} %get-tuple-element.22), channel_id=1, source_target_pairs={{0,64},{32,96},{64,0},{96,32},{128,192},{160,224},{192,128},{224,1... | collective-permute-start | bytes 393224 | tf_op jit(solution)/shard_map/ppermute | solution.py:247
  112.1 9.8 %collective-permute-start.16 = (f32[256,128]{1,0:T(8,128)S(1)}, f32[256,128]{1,0:T(8,128)S(1)}, u32[]{:S(2)}, u32[]{:S(2)}) collective-permute-start(f32[256,128]{1,0:T(8,128)S(1)} %get-tuple-element.24), channel_id=1, source_target_pairs={{0,128},{32,160},{64,192},{96,224},{128,0},{160,32},{192,64},{224,... | collective-permute-start | bytes 393224 | tf_op jit(solution)/shard_map/ppermute | solution.py:247
  115.7 8.4 %collective-permute-start.18 = (f32[256,128]{1,0:T(8,128)S(1)}, f32[256,128]{1,0:T(8,128)S(1)}, u32[]{:S(2)}, u32[]{:S(2)}) collective-permute-start(f32[256,128]{1,0:T(8,128)S(1)} %get-tuple-element.23), channel_id=1, source_target_pairs={{0,192},{32,224},{64,128},{96,160},{128,64},{160,96},{192,0},{224,... | collective-permute-start | bytes 393224 | tf_op jit(solution)/shard_map/ppermute | solution.py:247
  116.8 7.2 %collective-permute-start.13 = (f32[256,128]{1,0:T(8,128)S(1)}, f32[256,128]{1,0:T(8,128)S(1)}, u32[]{:S(2)}, u32[]{:S(2)}) collective-permute-start(f32[256,128]{1,0:T(8,128)S(1)} %get-tuple-element.25), channel_id=1, source_target_pairs={{0,2},{1,3},{2,4},{3,5},{4,6},{5,7},{6,8},{7,9},{8,10},{9,11},{10,... | collective-permute-start | bytes 393224 | tf_op jit(solution)/shard_map/ppermute | solution.py:195
  120.7 18.4 %collective-permute-start.15 = (f32[256,128]{1,0:T(8,128)S(1)}, f32[256,128]{1,0:T(8,128)S(1)}, u32[]{:S(2)}, u32[]{:S(2)}) collective-permute-start(f32[256,128]{1,0:T(8,128)S(1)} %collective-permute-done.14), channel_id=1, source_target_pairs={{0,10},{1,11},{2,12},{3,13},{4,14},{5,15},{6,16},{7,17},{8,18},{9,... | collective-permute-start | bytes 393224 | tf_op jit(solution)/shard_map/ppermute | solution.py:195
  121.9 17.1 %collective-permute-start.17 = (f32[256,128]{1,0:T(8,128)S(1)}, f32[256,128]{1,0:T(8,128)S(1)}, u32[]{:S(2)}, u32[]{:S(2)}) collective-permute-start(f32[256,128]{1,0:T(8,128)S(1)} %collective-permute-done.16), channel_id=1, source_target_pairs={{0,18},{1,19},{2,20},{3,21},{4,22},{5,23},{6,24},{7,25},{8,26},{9,... | collective-permute-start | bytes 393224 | tf_op jit(solution)/shard_map/ppermute | solution.py:195
  124.1 16.4 %collective-permute-start.19 = (f32[256,128]{1,0:T(8,128)S(1)}, f32[256,128]{1,0:T(8,128)S(1)}, u32[]{:S(2)}, u32[]{:S(2)}) collective-permute-start(f32[256,128]{1,0:T(8,128)S(1)} %collective-permute-done.18), channel_id=1, source_target_pairs={{0,26},{1,27},{2,28},{3,29},{4,30},{5,31},{6,0},{7,1},{8,2},{9,3},... | collective-permute-start | bytes 393224 | tf_op jit(solution)/shard_map/ppermute | solution.py:195
  140.5 4.4 %collective-permute-start.20 = (f32[128,128]{1,0:T(8,128)S(1)}, f32[128,128]{1,0:T(8,128)S(1)}, u32[]{:S(2)}, u32[]{:S(2)}) collective-permute-start(f32[128,128]{1,0:T(8,128)S(1)} %split.9), channel_id=1, source_target_pairs={{32,0},{0,32},{96,64},{64,96},{160,128},{128,160},{224,192},{192,2... | collective-permute-start | bytes 196616 | tf_op jit(solution)/shard_map/ppermute | solution.py:252

commit v2 on v1

--- a/solution.py
+++ b/solution.py
@@ -11,7 +11,7 @@
 BF16 = jnp.bfloat16
 HIGHEST = lax.Precision.HIGHEST
 SIDE = 128
-CHUNK = 8
+CHUNK = 16
 NEAR, FAR, OUTER, LOWEST, CORE = 0, 2, 3, 2, 4
 
 
@@ -209,6 +209,7 @@
     pair = lax.dynamic_update_slice(
         jnp.concatenate([own, own]), lax.ppermute(own, "rep", twin), (nodes, 0)
     )
+    pair, info = lax.optimization_barrier((pair, info))
     base = jnp.concatenate(
         [
             joint(pair, lambda g, r, k=k: (g + sections * r + 2, r ^ (2 * k)))
@@ -221,8 +222,9 @@
     partial_sum = forward_tiles(NEAR, info, [base, beside], tiles, None, False)
     lower, partial_sum = lax.optimization_barrier((lower, partial_sum))
     lower_beside = along(lower, -1, odds)
+    partial_sum = forward_tiles(FAR, info, [lower], tiles, partial_sum, False)
     partial_sum = forward_tiles(
-        FAR, info, [lower, lower_beside, upper], tiles, partial_sum, True
+        OUTER, info, [lower_beside, upper], tiles, partial_sum, True
     )
     partials = lax.all_to_all(
         partial_sum.reshape(replicas, -1, own.shape[-1]), "rep", 0, 0, tiled=True
@@ -236,9 +238,11 @@
     combined = lowest + outer_in
     from_upper = along(combined, -2, everyone)
     late_panel, _ = lax.optimization_barrier((grad_panel, combined))
-    mine, other = backward_tiles(NEAR, info, late_panel, tiles, 2)
-    other, from_upper = lax.optimization_barrier((other, from_upper))
-    total = mine + lax.ppermute(other, "blk", swap) + from_upper + to_lower
+    (other,) = backward_tiles(NEAR + 1, info, late_panel, tiles, 1)
+    late_panel, other = lax.optimization_barrier((late_panel, other))
+    (mine,) = backward_tiles(NEAR, info, late_panel, tiles, 1)
+    received = lax.optimization_barrier(mine + from_upper + to_lower)
+    total = received + lax.ppermute(other, "blk", swap)
     parts = total.reshape(replicas // 2, -1, own.shape[-1])
     pair_sum = 0.0
     for k in range(replicas // 2):

time: 147 us -> 149 us (1.014)
  waiting for transfers between devices: 46.2 us -> 35.1 us
  starting transfers between devices: 40.1 us -> 47.8 us
  blocking collectives: 31.3 us -> 33.8 us
    ppermute x6, waiting for transfers between devices: 14.5 us -> 7.29 us  [along(): lax.ppermute(block, 'blk', [(g, (g + distance) % groups) for g in ids])]
    ppermute x1, starting transfers between devices: 0.01 us -> 6.18 us  [shards(): total = received + lax.ppermute(other, 'blk', swap)]
    ppermute x4, waiting for transfers between devices: 16.4 us -> 13.4 us  [back(): lax.ppermute(block, ('rep', 'blk'), [(device(g, r), device(*target(g, r))...]
    ppermute x1, waiting for transfers between devices: 3.02 us -> 1.38 us  [shards(): lax.ppermute(own, 'rep', twin)]
    ppermute x4, starting transfers between devices: 5.51 us -> 7.09 us  [back(): lax.ppermute(block, ('rep', 'blk'), [(device(g, r), device(*target(g, r))...]
    pallas_call x5 -> x7, Pallas kernels: 21 us -> 22.4 us  [tile_call(): pl.pallas_call(body, in_specs=[pl.BlockSpec(memory_space=pltpu.SMEM)] + [...]
  transfers between devices with their start and end apart: 21 -> 21, of which waited for: 12 -> 11; matrix products, arithmetic and copies ran while one was open for 2% -> 2% of each run, Pallas kernels for 9% -> 11%
where the time goes in v2:
time: 149 us; the launch traced here: 146 us
  starting transfers between devices  47.8 us (32%)
  waiting for transfers between devices  35.1 us (24%)
  blocking collectives  33.8 us (23%)
  Pallas kernels  25 us (17%)
  other arithmetic  2.57 us (2%)
    pallas_call x7, Pallas kernels, tile_call(): pl.pallas_call(body, in_specs=[pl.BlockSpec(memory_space=pltpu.SMEM)] + [...  22.4 us
    all_to_all x1, blocking collectives, shards(): lax.all_to_all(partial_sum.reshape(replicas, -1, own.shape[-1]), 'rep', 0...  19.8 us
    ppermute x4, starting transfers between devices, joint(): lax.ppermute(block, ('rep', 'blk'), [(device(*source(g, r)), device(g, r)...  17.3 us
    all_to_all x1, blocking collectives, shards(): lax.all_to_all(spread, 'rep', 0, 0, tiled=True).reshape(base.shape)  13.9 us
    ppermute x4, waiting for transfers between devices, back(): lax.ppermute(block, ('rep', 'blk'), [(device(g, r), device(*target(g, r))...  13.4 us
    ppermute x6, starting transfers between devices, along(): lax.ppermute(block, 'blk', [(g, (g + distance) % groups) for g in ids])  11.6 us
    ppermute x6, waiting for transfers between devices, along(): lax.ppermute(block, 'blk', [(g, (g + distance) % groups) for g in ids])  7.29 us
    ppermute x4, starting transfers between devices, back(): lax.ppermute(block, ('rep', 'blk'), [(device(g, r), device(*target(g, r))...  7.09 us
  transfers between devices with their start and end apart: 21, of which 11 were waited for; matrix products, arithmetic and copies ran while one was open for 2% of the time, Pallas kernels for 11%

profile of v2, /device:TPU:26, one launch (start us, length us, event | category | flops | bytes accessed | tf_op | source)
XLA Modules:
  0.0 146.1 jit_solution(5345907211305604846)
XLA Ops:
  7.1 6.7 %collective-permute-start.2 = (f32[256,128]{1,0:T(8,128)S(1)}, f32[256,128]{1,0:T(8,128)S(1)}, u32[]{:S(2)}, u32[]{:S(2)}) collective-permute-start(f32[256,128]{1,0:T(8,128)S(1)} %constant_dynamic-update-slice_fusion.4), channel_id=1, source_target_pairs={{66,0},{67,1},{68,2},{69,3},{70,4},{71,5},{72,6},{73,7},{74,8},{75... | collective-permute-start | bytes 393224 | tf_op jit(solution)/shard_map/ppermute | solution.py:189
  13.8 3.1 %collective-permute-start.3 = (f32[256,128]{1,0:T(8,128)S(1)}, f32[256,128]{1,0:T(8,128)S(1)}, u32[]{:S(2)}, u32[]{:S(2)}) collective-permute-start(f32[256,128]{1,0:T(8,128)S(1)} %constant_dynamic-update-slice_fusion.4), channel_id=1, source_target_pairs={{130,0},{131,1},{132,2},{133,3},{134,4},{135,5},{136,6},{137,7},{1... | collective-permute-start | bytes 393224 | tf_op jit(solution)/shard_map/ppermute | solution.py:189
  16.9 5.6 %collective-permute-start.4 = (f32[256,128]{1,0:T(8,128)S(1)}, f32[256,128]{1,0:T(8,128)S(1)}, u32[]{:S(2)}, u32[]{:S(2)}) collective-permute-start(f32[256,128]{1,0:T(8,128)S(1)} %constant_dynamic-update-slice_fusion.4), channel_id=1, source_target_pairs={{194,0},{195,1},{196,2},{197,3},{198,4},{199,5},{200,6},{201,7},{2... | collective-permute-start | bytes 393224 | tf_op jit(solution)/shard_map/ppermute | solution.py:189
  22.5 3.4 %collective-permute-done.3 = f32[256,128]{1,0:T(8,128)S(1)} collective-permute-done((f32[256,128]{1,0:T(8,128)S(1)}, f32[256,128]{1,0:T(8,128)S(1)}, u32[]{:S(2)}, u32[]{:S(2)}) %collective-permute-start.3) | collective-permute-done | bytes 131104 | tf_op jit(solution)/shard_map/ppermute | solution.py:189
  26.0 2.8 %collective-permute-done.4 = f32[256,128]{1,0:T(8,128)S(1)} collective-permute-done((f32[256,128]{1,0:T(8,128)S(1)}, f32[256,128]{1,0:T(8,128)S(1)}, u32[]{:S(2)}, u32[]{:S(2)}) %collective-permute-start.4) | collective-permute-done | bytes 131104 | tf_op jit(solution)/shard_map/ppermute | solution.py:189
  29.0 7.3 %collective-permute-start.8 = (f32[1024,128]{1,0:T(8,128)S(1)}, f32[1024,128]{1,0:T(8,128)S(1)}, u32[]{:S(2)}, u32[]{:S(2)}) collective-permute-start(f32[1024,128]{1,0:T(8,128)S(1)} %constant_dynamic-update-slice_fusion.refs_0_), channel_id=1, source_target_pairs={{0,31},{2,1},{4,3},{6,5},{8,7},{10,9},{12,11},{14,13},{16,15},{18,... | collective-permute-start | bytes 1572872 | tf_op jit(solution)/shard_map/ppermute | solution.py:201
  36.3 4.1 %shard_map.86.refs_2_ = f32[1024,128]{1,0:T(8,128)S(1)} custom-call(s32[17,32]{1,0:T(8,128)S(1)} %concatenate.10.info, f32[1024,128]{1,0:T(8,128)S(1)} %constant_dynamic-update-slice_fusion.refs_0_, f32[1024,128]{1,0:T(8,128)S(1)} %collective-permute-done.6.refs_1_, f32[4,32,128,128]{3,2,1,0:T(8,128)} %bitcast.19), custom_call_target="tpu_custom_call" | custom-call | flops 4294967296 | bytes 4194304 | tf_op jit(solution)/shard_map/pallas_call | solution.py:107
  40.4 6.4 %collective-permute-done.5.refs_0_ = f32[1024,128]{1,0:T(8,128)S(1)} collective-permute-done((f32[1024,128]{1,0:T(8,128)S(1)}, f32[1024,128]{1,0:T(8,128)S(1)}, u32[]{:S(2)}, u32[]{:S(2)}) %collective-permute-start.5) | collective-permute-done | bytes 524320 | tf_op jit(solution)/shard_map/ppermute | solution.py:201
  48.1 3.0 %shard_map.87.refs_3_ = f32[1024,128]{1,0:T(8,128)S(1)} custom-call(s32[17,32]{1,0:T(8,128)S(1)} %concatenate.10.info, f32[1024,128]{1,0:T(8,128)S(1)} %collective-permute-done.5.refs_0_, f32[4,32,128,128]{3,2,1,0:T(8,128)} %bitcast.20, f32[1024,128]{1,0:T(8,128)S(1)} %shard_map.86.refs_2_), custom_call_target="tpu_custom_call" | custom-call | flops 2147483648 | bytes 2097152 | tf_op jit(solution)/shard_map/pallas_call | solution.py:107
  51.2 3.0 %shard_map.88 = f32[1024,128]{1,0:T(8,128)S(1)} custom-call(s32[17,32]{1,0:T(8,128)S(1)} %concatenate.10.info, f32[1024,128]{1,0:T(8,128)S(1)} %collective-permute-done.7.refs_0_, f32[1024,128]{1,0:T(8,128)S(1)} %collective-permute-done.8.refs_1_, f32[4,32,128,128]{3,2,1,0:T(8,128)} %bitcast.21, f32[1024,128]{1,0:T(8,128)S(1)} %shard_map.87.refs_3_), custom_call_target="tpu_custom_call" | custom-call | flops 2147483648 | bytes 2097152 | tf_op jit(solution)/shard_map/pallas_call | solution.py:107
  54.2 19.8 %all_to_all.10.partials = f32[8,128,128]{2,1,0:T(8,128)} all-to-all(f32[8,128,128]{2,1,0:T(8,128)S(1)} %bitcast.18), channel_id=1, replica_groups=mesh['rep'=8,'blk'=32] {'rep'}, dimensions={0} | all-to-all | bytes 1048576 | tf_op jit(solution)/shard_map/all_to_all | solution.py:229
  74.1 2.6 %shard_map.89 = (f32[128,256]{1,0:T(8,128)}, f32[8,128,128]{2,1,0:T(8,128)}) custom-call(f32[8,128,128]{2,1,0:T(8,128)} %all_to_all.10.partials, f32[128,256]{1,0:T(8,128)} %weight.1, f32[128,256]{1,0:T(8,128)} %bitcast.26), custom_call_target="tpu_custom_call" | custom-call | tf_op jit(solution)/shard_map/pallas_call | solution.py:158
  76.6 13.9 %all_to_all.11 = f32[8,128,128]{2,1,0:T(8,128)S(1)} all-to-all(f32[8,128,128]{2,1,0:T(8,128)} %get-tuple-element.16), channel_id=1, replica_groups=mesh['rep'=8,'blk'=32] {'rep'}, dimensions={0} | all-to-all | bytes 1048576 | tf_op jit(solution)/shard_map/all_to_all | solution.py:233
  90.6 3.1 %shard_map.91 = f32[1024,128]{1,0:T(8,128)S(1)} custom-call(s32[17,32]{1,0:T(8,128)S(1)} %concatenate.10.info, f32[1024,128]{1,0:T(8,128)S(1)} %bitcast.14, f32[4,32,128,128]{3,2,1,0:T(8,128)} %bitcast.22), custom_call_target="tpu_custom_call" | custom-call | flops 2147483648 | bytes 2097152 | tf_op jit(solution)/shard_map/pallas_call | solution.py:107
  96.4 3.1 %shard_map.90 = f32[1024,128]{1,0:T(8,128)S(1)} custom-call(s32[17,32]{1,0:T(8,128)S(1)} %concatenate.10.info, f32[1024,128]{1,0:T(8,128)S(1)} %bitcast.15, f32[4,32,128,128]{3,2,1,0:T(8,128)} %bitcast.23), custom_call_target="tpu_custom_call" | custom-call | flops 2147483648 | bytes 2097152 | tf_op jit(solution)/shard_map/pallas_call | solution.py:107
  99.8 3.1 %shard_map.92 = f32[1024,128]{1,0:T(8,128)S(1)} custom-call(s32[17,32]{1,0:T(8,128)S(1)} %concatenate.10.info, f32[1024,128]{1,0:T(8,128)S(1)} %bitcast.16, f32[4,32,128,128]{3,2,1,0:T(8,128)} %bitcast.24), custom_call_target="tpu_custom_call" | custom-call | flops 2147483648 | bytes 2097152 | tf_op jit(solution)/shard_map/pallas_call | solution.py:107
  102.9 6.2 %collective-permute-start.12 = (f32[1024,128]{1,0:T(8,128)S(1)}, f32[1024,128]{1,0:T(8,128)S(1)}, u32[]{:S(2)}, u32[]{:S(2)}) collective-permute-start(f32[1024,128]{1,0:T(8,128)S(1)} %shard_map.92), channel_id=1, source_target_pairs={{1,0},{0,1},{3,2},{2,3},{5,4},{4,5},{7,6},{6,7},{9,8},{8,9},{11,10... | collective-permute-start | bytes 1572872 | tf_op jit(solution)/shard_map/ppermute | solution.py:245
  109.1 3.1 %shard_map.93 = f32[1024,128]{1,0:T(8,128)S(1)} custom-call(s32[17,32]{1,0:T(8,128)S(1)} %concatenate.10.info, f32[1024,128]{1,0:T(8,128)S(1)} %bitcast.17, f32[4,32,128,128]{3,2,1,0:T(8,128)} %bitcast.25), custom_call_target="tpu_custom_call" | custom-call | flops 2147483648 | bytes 2097152 | tf_op jit(solution)/shard_map/pallas_call | solution.py:107
  113.4 3.3 %collective-permute-start.16 = (f32[256,128]{1,0:T(8,128)S(1)}, f32[256,128]{1,0:T(8,128)S(1)}, u32[]{:S(2)}, u32[]{:S(2)}) collective-permute-start(f32[256,128]{1,0:T(8,128)S(1)} %get-tuple-element.24), channel_id=1, source_target_pairs={{0,128},{32,160},{64,192},{96,224},{128,0},{160,32},{192,64},{224,... | collective-permute-start | bytes 393224 | tf_op jit(solution)/shard_map/ppermute | solution.py:251
  119.3 2.2 %collective-permute-start.15 = (f32[256,128]{1,0:T(8,128)S(1)}, f32[256,128]{1,0:T(8,128)S(1)}, u32[]{:S(2)}, u32[]{:S(2)}) collective-permute-start(f32[256,128]{1,0:T(8,128)S(1)} %collective-permute-done.14), channel_id=1, source_target_pairs={{0,10},{1,11},{2,12},{3,13},{4,14},{5,15},{6,16},{7,17},{8,18},{9,... | collective-permute-start | bytes 393224 | tf_op jit(solution)/shard_map/ppermute | solution.py:195
  124.1 3.6 %collective-permute-start.19 = (f32[256,128]{1,0:T(8,128)S(1)}, f32[256,128]{1,0:T(8,128)S(1)}, u32[]{:S(2)}, u32[]{:S(2)}) collective-permute-start(f32[256,128]{1,0:T(8,128)S(1)} %collective-permute-done.18), channel_id=1, source_target_pairs={{0,26},{1,27},{2,28},{3,29},{4,30},{5,31},{6,0},{7,1},{8,2},{9,3},... | collective-permute-start | bytes 393224 | tf_op jit(solution)/shard_map/ppermute | solution.py:195
  127.6 5.0 %collective-permute-done.15 = f32[256,128]{1,0:T(8,128)S(1)} collective-permute-done((f32[256,128]{1,0:T(8,128)S(1)}, f32[256,128]{1,0:T(8,128)S(1)}, u32[]{:S(2)}, u32[]{:S(2)}) %collective-permute-start.15) | collective-permute-done | bytes 131104 | tf_op jit(solution)/shard_map/ppermute | solution.py:195
  132.6 8.4 %collective-permute-done.19 = f32[256,128]{1,0:T(8,128)S(1)} collective-permute-done((f32[256,128]{1,0:T(8,128)S(1)}, f32[256,128]{1,0:T(8,128)S(1)}, u32[]{:S(2)}, u32[]{:S(2)}) %collective-permute-start.19) | collective-permute-done | bytes 131104 | tf_op jit(solution)/shard_map/ppermute | solution.py:195
  141.2 4.3 %collective-permute-done.20 = f32[128,128]{1,0:T(8,128)S(1)} collective-permute-done((f32[128,128]{1,0:T(8,128)S(1)}, f32[128,128]{1,0:T(8,128)S(1)}, u32[]{:S(2)}, u32[]{:S(2)}) %collective-permute-start.20) | collective-permute-done | bytes 65568 | tf_op jit(solution)/shard_map/ppermute | solution.py:256
  (44 shorter events, 18.1 us)
Async XLA Ops:
  0.6 4.6 %collective-permute-start = (f32[128,128]{1,0:T(8,128)}, f32[128,128]{1,0:T(8,128)S(1)}, u32[]{:S(2)}, u32[]{:S(2)}) collective-permute-start(f32[128,128]{1,0:T(8,128)} %bitcast.27), channel_id=1, source_target_pairs={{32,0},{0,32},{96,64},{64,96},{160,128},{128,160},{224,192},{192,2... | collective-permute-start | bytes 196616 | tf_op jit(solution)/shard_map/ppermute | solution.py:210
  5.2 17.3 %collective-permute-start.1 = (f32[256,128]{1,0:T(8,128)S(1)}, f32[256,128]{1,0:T(8,128)S(1)}, u32[]{:S(2)}, u32[]{:S(2)}) collective-permute-start(f32[256,128]{1,0:T(8,128)S(1)} %constant_dynamic-update-slice_fusion.4), channel_id=1, source_target_pairs={{2,0},{3,1},{4,2},{5,3},{6,4},{7,5},{8,6},{9,7},{10,8},{11,9},{12,... | collective-permute-start | bytes 393224 | tf_op jit(solution)/shard_map/ppermute | solution.py:189
  7.1 15.4 %collective-permute-start.2 = (f32[256,128]{1,0:T(8,128)S(1)}, f32[256,128]{1,0:T(8,128)S(1)}, u32[]{:S(2)}, u32[]{:S(2)}) collective-permute-start(f32[256,128]{1,0:T(8,128)S(1)} %constant_dynamic-update-slice_fusion.4), channel_id=1, source_target_pairs={{66,0},{67,1},{68,2},{69,3},{70,4},{71,5},{72,6},{73,7},{74,8},{75... | collective-permute-start | bytes 393224 | tf_op jit(solution)/shard_map/ppermute | solution.py:189
  13.8 12.2 %collective-permute-start.3 = (f32[256,128]{1,0:T(8,128)S(1)}, f32[256,128]{1,0:T(8,128)S(1)}, u32[]{:S(2)}, u32[]{:S(2)}) collective-permute-start(f32[256,128]{1,0:T(8,128)S(1)} %constant_dynamic-update-slice_fusion.4), channel_id=1, source_target_pairs={{130,0},{131,1},{132,2},{133,3},{134,4},{135,5},{136,6},{137,7},{1... | collective-permute-start | bytes 393224 | tf_op jit(solution)/shard_map/ppermute | solution.py:189
  16.9 11.9 %collective-permute-start.4 = (f32[256,128]{1,0:T(8,128)S(1)}, f32[256,128]{1,0:T(8,128)S(1)}, u32[]{:S(2)}, u32[]{:S(2)}) collective-permute-start(f32[256,128]{1,0:T(8,128)S(1)} %constant_dynamic-update-slice_fusion.4), channel_id=1, source_target_pairs={{194,0},{195,1},{196,2},{197,3},{198,4},{199,5},{200,6},{201,7},{2... | collective-permute-start | bytes 393224 | tf_op jit(solution)/shard_map/ppermute | solution.py:189
  28.8 7.5 %collective-permute-start.6 = (f32[1024,128]{1,0:T(8,128)S(1)}, f32[1024,128]{1,0:T(8,128)S(1)}, u32[]{:S(2)}, u32[]{:S(2)}) collective-permute-start(f32[1024,128]{1,0:T(8,128)S(1)} %constant_dynamic-update-slice_fusion.refs_0_), channel_id=1, source_target_pairs={{1,0},{0,1},{3,2},{2,3},{5,4},{4,5},{7,6},{6,7},{9,8},{8,9},{11,10... | collective-permute-start | bytes 1572872 | tf_op jit(solution)/shard_map/ppermute | solution.py:221
  28.9 18.0 %collective-permute-start.5 = (f32[1024,128]{1,0:T(8,128)S(1)}, f32[1024,128]{1,0:T(8,128)S(1)}, u32[]{:S(2)}, u32[]{:S(2)}) collective-permute-start(f32[1024,128]{1,0:T(8,128)S(1)} %constant_dynamic-update-slice_fusion.refs_0_), channel_id=1, source_target_pairs={{0,2},{1,3},{2,4},{3,5},{4,6},{5,7},{6,8},{7,9},{8,10},{9,11},{10,... | collective-permute-start | bytes 1572872 | tf_op jit(solution)/shard_map/ppermute | solution.py:201
  29.0 22.2 %collective-permute-start.8 = (f32[1024,128]{1,0:T(8,128)S(1)}, f32[1024,128]{1,0:T(8,128)S(1)}, u32[]{:S(2)}, u32[]{:S(2)}) collective-permute-start(f32[1024,128]{1,0:T(8,128)S(1)} %constant_dynamic-update-slice_fusion.refs_0_), channel_id=1, source_target_pairs={{0,31},{2,1},{4,3},{6,5},{8,7},{10,9},{12,11},{14,13},{16,15},{18,... | collective-permute-start | bytes 1572872 | tf_op jit(solution)/shard_map/ppermute | solution.py:201
  46.9 4.3 %collective-permute-start.7 = (f32[1024,128]{1,0:T(8,128)S(1)}, f32[1024,128]{1,0:T(8,128)S(1)}, u32[]{:S(2)}, u32[]{:S(2)}) collective-permute-start(f32[1024,128]{1,0:T(8,128)S(1)} %collective-permute-done.5.refs_0_), channel_id=1, source_target_pairs={{1,0},{3,2},{5,4},{7,6},{9,8},{11,10},{13,12},{15,14},{17,16},{19,... | collective-permute-start | bytes 1572872 | tf_op jit(solution)/shard_map/ppermute | solution.py:201
  93.7 5.8 %collective-permute-start.9 = (f32[1024,128]{1,0:T(8,128)S(1)}, f32[1024,128]{1,0:T(8,128)S(1)}, u32[]{:S(2)}, u32[]{:S(2)}) collective-permute-start(f32[1024,128]{1,0:T(8,128)S(1)} %shard_map.91), channel_id=1, source_target_pairs={{0,1},{2,3},{4,5},{6,7},{8,9},{10,11},{12,13},{14,15},{16,17},{18,... | collective-permute-start | bytes 1572872 | tf_op jit(solution)/shard_map/ppermute | solution.py:201
  95.1 17.1 %collective-permute-start.11 = (f32[1024,128]{1,0:T(8,128)S(1)}, f32[1024,128]{1,0:T(8,128)S(1)}, u32[]{:S(2)}, u32[]{:S(2)}) collective-permute-start(f32[1024,128]{1,0:T(8,128)S(1)} %shard_map.91), channel_id=1, source_target_pairs={{1,2},{3,4},{5,6},{7,8},{9,10},{11,12},{13,14},{15,16},{17,18},{19... | collective-permute-start | bytes 1572872 | tf_op jit(solution)/shard_map/ppermute | solution.py:201
  99.5 13.5 %collective-permute-start.10 = (f32[1024,128]{1,0:T(8,128)S(1)}, f32[1024,128]{1,0:T(8,128)S(1)}, u32[]{:S(2)}, u32[]{:S(2)}) collective-permute-start(f32[1024,128]{1,0:T(8,128)S(1)} %add.33), channel_id=1, source_target_pairs={{0,30},{1,31},{2,0},{3,1},{4,2},{5,3},{6,4},{7,5},{8,6},{9,7},{10,... | collective-permute-start | bytes 1572872 | tf_op jit(solution)/shard_map/ppermute | solution.py:201
  102.9 10.2 %collective-permute-start.12 = (f32[1024,128]{1,0:T(8,128)S(1)}, f32[1024,128]{1,0:T(8,128)S(1)}, u32[]{:S(2)}, u32[]{:S(2)}) collective-permute-start(f32[1024,128]{1,0:T(8,128)S(1)} %shard_map.92), channel_id=1, source_target_pairs={{1,0},{0,1},{3,2},{2,3},{5,4},{4,5},{7,6},{6,7},{9,8},{8,9},{11,10... | collective-permute-start | bytes 1572872 | tf_op jit(solution)/shard_map/ppermute | solution.py:245
  113.2 6.1 %collective-permute-start.14 = (f32[256,128]{1,0:T(8,128)S(1)}, f32[256,128]{1,0:T(8,128)S(1)}, u32[]{:S(2)}, u32[]{:S(2)}) collective-permute-start(f32[256,128]{1,0:T(8,128)S(1)} %get-tuple-element.22), channel_id=1, source_target_pairs={{0,64},{32,96},{64,0},{96,32},{128,192},{160,224},{192,128},{224,1... | collective-permute-start | bytes 393224 | tf_op jit(solution)/shard_map/ppermute | solution.py:251
  113.4 8.9 %collective-permute-start.16 = (f32[256,128]{1,0:T(8,128)S(1)}, f32[256,128]{1,0:T(8,128)S(1)}, u32[]{:S(2)}, u32[]{:S(2)}) collective-permute-start(f32[256,128]{1,0:T(8,128)S(1)} %get-tuple-element.24), channel_id=1, source_target_pairs={{0,128},{32,160},{64,192},{96,224},{128,0},{160,32},{192,64},{224,... | collective-permute-start | bytes 393224 | tf_op jit(solution)/shard_map/ppermute | solution.py:251
  116.7 7.4 %collective-permute-start.18 = (f32[256,128]{1,0:T(8,128)S(1)}, f32[256,128]{1,0:T(8,128)S(1)}, u32[]{:S(2)}, u32[]{:S(2)}) collective-permute-start(f32[256,128]{1,0:T(8,128)S(1)} %get-tuple-element.23), channel_id=1, source_target_pairs={{0,192},{32,224},{64,128},{96,160},{128,64},{160,96},{192,0},{224,... | collective-permute-start | bytes 393224 | tf_op jit(solution)/shard_map/ppermute | solution.py:251
  118.0 9.6 %collective-permute-start.13 = (f32[256,128]{1,0:T(8,128)S(1)}, f32[256,128]{1,0:T(8,128)S(1)}, u32[]{:S(2)}, u32[]{:S(2)}) collective-permute-start(f32[256,128]{1,0:T(8,128)S(1)} %get-tuple-element.25), channel_id=1, source_target_pairs={{0,2},{1,3},{2,4},{3,5},{4,6},{5,7},{6,8},{7,9},{8,10},{9,11},{10,... | collective-permute-start | bytes 393224 | tf_op jit(solution)/shard_map/ppermute | solution.py:195
  119.3 13.3 %collective-permute-start.15 = (f32[256,128]{1,0:T(8,128)S(1)}, f32[256,128]{1,0:T(8,128)S(1)}, u32[]{:S(2)}, u32[]{:S(2)}) collective-permute-start(f32[256,128]{1,0:T(8,128)S(1)} %collective-permute-done.14), channel_id=1, source_target_pairs={{0,10},{1,11},{2,12},{3,13},{4,14},{5,15},{6,16},{7,17},{8,18},{9,... | collective-permute-start | bytes 393224 | tf_op jit(solution)/shard_map/ppermute | solution.py:195
  122.3 10.3 %collective-permute-start.17 = (f32[256,128]{1,0:T(8,128)S(1)}, f32[256,128]{1,0:T(8,128)S(1)}, u32[]{:S(2)}, u32[]{:S(2)}) collective-permute-start(f32[256,128]{1,0:T(8,128)S(1)} %collective-permute-done.16), channel_id=1, source_target_pairs={{0,18},{1,19},{2,20},{3,21},{4,22},{5,23},{6,24},{7,25},{8,26},{9,... | collective-permute-start | bytes 393224 | tf_op jit(solution)/shard_map/ppermute | solution.py:195
  124.1 17.0 %collective-permute-start.19 = (f32[256,128]{1,0:T(8,128)S(1)}, f32[256,128]{1,0:T(8,128)S(1)}, u32[]{:S(2)}, u32[]{:S(2)}) collective-permute-start(f32[256,128]{1,0:T(8,128)S(1)} %collective-permute-done.18), channel_id=1, source_target_pairs={{0,26},{1,27},{2,28},{3,29},{4,30},{5,31},{6,0},{7,1},{8,2},{9,3},... | collective-permute-start | bytes 393224 | tf_op jit(solution)/shard_map/ppermute | solution.py:195
  141.1 4.4 %collective-permute-start.20 = (f32[128,128]{1,0:T(8,128)S(1)}, f32[128,128]{1,0:T(8,128)S(1)}, u32[]{:S(2)}, u32[]{:S(2)}) collective-permute-start(f32[128,128]{1,0:T(8,128)S(1)} %split.9), channel_id=1, source_target_pairs={{32,0},{0,32},{96,64},{64,96},{160,128},{128,160},{224,192},{192,2... | collective-permute-start | bytes 196616 | tf_op jit(solution)/shard_map/ppermute | solution.py:256

commit v3 on v2

--- a/solution.py
+++ b/solution.py
@@ -161,6 +161,8 @@
             jax.ShapeDtypeStruct(cotangent.shape, F32),
             jax.ShapeDtypeStruct(partials.shape, F32),
         ],
+        in_specs=[pl.BlockSpec(memory_space=pltpu.VMEM)] * 3,
+        out_specs=[pl.BlockSpec(memory_space=pltpu.VMEM)] * 2,
     )(partials, weight, cotangent)
 
 
@@ -179,7 +181,13 @@
     plan = jnp.where(lane == CORE, core, plan)
     spare = replicas
     info = jnp.concatenate(
-        [plan, jnp.where(live, rows, spare), cols ^ rep, rows, jnp.where(live, cols ^ rep, spare)]
+        [
+            plan,
+            jnp.where(live, rows, spare),
+            cols ^ rep ^ (rep >> 2),
+            rows,
+            jnp.where(live, cols ^ rep ^ ((cols ^ rep) >> 2), spare),
+        ]
     )
 
     def device(group, replica):
@@ -212,7 +220,7 @@
     pair, info = lax.optimization_barrier((pair, info))
     base = jnp.concatenate(
         [
-            joint(pair, lambda g, r, k=k: (g + sections * r + 2, r ^ (2 * k)))
+            joint(pair, lambda g, r, k=k: (g + sections * r + 2, r ^ (r >> 2) ^ (2 * k)))
             for k in range(replicas // 2)
         ]
     )
@@ -246,11 +254,11 @@
     parts = total.reshape(replicas // 2, -1, own.shape[-1])
     pair_sum = 0.0
     for k in range(replicas // 2):
-        part = parts[k]
+        part, across = parts[k], (2 * k) ^ (k >> 1)
         if k:
-            part = lax.ppermute(part, "rep", [(r, r ^ (2 * k)) for r in range(replicas)])
+            part = lax.ppermute(part, "rep", [(r, r ^ across) for r in range(replicas)])
         pair_sum = pair_sum + back(
-            part, lambda g, r, k=k: (g + sections * (r ^ (2 * k)) + 2, r)
+            part, lambda g, r, across=across: (g + sections * (r ^ across) + 2, r)
         )
     kept, sent = jnp.split(pair_sum, 2)
     feature_grad = kept + lax.ppermute(sent, "rep", twin)

time: 149 us -> 145 us (0.973)
  the two profiles are of different devices: /device:TPU:26 before, /device:TPU:56 now
where the time goes in v3:
time: 145 us; the launch traced here: 144 us
  waiting for transfers between devices  44.9 us (31%)
  starting transfers between devices  42.6 us (29%)
  blocking collectives  27.4 us (19%)
  Pallas kernels  25 us (17%)
  other arithmetic  2.57 us (2%)
    pallas_call x7, Pallas kernels, tile_call(): pl.pallas_call(body, in_specs=[pl.BlockSpec(memory_space=pltpu.SMEM)] + [...  22.4 us
    ppermute x4, waiting for transfers between devices, back(): lax.ppermute(block, ('rep', 'blk'), [(device(g, r), device(*target(g, r))...  15.1 us
    ppermute x4, waiting for transfers between devices, joint(): lax.ppermute(block, ('rep', 'blk'), [(device(*source(g, r)), device(g, r)...  14.2 us
    all_to_all x1, blocking collectives, shards(): lax.all_to_all(spread, 'rep', 0, 0, tiled=True).reshape(base.shape)  14 us
    all_to_all x1, blocking collectives, shards(): lax.all_to_all(partial_sum.reshape(replicas, -1, own.shape[-1]), 'rep', 0...  13.4 us
    ppermute x4, starting transfers between devices, joint(): lax.ppermute(block, ('rep', 'blk'), [(device(*source(g, r)), device(g, r)...  12.6 us
    ppermute x6, starting transfers between devices, along(): lax.ppermute(block, 'blk', [(g, (g + distance) % groups) for g in ids])  12.2 us
    ppermute x6, waiting for transfers between devices, along(): lax.ppermute(block, 'blk', [(g, (g + distance) % groups) for g in ids])  10.7 us
  transfers between devices with their start and end apart: 21, of which 12 were waited for; matrix products, arithmetic and copies ran while one was open for 2% of the time, Pallas kernels for 11%

profile of v3, /device:TPU:56, one launch (start us, length us, event | category | flops | bytes accessed | tf_op | source)
XLA Modules:
  0.0 144.4 jit_solution(5634937090542811386)
XLA Ops:
  5.2 2.8 %collective-permute-start.1 = (f32[256,128]{1,0:T(8,128)S(1)}, f32[256,128]{1,0:T(8,128)S(1)}, u32[]{:S(2)}, u32[]{:S(2)}) collective-permute-start(f32[256,128]{1,0:T(8,128)S(1)} %constant_dynamic-update-slice_fusion.4), channel_id=1, source_target_pairs={{2,0},{3,1},{4,2},{5,3},{6,4},{7,5},{8,6},{9,7},{10,8},{11,9},{12,... | collective-permute-start | bytes 393224 | tf_op jit(solution)/shard_map/ppermute | solution.py:197
  8.0 6.0 %collective-permute-start.2 = (f32[256,128]{1,0:T(8,128)S(1)}, f32[256,128]{1,0:T(8,128)S(1)}, u32[]{:S(2)}, u32[]{:S(2)}) collective-permute-start(f32[256,128]{1,0:T(8,128)S(1)} %constant_dynamic-update-slice_fusion.4), channel_id=1, source_target_pairs={{66,0},{67,1},{68,2},{69,3},{70,4},{71,5},{72,6},{73,7},{74,8},{75... | collective-permute-start | bytes 393224 | tf_op jit(solution)/shard_map/ppermute | solution.py:197
  17.8 3.0 %collective-permute-done.1 = f32[256,128]{1,0:T(8,128)S(1)} collective-permute-done((f32[256,128]{1,0:T(8,128)S(1)}, f32[256,128]{1,0:T(8,128)S(1)}, u32[]{:S(2)}, u32[]{:S(2)}) %collective-permute-start.1) | collective-permute-done | bytes 131104 | tf_op jit(solution)/shard_map/ppermute | solution.py:197
  23.1 6.1 %collective-permute-done.3 = f32[256,128]{1,0:T(8,128)S(1)} collective-permute-done((f32[256,128]{1,0:T(8,128)S(1)}, f32[256,128]{1,0:T(8,128)S(1)}, u32[]{:S(2)}, u32[]{:S(2)}) %collective-permute-start.3) | collective-permute-done | bytes 131104 | tf_op jit(solution)/shard_map/ppermute | solution.py:197
  29.2 2.8 %collective-permute-done.4 = f32[256,128]{1,0:T(8,128)S(1)} collective-permute-done((f32[256,128]{1,0:T(8,128)S(1)}, f32[256,128]{1,0:T(8,128)S(1)}, u32[]{:S(2)}, u32[]{:S(2)}) %collective-permute-start.4) | collective-permute-done | bytes 131104 | tf_op jit(solution)/shard_map/ppermute | solution.py:197
  32.2 3.6 %collective-permute-start.8 = (f32[1024,128]{1,0:T(8,128)S(1)}, f32[1024,128]{1,0:T(8,128)S(1)}, u32[]{:S(2)}, u32[]{:S(2)}) collective-permute-start(f32[1024,128]{1,0:T(8,128)S(1)} %constant_dynamic-update-slice_fusion.refs_0_), channel_id=1, source_target_pairs={{0,31},{2,1},{4,3},{6,5},{8,7},{10,9},{12,11},{14,13},{16,15},{18,... | collective-permute-start | bytes 1572872 | tf_op jit(solution)/shard_map/ppermute | solution.py:209
  35.9 4.1 %shard_map.86.refs_2_ = f32[1024,128]{1,0:T(8,128)S(1)} custom-call(s32[17,32]{1,0:T(8,128)S(1)} %concatenate.10.info, f32[1024,128]{1,0:T(8,128)S(1)} %constant_dynamic-update-slice_fusion.refs_0_, f32[1024,128]{1,0:T(8,128)S(1)} %collective-permute-done.6.refs_1_, f32[4,32,128,128]{3,2,1,0:T(8,128)} %bitcast.19), custom_call_target="tpu_custom_call" | custom-call | flops 4294967296 | bytes 4194304 | tf_op jit(solution)/shard_map/pallas_call | solution.py:107
  40.0 6.4 %collective-permute-done.5.refs_0_ = f32[1024,128]{1,0:T(8,128)S(1)} collective-permute-done((f32[1024,128]{1,0:T(8,128)S(1)}, f32[1024,128]{1,0:T(8,128)S(1)}, u32[]{:S(2)}, u32[]{:S(2)}) %collective-permute-start.5) | collective-permute-done | bytes 524320 | tf_op jit(solution)/shard_map/ppermute | solution.py:209
  47.7 3.0 %shard_map.87.refs_3_ = f32[1024,128]{1,0:T(8,128)S(1)} custom-call(s32[17,32]{1,0:T(8,128)S(1)} %concatenate.10.info, f32[1024,128]{1,0:T(8,128)S(1)} %collective-permute-done.5.refs_0_, f32[4,32,128,128]{3,2,1,0:T(8,128)} %bitcast.20, f32[1024,128]{1,0:T(8,128)S(1)} %shard_map.86.refs_2_), custom_call_target="tpu_custom_call" | custom-call | flops 2147483648 | bytes 2097152 | tf_op jit(solution)/shard_map/pallas_call | solution.py:107
  50.8 3.0 %shard_map.88 = f32[1024,128]{1,0:T(8,128)S(1)} custom-call(s32[17,32]{1,0:T(8,128)S(1)} %concatenate.10.info, f32[1024,128]{1,0:T(8,128)S(1)} %collective-permute-done.7.refs_0_, f32[1024,128]{1,0:T(8,128)S(1)} %collective-permute-done.8.refs_1_, f32[4,32,128,128]{3,2,1,0:T(8,128)} %bitcast.21, f32[1024,128]{1,0:T(8,128)S(1)} %shard_map.87.refs_3_), custom_call_target="tpu_custom_call" | custom-call | flops 2147483648 | bytes 2097152 | tf_op jit(solution)/shard_map/pallas_call | solution.py:107
  53.8 13.4 %all_to_all.10.partials = f32[8,128,128]{2,1,0:T(8,128)} all-to-all(f32[8,128,128]{2,1,0:T(8,128)S(1)} %bitcast.18), channel_id=1, replica_groups=mesh['rep'=8,'blk'=32] {'rep'}, dimensions={0} | all-to-all | bytes 1048576 | tf_op jit(solution)/shard_map/all_to_all | solution.py:237
  69.8 14.0 %all_to_all.11 = f32[8,128,128]{2,1,0:T(8,128)S(1)} all-to-all(f32[8,128,128]{2,1,0:T(8,128)} %get-tuple-element.16), channel_id=1, replica_groups=mesh['rep'=8,'blk'=32] {'rep'}, dimensions={0} | all-to-all | bytes 1048576 | tf_op jit(solution)/shard_map/all_to_all | solution.py:241
  83.8 3.1 %shard_map.91 = f32[1024,128]{1,0:T(8,128)S(1)} custom-call(s32[17,32]{1,0:T(8,128)S(1)} %concatenate.10.info, f32[1024,128]{1,0:T(8,128)S(1)} %bitcast.14, f32[4,32,128,128]{3,2,1,0:T(8,128)} %bitcast.22), custom_call_target="tpu_custom_call" | custom-call | flops 2147483648 | bytes 2097152 | tf_op jit(solution)/shard_map/pallas_call | solution.py:107
  89.5 3.1 %shard_map.90 = f32[1024,128]{1,0:T(8,128)S(1)} custom-call(s32[17,32]{1,0:T(8,128)S(1)} %concatenate.10.info, f32[1024,128]{1,0:T(8,128)S(1)} %bitcast.15, f32[4,32,128,128]{3,2,1,0:T(8,128)} %bitcast.23), custom_call_target="tpu_custom_call" | custom-call | flops 2147483648 | bytes 2097152 | tf_op jit(solution)/shard_map/pallas_call | solution.py:107
  92.7 4.5 %collective-permute-start.10 = (f32[1024,128]{1,0:T(8,128)S(1)}, f32[1024,128]{1,0:T(8,128)S(1)}, u32[]{:S(2)}, u32[]{:S(2)}) collective-permute-start(f32[1024,128]{1,0:T(8,128)S(1)} %add.33), channel_id=1, source_target_pairs={{0,30},{1,31},{2,0},{3,1},{4,2},{5,3},{6,4},{7,5},{8,6},{9,7},{10,... | collective-permute-start | bytes 1572872 | tf_op jit(solution)/shard_map/ppermute | solution.py:209
  97.2 3.1 %shard_map.92 = f32[1024,128]{1,0:T(8,128)S(1)} custom-call(s32[17,32]{1,0:T(8,128)S(1)} %concatenate.10.info, f32[1024,128]{1,0:T(8,128)S(1)} %bitcast.16, f32[4,32,128,128]{3,2,1,0:T(8,128)} %bitcast.24), custom_call_target="tpu_custom_call" | custom-call | flops 2147483648 | bytes 2097152 | tf_op jit(solution)/shard_map/pallas_call | solution.py:107
  100.3 3.1 %shard_map.93 = f32[1024,128]{1,0:T(8,128)S(1)} custom-call(s32[17,32]{1,0:T(8,128)S(1)} %concatenate.10.info, f32[1024,128]{1,0:T(8,128)S(1)} %bitcast.17, f32[4,32,128,128]{3,2,1,0:T(8,128)} %bitcast.25), custom_call_target="tpu_custom_call" | custom-call | flops 2147483648 | bytes 2097152 | tf_op jit(solution)/shard_map/pallas_call | solution.py:107
  103.4 4.2 %collective-permute-done.10 = f32[1024,128]{1,0:T(8,128)S(1)} collective-permute-done((f32[1024,128]{1,0:T(8,128)S(1)}, f32[1024,128]{1,0:T(8,128)S(1)}, u32[]{:S(2)}, u32[]{:S(2)}) %collective-permute-start.10) | collective-permute-done | bytes 524320 | tf_op jit(solution)/shard_map/ppermute | solution.py:209
  108.8 3.3 %collective-permute-start.16 = (f32[256,128]{1,0:T(8,128)S(1)}, f32[256,128]{1,0:T(8,128)S(1)}, u32[]{:S(2)}, u32[]{:S(2)}) collective-permute-start(f32[256,128]{1,0:T(8,128)S(1)} %get-tuple-element.22), channel_id=1, source_target_pairs={{0,160},{32,128},{64,224},{96,192},{128,32},{160,0},{192,96},{224,... | collective-permute-start | bytes 393224 | tf_op jit(solution)/shard_map/ppermute | solution.py:259
  116.2 2.9 %collective-permute-start.15 = (f32[256,128]{1,0:T(8,128)S(1)}, f32[256,128]{1,0:T(8,128)S(1)}, u32[]{:S(2)}, u32[]{:S(2)}) collective-permute-start(f32[256,128]{1,0:T(8,128)S(1)} %collective-permute-done.14), channel_id=1, source_target_pairs={{0,10},{1,11},{2,12},{3,13},{4,14},{5,15},{6,16},{7,17},{8,18},{9,... | collective-permute-start | bytes 393224 | tf_op jit(solution)/shard_map/ppermute | solution.py:203
  119.4 4.3 %collective-permute-start.17 = (f32[256,128]{1,0:T(8,128)S(1)}, f32[256,128]{1,0:T(8,128)S(1)}, u32[]{:S(2)}, u32[]{:S(2)}) collective-permute-start(f32[256,128]{1,0:T(8,128)S(1)} %collective-permute-done.16), channel_id=1, source_target_pairs={{0,22},{1,23},{2,24},{3,25},{4,26},{5,27},{6,28},{7,29},{8,30},{9,... | collective-permute-start | bytes 393224 | tf_op jit(solution)/shard_map/ppermute | solution.py:203
  126.4 3.8 %collective-permute-done.17 = f32[256,128]{1,0:T(8,128)S(1)} collective-permute-done((f32[256,128]{1,0:T(8,128)S(1)}, f32[256,128]{1,0:T(8,128)S(1)}, u32[]{:S(2)}, u32[]{:S(2)}) %collective-permute-start.17) | collective-permute-done | bytes 131104 | tf_op jit(solution)/shard_map/ppermute | solution.py:203
  130.2 9.1 %collective-permute-done.19 = f32[256,128]{1,0:T(8,128)S(1)} collective-permute-done((f32[256,128]{1,0:T(8,128)S(1)}, f32[256,128]{1,0:T(8,128)S(1)}, u32[]{:S(2)}, u32[]{:S(2)}) %collective-permute-start.19) | collective-permute-done | bytes 131104 | tf_op jit(solution)/shard_map/ppermute | solution.py:203
  139.5 4.3 %collective-permute-done.20 = f32[128,128]{1,0:T(8,128)S(1)} collective-permute-done((f32[128,128]{1,0:T(8,128)S(1)}, f32[128,128]{1,0:T(8,128)S(1)}, u32[]{:S(2)}, u32[]{:S(2)}) %collective-permute-start.20) | collective-permute-done | bytes 65568 | tf_op jit(solution)/shard_map/ppermute | solution.py:264
  (44 shorter events, 26.5 us)
Async XLA Ops:
  0.6 4.6 %collective-permute-start = (f32[128,128]{1,0:T(8,128)}, f32[128,128]{1,0:T(8,128)S(1)}, u32[]{:S(2)}, u32[]{:S(2)}) collective-permute-start(f32[128,128]{1,0:T(8,128)} %bitcast.27), channel_id=1, source_target_pairs={{32,0},{0,32},{96,64},{64,96},{160,128},{128,160},{224,192},{192,2... | collective-permute-start | bytes 196616 | tf_op jit(solution)/shard_map/ppermute | solution.py:218
  5.2 15.5 %collective-permute-start.1 = (f32[256,128]{1,0:T(8,128)S(1)}, f32[256,128]{1,0:T(8,128)S(1)}, u32[]{:S(2)}, u32[]{:S(2)}) collective-permute-start(f32[256,128]{1,0:T(8,128)S(1)} %constant_dynamic-update-slice_fusion.4), channel_id=1, source_target_pairs={{2,0},{3,1},{4,2},{5,3},{6,4},{7,5},{8,6},{9,7},{10,8},{11,9},{12,... | collective-permute-start | bytes 393224 | tf_op jit(solution)/shard_map/ppermute | solution.py:197
  8.0 15.0 %collective-permute-start.2 = (f32[256,128]{1,0:T(8,128)S(1)}, f32[256,128]{1,0:T(8,128)S(1)}, u32[]{:S(2)}, u32[]{:S(2)}) collective-permute-start(f32[256,128]{1,0:T(8,128)S(1)} %constant_dynamic-update-slice_fusion.4), channel_id=1, source_target_pairs={{66,0},{67,1},{68,2},{69,3},{70,4},{71,5},{72,6},{73,7},{74,8},{75... | collective-permute-start | bytes 393224 | tf_op jit(solution)/shard_map/ppermute | solution.py:197
  14.1 15.1 %collective-permute-start.3 = (f32[256,128]{1,0:T(8,128)S(1)}, f32[256,128]{1,0:T(8,128)S(1)}, u32[]{:S(2)}, u32[]{:S(2)}) collective-permute-start(f32[256,128]{1,0:T(8,128)S(1)} %constant_dynamic-update-slice_fusion.4), channel_id=1, source_target_pairs={{130,0},{131,1},{132,2},{133,3},{134,4},{135,5},{136,6},{137,7},{1... | collective-permute-start | bytes 393224 | tf_op jit(solution)/shard_map/ppermute | solution.py:197
  16.0 15.9 %collective-permute-start.4 = (f32[256,128]{1,0:T(8,128)S(1)}, f32[256,128]{1,0:T(8,128)S(1)}, u32[]{:S(2)}, u32[]{:S(2)}) collective-permute-start(f32[256,128]{1,0:T(8,128)S(1)} %constant_dynamic-update-slice_fusion.4), channel_id=1, source_target_pairs={{194,0},{195,1},{196,2},{197,3},{198,4},{199,5},{200,6},{201,7},{2... | collective-permute-start | bytes 393224 | tf_op jit(solution)/shard_map/ppermute | solution.py:197
  32.0 3.9 %collective-permute-start.6 = (f32[1024,128]{1,0:T(8,128)S(1)}, f32[1024,128]{1,0:T(8,128)S(1)}, u32[]{:S(2)}, u32[]{:S(2)}) collective-permute-start(f32[1024,128]{1,0:T(8,128)S(1)} %constant_dynamic-update-slice_fusion.refs_0_), channel_id=1, source_target_pairs={{1,0},{0,1},{3,2},{2,3},{5,4},{4,5},{7,6},{6,7},{9,8},{8,9},{11,10... | collective-permute-start | bytes 1572872 | tf_op jit(solution)/shard_map/ppermute | solution.py:229
  32.1 14.3 %collective-permute-start.5 = (f32[1024,128]{1,0:T(8,128)S(1)}, f32[1024,128]{1,0:T(8,128)S(1)}, u32[]{:S(2)}, u32[]{:S(2)}) collective-permute-start(f32[1024,128]{1,0:T(8,128)S(1)} %constant_dynamic-update-slice_fusion.refs_0_), channel_id=1, source_target_pairs={{0,2},{1,3},{2,4},{3,5},{4,6},{5,7},{6,8},{7,9},{8,10},{9,11},{10,... | collective-permute-start | bytes 1572872 | tf_op jit(solution)/shard_map/ppermute | solution.py:209
  32.2 18.5 %collective-permute-start.8 = (f32[1024,128]{1,0:T(8,128)S(1)}, f32[1024,128]{1,0:T(8,128)S(1)}, u32[]{:S(2)}, u32[]{:S(2)}) collective-permute-start(f32[1024,128]{1,0:T(8,128)S(1)} %constant_dynamic-update-slice_fusion.refs_0_), channel_id=1, source_target_pairs={{0,31},{2,1},{4,3},{6,5},{8,7},{10,9},{12,11},{14,13},{16,15},{18,... | collective-permute-start | bytes 1572872 | tf_op jit(solution)/shard_map/ppermute | solution.py:209
  46.4 4.3 %collective-permute-start.7 = (f32[1024,128]{1,0:T(8,128)S(1)}, f32[1024,128]{1,0:T(8,128)S(1)}, u32[]{:S(2)}, u32[]{:S(2)}) collective-permute-start(f32[1024,128]{1,0:T(8,128)S(1)} %collective-permute-done.5.refs_0_), channel_id=1, source_target_pairs={{1,0},{3,2},{5,4},{7,6},{9,8},{11,10},{13,12},{15,14},{17,16},{19,... | collective-permute-start | bytes 1572872 | tf_op jit(solution)/shard_map/ppermute | solution.py:209
  86.9 5.7 %collective-permute-start.9 = (f32[1024,128]{1,0:T(8,128)S(1)}, f32[1024,128]{1,0:T(8,128)S(1)}, u32[]{:S(2)}, u32[]{:S(2)}) collective-permute-start(f32[1024,128]{1,0:T(8,128)S(1)} %shard_map.91), channel_id=1, source_target_pairs={{0,1},{2,3},{4,5},{6,7},{8,9},{10,11},{12,13},{14,15},{16,17},{18,... | collective-permute-start | bytes 1572872 | tf_op jit(solution)/shard_map/ppermute | solution.py:209
  88.2 15.2 %collective-permute-start.11 = (f32[1024,128]{1,0:T(8,128)S(1)}, f32[1024,128]{1,0:T(8,128)S(1)}, u32[]{:S(2)}, u32[]{:S(2)}) collective-permute-start(f32[1024,128]{1,0:T(8,128)S(1)} %shard_map.91), channel_id=1, source_target_pairs={{1,2},{3,4},{5,6},{7,8},{9,10},{11,12},{13,14},{15,16},{17,18},{19... | collective-permute-start | bytes 1572872 | tf_op jit(solution)/shard_map/ppermute | solution.py:209
  92.7 15.0 %collective-permute-start.10 = (f32[1024,128]{1,0:T(8,128)S(1)}, f32[1024,128]{1,0:T(8,128)S(1)}, u32[]{:S(2)}, u32[]{:S(2)}) collective-permute-start(f32[1024,128]{1,0:T(8,128)S(1)} %add.33), channel_id=1, source_target_pairs={{0,30},{1,31},{2,0},{3,1},{4,2},{5,3},{6,4},{7,5},{8,6},{9,7},{10,... | collective-permute-start | bytes 1572872 | tf_op jit(solution)/shard_map/ppermute | solution.py:209
  100.2 7.5 %collective-permute-start.12 = (f32[1024,128]{1,0:T(8,128)S(1)}, f32[1024,128]{1,0:T(8,128)S(1)}, u32[]{:S(2)}, u32[]{:S(2)}) collective-permute-start(f32[1024,128]{1,0:T(8,128)S(1)} %shard_map.92), channel_id=1, source_target_pairs={{1,0},{0,1},{3,2},{2,3},{5,4},{4,5},{7,6},{6,7},{9,8},{8,9},{11,10... | collective-permute-start | bytes 1572872 | tf_op jit(solution)/shard_map/ppermute | solution.py:253
  107.9 8.3 %collective-permute-start.14 = (f32[256,128]{1,0:T(8,128)S(1)}, f32[256,128]{1,0:T(8,128)S(1)}, u32[]{:S(2)}, u32[]{:S(2)}) collective-permute-start(f32[256,128]{1,0:T(8,128)S(1)} %get-tuple-element.20), channel_id=1, source_target_pairs={{0,64},{32,96},{64,0},{96,32},{128,192},{160,224},{192,128},{224,1... | collective-permute-start | bytes 393224 | tf_op jit(solution)/shard_map/ppermute | solution.py:259
  108.8 10.6 %collective-permute-start.16 = (f32[256,128]{1,0:T(8,128)S(1)}, f32[256,128]{1,0:T(8,128)S(1)}, u32[]{:S(2)}, u32[]{:S(2)}) collective-permute-start(f32[256,128]{1,0:T(8,128)S(1)} %get-tuple-element.22), channel_id=1, source_target_pairs={{0,160},{32,128},{64,224},{96,192},{128,32},{160,0},{192,96},{224,... | collective-permute-start | bytes 393224 | tf_op jit(solution)/shard_map/ppermute | solution.py:259
  112.1 11.6 %collective-permute-start.18 = (f32[256,128]{1,0:T(8,128)S(1)}, f32[256,128]{1,0:T(8,128)S(1)}, u32[]{:S(2)}, u32[]{:S(2)}) collective-permute-start(f32[256,128]{1,0:T(8,128)S(1)} %get-tuple-element.21), channel_id=1, source_target_pairs={{0,224},{32,192},{64,160},{96,128},{128,96},{160,64},{192,32},{224... | collective-permute-start | bytes 393224 | tf_op jit(solution)/shard_map/ppermute | solution.py:259
  113.5 12.9 %collective-permute-start.13 = (f32[256,128]{1,0:T(8,128)S(1)}, f32[256,128]{1,0:T(8,128)S(1)}, u32[]{:S(2)}, u32[]{:S(2)}) collective-permute-start(f32[256,128]{1,0:T(8,128)S(1)} %get-tuple-element.23), channel_id=1, source_target_pairs={{0,2},{1,3},{2,4},{3,5},{4,6},{5,7},{6,8},{7,9},{8,10},{9,11},{10,... | collective-permute-start | bytes 393224 | tf_op jit(solution)/shard_map/ppermute | solution.py:203
  116.2 10.2 %collective-permute-start.15 = (f32[256,128]{1,0:T(8,128)S(1)}, f32[256,128]{1,0:T(8,128)S(1)}, u32[]{:S(2)}, u32[]{:S(2)}) collective-permute-start(f32[256,128]{1,0:T(8,128)S(1)} %collective-permute-done.14), channel_id=1, source_target_pairs={{0,10},{1,11},{2,12},{3,13},{4,14},{5,15},{6,16},{7,17},{8,18},{9,... | collective-permute-start | bytes 393224 | tf_op jit(solution)/shard_map/ppermute | solution.py:203
  119.4 10.8 %collective-permute-start.17 = (f32[256,128]{1,0:T(8,128)S(1)}, f32[256,128]{1,0:T(8,128)S(1)}, u32[]{:S(2)}, u32[]{:S(2)}) collective-permute-start(f32[256,128]{1,0:T(8,128)S(1)} %collective-permute-done.16), channel_id=1, source_target_pairs={{0,22},{1,23},{2,24},{3,25},{4,26},{5,27},{6,28},{7,29},{8,30},{9,... | collective-permute-start | bytes 393224 | tf_op jit(solution)/shard_map/ppermute | solution.py:203
  123.7 15.6 %collective-permute-start.19 = (f32[256,128]{1,0:T(8,128)S(1)}, f32[256,128]{1,0:T(8,128)S(1)}, u32[]{:S(2)}, u32[]{:S(2)}) collective-permute-start(f32[256,128]{1,0:T(8,128)S(1)} %collective-permute-done.18), channel_id=1, source_target_pairs={{0,30},{1,31},{2,0},{3,1},{4,2},{5,3},{6,4},{7,5},{8,6},{9,7},{10,... | collective-permute-start | bytes 393224 | tf_op jit(solution)/shard_map/ppermute | solution.py:203
  139.4 4.4 %collective-permute-start.20 = (f32[128,128]{1,0:T(8,128)S(1)}, f32[128,128]{1,0:T(8,128)S(1)}, u32[]{:S(2)}, u32[]{:S(2)}) collective-permute-start(f32[128,128]{1,0:T(8,128)S(1)} %split.9), channel_id=1, source_target_pairs={{32,0},{0,32},{96,64},{64,96},{160,128},{128,160},{224,192},{192,2... | collective-permute-start | bytes 196616 | tf_op jit(solution)/shard_map/ppermute | solution.py:264

commit v4 on v3

--- a/solution.py
+++ b/solution.py
@@ -170,7 +170,8 @@
     replicas, groups = lax.axis_size("rep"), lax.axis_size("blk")
     sections = groups // replicas
     rep = lax.axis_index("rep")
-    core = lax.axis_index("blk") % 2
+    group = lax.axis_index("blk")
+    core = group % 2
     tiles, rows, cols, count = tile_vals[0, 0], tile_rows[0, 0], tile_cols[0, 0], tile_count[0, 0]
     slots = rows.shape[-1]
     live = lax.broadcasted_iota(jnp.int32, rows.shape, 1) < count[:, None]
@@ -180,13 +181,18 @@
     plan = jnp.where(lane == 3, 1 + 2 * core, plan)
     plan = jnp.where(lane == CORE, core, plan)
     spare = replicas
+    span, half = groups // 2, replicas // 2
+    step = lax.broadcasted_iota(jnp.int32, cols.shape, 0)
+    turned = jnp.where((group % span < 2) & (step == 1 - core), half | (half >> 2), 0)
+    source = cols ^ rep
+    target = source ^ (source >> 2) ^ turned
     info = jnp.concatenate(
         [
             plan,
             jnp.where(live, rows, spare),
-            cols ^ rep ^ (rep >> 2),
+            source ^ (rep >> 2) ^ turned,
             rows,
-            jnp.where(live, cols ^ rep ^ ((cols ^ rep) >> 2), spare),
+            jnp.where(live, target, spare),
         ]
     )
 
@@ -205,10 +211,16 @@
             [(device(g, r), device(*target(g, r))) for r in range(replicas) for g in range(groups)],
         )
 
+    def below(group, replica):
+        lower = (group - 2) % groups
+        if group % span < 2 and group % 2:
+            return lower ^ span, replica ^ half
+        return lower, replica
+
     def along(block, distance, ids):
         return lax.ppermute(block, "blk", [(g, (g + distance) % groups) for g in ids])
 
-    everyone, evens, odds = range(groups), range(0, groups, 2), range(1, groups, 2)
+    evens, odds = range(0, groups, 2), range(1, groups, 2)
     twin = [(r ^ 1, r) for r in range(replicas)]
     swap = [(g ^ 1, g) for g in range(groups)]
 
@@ -224,7 +236,7 @@
             for k in range(replicas // 2)
         ]
     )
-    lower = along(base, 2, everyone)
+    lower = joint(base, below)
     upper = along(base, -1, evens)
     beside = lax.ppermute(base, "blk", swap)
     partial_sum = forward_tiles(NEAR, info, [base, beside], tiles, None, False)
@@ -244,7 +256,7 @@
     to_lower = along(outer, 1, odds)
     (lowest,) = backward_tiles(LOWEST, info, grad_panel, tiles, 1)
     combined = lowest + outer_in
-    from_upper = along(combined, -2, everyone)
+    from_upper = back(combined, below)
     late_panel, _ = lax.optimization_barrier((grad_panel, combined))
     (other,) = backward_tiles(NEAR + 1, info, late_panel, tiles, 1)
     late_panel, other = lax.optimization_barrier((late_panel, other))

time: 145 us -> 143 us (0.986)
  the two profiles are of different devices: /device:TPU:56 before, /device:TPU:26 now
where the time goes in v4:
time: 143 us; the launch traced here: 141 us
  starting transfers between devices  44.6 us (31%)
  waiting for transfers between devices  36.3 us (25%)
  blocking collectives  30.5 us (21%)
  Pallas kernels  25 us (17%)
  other arithmetic  2.58 us (2%)
    pallas_call x7, Pallas kernels, tile_call(): pl.pallas_call(body, in_specs=[pl.BlockSpec(memory_space=pltpu.SMEM)] + [...  22.4 us
    all_to_all x1, blocking collectives, shards(): lax.all_to_all(partial_sum.reshape(replicas, -1, own.shape[-1]), 'rep', 0...  16.6 us
    ppermute x5, starting transfers between devices, joint(): lax.ppermute(block, ('rep', 'blk'), [(device(*source(g, r)), device(g, r)...  15.9 us
    ppermute x5, waiting for transfers between devices, joint(): lax.ppermute(block, ('rep', 'blk'), [(device(*source(g, r)), device(g, r)...  15.4 us
    all_to_all x1, blocking collectives, shards(): lax.all_to_all(spread, 'rep', 0, 0, tiled=True).reshape(base.shape)  13.9 us
    ppermute x5, waiting for transfers between devices, back(): lax.ppermute(block, ('rep', 'blk'), [(device(g, r), device(*target(g, r))...  9.97 us
    ppermute x4, starting transfers between devices, along(): lax.ppermute(block, 'blk', [(g, (g + distance) % groups) for g in ids])  7.92 us
    ppermute x3, waiting for transfers between devices, shards(): part = lax.ppermute(part, 'rep', [(r, r ^ across) for r in range(replicas)])  7.34 us
  transfers between devices with their start and end apart: 21, of which 12 were waited for; matrix products, arithmetic and copies ran while one was open for 2% of the time, Pallas kernels for 12%

profile of v4, /device:TPU:26, one launch (start us, length us, event | category | flops | bytes accessed | tf_op | source)
XLA Modules:
  0.0 140.8 jit_solution(10419606615056983707)
XLA Ops:
  5.2 4.6 %collective-permute-start.1 = (f32[256,128]{1,0:T(8,128)S(1)}, f32[256,128]{1,0:T(8,128)S(1)}, u32[]{:S(2)}, u32[]{:S(2)}) collective-permute-start(f32[256,128]{1,0:T(8,128)S(1)} %constant_dynamic-update-slice_fusion.4), channel_id=1, source_target_pairs={{2,0},{3,1},{4,2},{5,3},{6,4},{7,5},{8,6},{9,7},{10,8},{11,9},{12,... | collective-permute-start | bytes 393224 | tf_op jit(solution)/shard_map/ppermute | solution.py:203
  9.8 5.5 %collective-permute-start.2 = (f32[256,128]{1,0:T(8,128)S(1)}, f32[256,128]{1,0:T(8,128)S(1)}, u32[]{:S(2)}, u32[]{:S(2)}) collective-permute-start(f32[256,128]{1,0:T(8,128)S(1)} %constant_dynamic-update-slice_fusion.4), channel_id=1, source_target_pairs={{66,0},{67,1},{68,2},{69,3},{70,4},{71,5},{72,6},{73,7},{74,8},{75... | collective-permute-start | bytes 393224 | tf_op jit(solution)/shard_map/ppermute | solution.py:203
  16.9 2.5 %collective-permute-start.4 = (f32[256,128]{1,0:T(8,128)S(1)}, f32[256,128]{1,0:T(8,128)S(1)}, u32[]{:S(2)}, u32[]{:S(2)}) collective-permute-start(f32[256,128]{1,0:T(8,128)S(1)} %constant_dynamic-update-slice_fusion.4), channel_id=1, source_target_pairs={{194,0},{195,1},{196,2},{197,3},{198,4},{199,5},{200,6},{201,7},{2... | collective-permute-start | bytes 393224 | tf_op jit(solution)/shard_map/ppermute | solution.py:203
  19.5 5.4 %collective-permute-done.3 = f32[256,128]{1,0:T(8,128)S(1)} collective-permute-done((f32[256,128]{1,0:T(8,128)S(1)}, f32[256,128]{1,0:T(8,128)S(1)}, u32[]{:S(2)}, u32[]{:S(2)}) %collective-permute-start.3) | collective-permute-done | bytes 131104 | tf_op jit(solution)/shard_map/ppermute | solution.py:203
  24.9 3.5 %collective-permute-done.4 = f32[256,128]{1,0:T(8,128)S(1)} collective-permute-done((f32[256,128]{1,0:T(8,128)S(1)}, f32[256,128]{1,0:T(8,128)S(1)}, u32[]{:S(2)}, u32[]{:S(2)}) %collective-permute-start.4) | collective-permute-done | bytes 131104 | tf_op jit(solution)/shard_map/ppermute | solution.py:203
  30.1 4.0 %collective-permute-start.8 = (f32[1024,128]{1,0:T(8,128)S(1)}, f32[1024,128]{1,0:T(8,128)S(1)}, u32[]{:S(2)}, u32[]{:S(2)}) collective-permute-start(f32[1024,128]{1,0:T(8,128)S(1)} %constant_dynamic-update-slice_fusion.refs_0_), channel_id=1, source_target_pairs={{0,31},{2,1},{4,3},{6,5},{8,7},{10,9},{12,11},{14,13},{16,15},{18,... | collective-permute-start | bytes 1572872 | tf_op jit(solution)/shard_map/ppermute | solution.py:221
  34.1 4.1 %shard_map.86.refs_2_ = f32[1024,128]{1,0:T(8,128)S(1)} custom-call(s32[17,32]{1,0:T(8,128)S(1)} %concatenate.10.info, f32[1024,128]{1,0:T(8,128)S(1)} %constant_dynamic-update-slice_fusion.refs_0_, f32[1024,128]{1,0:T(8,128)S(1)} %collective-permute-done.6.refs_1_, f32[4,32,128,128]{3,2,1,0:T(8,128)} %bitcast.21), custom_call_target="tpu_custom_call" | custom-call | flops 4294967296 | bytes 4194304 | tf_op jit(solution)/shard_map/pallas_call | solution.py:107
  38.2 6.4 %collective-permute-done.5.refs_0_ = f32[1024,128]{1,0:T(8,128)S(1)} collective-permute-done((f32[1024,128]{1,0:T(8,128)S(1)}, f32[1024,128]{1,0:T(8,128)S(1)}, u32[]{:S(2)}, u32[]{:S(2)}) %collective-permute-start.5) | collective-permute-done | bytes 524320 | tf_op jit(solution)/shard_map/ppermute | solution.py:203
  46.0 3.0 %shard_map.87.refs_3_ = f32[1024,128]{1,0:T(8,128)S(1)} custom-call(s32[17,32]{1,0:T(8,128)S(1)} %concatenate.10.info, f32[1024,128]{1,0:T(8,128)S(1)} %collective-permute-done.5.refs_0_, f32[4,32,128,128]{3,2,1,0:T(8,128)} %bitcast.22, f32[1024,128]{1,0:T(8,128)S(1)} %shard_map.86.refs_2_), custom_call_target="tpu_custom_call" | custom-call | flops 2147483648 | bytes 2097152 | tf_op jit(solution)/shard_map/pallas_call | solution.py:107
  49.0 3.0 %shard_map.88 = f32[1024,128]{1,0:T(8,128)S(1)} custom-call(s32[17,32]{1,0:T(8,128)S(1)} %concatenate.10.info, f32[1024,128]{1,0:T(8,128)S(1)} %collective-permute-done.7.refs_0_, f32[1024,128]{1,0:T(8,128)S(1)} %collective-permute-done.8.refs_1_, f32[4,32,128,128]{3,2,1,0:T(8,128)} %bitcast.23, f32[1024,128]{1,0:T(8,128)S(1)} %shard_map.87.refs_3_), custom_call_target="tpu_custom_call" | custom-call | flops 2147483648 | bytes 2097152 | tf_op jit(solution)/shard_map/pallas_call | solution.py:107
  52.0 16.6 %all_to_all.10.partials = f32[8,128,128]{2,1,0:T(8,128)} all-to-all(f32[8,128,128]{2,1,0:T(8,128)S(1)} %bitcast.20), channel_id=1, replica_groups=mesh['rep'=8,'blk'=32] {'rep'}, dimensions={0} | all-to-all | bytes 1048576 | tf_op jit(solution)/shard_map/all_to_all | solution.py:249
  68.6 2.6 %shard_map.89 = (f32[128,256]{1,0:T(8,128)}, f32[8,128,128]{2,1,0:T(8,128)}) custom-call(f32[8,128,128]{2,1,0:T(8,128)} %all_to_all.10.partials, f32[128,256]{1,0:T(8,128)} %weight.1, f32[128,256]{1,0:T(8,128)} %bitcast.28), custom_call_target="tpu_custom_call" | custom-call | tf_op jit(solution)/shard_map/pallas_call | solution.py:158
  71.2 13.9 %all_to_all.11 = f32[8,128,128]{2,1,0:T(8,128)S(1)} all-to-all(f32[8,128,128]{2,1,0:T(8,128)} %get-tuple-element.16), channel_id=1, replica_groups=mesh['rep'=8,'blk'=32] {'rep'}, dimensions={0} | all-to-all | bytes 1048576 | tf_op jit(solution)/shard_map/all_to_all | solution.py:253
  85.1 3.1 %shard_map.91 = f32[1024,128]{1,0:T(8,128)S(1)} custom-call(s32[17,32]{1,0:T(8,128)S(1)} %concatenate.10.info, f32[1024,128]{1,0:T(8,128)S(1)} %bitcast.16, f32[4,32,128,128]{3,2,1,0:T(8,128)} %bitcast.24), custom_call_target="tpu_custom_call" | custom-call | flops 2147483648 | bytes 2097152 | tf_op jit(solution)/shard_map/pallas_call | solution.py:107
  90.9 3.1 %shard_map.90 = f32[1024,128]{1,0:T(8,128)S(1)} custom-call(s32[17,32]{1,0:T(8,128)S(1)} %concatenate.10.info, f32[1024,128]{1,0:T(8,128)S(1)} %bitcast.17, f32[4,32,128,128]{3,2,1,0:T(8,128)} %bitcast.25), custom_call_target="tpu_custom_call" | custom-call | flops 2147483648 | bytes 2097152 | tf_op jit(solution)/shard_map/pallas_call | solution.py:107
  95.4 3.1 %shard_map.92 = f32[1024,128]{1,0:T(8,128)S(1)} custom-call(s32[17,32]{1,0:T(8,128)S(1)} %concatenate.10.info, f32[1024,128]{1,0:T(8,128)S(1)} %bitcast.18, f32[4,32,128,128]{3,2,1,0:T(8,128)} %bitcast.26), custom_call_target="tpu_custom_call" | custom-call | flops 2147483648 | bytes 2097152 | tf_op jit(solution)/shard_map/pallas_call | solution.py:107
  98.5 6.1 %collective-permute-start.12 = (f32[1024,128]{1,0:T(8,128)S(1)}, f32[1024,128]{1,0:T(8,128)S(1)}, u32[]{:S(2)}, u32[]{:S(2)}) collective-permute-start(f32[1024,128]{1,0:T(8,128)S(1)} %shard_map.92), channel_id=1, source_target_pairs={{1,0},{0,1},{3,2},{2,3},{5,4},{4,5},{7,6},{6,7},{9,8},{8,9},{11,10... | collective-permute-start | bytes 1572872 | tf_op jit(solution)/shard_map/ppermute | solution.py:265
  104.6 3.1 %shard_map.93 = f32[1024,128]{1,0:T(8,128)S(1)} custom-call(s32[17,32]{1,0:T(8,128)S(1)} %concatenate.10.info, f32[1024,128]{1,0:T(8,128)S(1)} %bitcast.19, f32[4,32,128,128]{3,2,1,0:T(8,128)} %bitcast.27), custom_call_target="tpu_custom_call" | custom-call | flops 2147483648 | bytes 2097152 | tf_op jit(solution)/shard_map/pallas_call | solution.py:107
  109.4 4.0 %collective-permute-start.16 = (f32[256,128]{1,0:T(8,128)S(1)}, f32[256,128]{1,0:T(8,128)S(1)}, u32[]{:S(2)}, u32[]{:S(2)}) collective-permute-start(f32[256,128]{1,0:T(8,128)S(1)} %get-tuple-element.22), channel_id=1, source_target_pairs={{0,160},{32,128},{64,224},{96,192},{128,32},{160,0},{192,96},{224,... | collective-permute-start | bytes 393224 | tf_op jit(solution)/shard_map/ppermute | solution.py:271
  118.2 4.0 %collective-permute-start.17 = (f32[256,128]{1,0:T(8,128)S(1)}, f32[256,128]{1,0:T(8,128)S(1)}, u32[]{:S(2)}, u32[]{:S(2)}) collective-permute-start(f32[256,128]{1,0:T(8,128)S(1)} %collective-permute-done.16), channel_id=1, source_target_pairs={{0,22},{1,23},{2,24},{3,25},{4,26},{5,27},{6,28},{7,29},{8,30},{9,... | collective-permute-start | bytes 393224 | tf_op jit(solution)/shard_map/ppermute | solution.py:209
  122.3 4.0 %collective-permute-done.18 = f32[256,128]{1,0:T(8,128)S(1)} collective-permute-done((f32[256,128]{1,0:T(8,128)S(1)}, f32[256,128]{1,0:T(8,128)S(1)}, u32[]{:S(2)}, u32[]{:S(2)}) %collective-permute-start.18) | collective-permute-done | bytes 131104 | tf_op jit(solution)/shard_map/ppermute | solution.py:271
  128.2 4.0 %collective-permute-done.17 = f32[256,128]{1,0:T(8,128)S(1)} collective-permute-done((f32[256,128]{1,0:T(8,128)S(1)}, f32[256,128]{1,0:T(8,128)S(1)}, u32[]{:S(2)}, u32[]{:S(2)}) %collective-permute-start.17) | collective-permute-done | bytes 131104 | tf_op jit(solution)/shard_map/ppermute | solution.py:209
  132.2 2.7 %collective-permute-done.19 = f32[256,128]{1,0:T(8,128)S(1)} collective-permute-done((f32[256,128]{1,0:T(8,128)S(1)}, f32[256,128]{1,0:T(8,128)S(1)}, u32[]{:S(2)}, u32[]{:S(2)}) %collective-permute-start.19) | collective-permute-done | bytes 131104 | tf_op jit(solution)/shard_map/ppermute | solution.py:209
  134.9 3.0 %collective-permute-start.20 = (f32[128,128]{1,0:T(8,128)S(1)}, f32[128,128]{1,0:T(8,128)S(1)}, u32[]{:S(2)}, u32[]{:S(2)}) collective-permute-start(f32[128,128]{1,0:T(8,128)S(1)} %split.9), channel_id=1, source_target_pairs={{32,0},{0,32},{96,64},{64,96},{160,128},{128,160},{224,192},{192,2... | collective-permute-start | bytes 196616 | tf_op jit(solution)/shard_map/ppermute | solution.py:276
  (45 shorter events, 24.6 us)
Async XLA Ops:
  0.6 4.6 %collective-permute-start = (f32[128,128]{1,0:T(8,128)}, f32[128,128]{1,0:T(8,128)S(1)}, u32[]{:S(2)}, u32[]{:S(2)}) collective-permute-start(f32[128,128]{1,0:T(8,128)} %bitcast.29), channel_id=1, source_target_pairs={{32,0},{0,32},{96,64},{64,96},{160,128},{128,160},{224,192},{192,2... | collective-permute-start | bytes 196616 | tf_op jit(solution)/shard_map/ppermute | solution.py:230
  5.2 14.3 %collective-permute-start.1 = (f32[256,128]{1,0:T(8,128)S(1)}, f32[256,128]{1,0:T(8,128)S(1)}, u32[]{:S(2)}, u32[]{:S(2)}) collective-permute-start(f32[256,128]{1,0:T(8,128)S(1)} %constant_dynamic-update-slice_fusion.4), channel_id=1, source_target_pairs={{2,0},{3,1},{4,2},{5,3},{6,4},{7,5},{8,6},{9,7},{10,8},{11,9},{12,... | collective-permute-start | bytes 393224 | tf_op jit(solution)/shard_map/ppermute | solution.py:203
  9.8 9.7 %collective-permute-start.2 = (f32[256,128]{1,0:T(8,128)S(1)}, f32[256,128]{1,0:T(8,128)S(1)}, u32[]{:S(2)}, u32[]{:S(2)}) collective-permute-start(f32[256,128]{1,0:T(8,128)S(1)} %constant_dynamic-update-slice_fusion.4), channel_id=1, source_target_pairs={{66,0},{67,1},{68,2},{69,3},{70,4},{71,5},{72,6},{73,7},{74,8},{75... | collective-permute-start | bytes 393224 | tf_op jit(solution)/shard_map/ppermute | solution.py:203
  15.3 9.6 %collective-permute-start.3 = (f32[256,128]{1,0:T(8,128)S(1)}, f32[256,128]{1,0:T(8,128)S(1)}, u32[]{:S(2)}, u32[]{:S(2)}) collective-permute-start(f32[256,128]{1,0:T(8,128)S(1)} %constant_dynamic-update-slice_fusion.4), channel_id=1, source_target_pairs={{130,0},{131,1},{132,2},{133,3},{134,4},{135,5},{136,6},{137,7},{1... | collective-permute-start | bytes 393224 | tf_op jit(solution)/shard_map/ppermute | solution.py:203
  16.9 11.5 %collective-permute-start.4 = (f32[256,128]{1,0:T(8,128)S(1)}, f32[256,128]{1,0:T(8,128)S(1)}, u32[]{:S(2)}, u32[]{:S(2)}) collective-permute-start(f32[256,128]{1,0:T(8,128)S(1)} %constant_dynamic-update-slice_fusion.4), channel_id=1, source_target_pairs={{194,0},{195,1},{196,2},{197,3},{198,4},{199,5},{200,6},{201,7},{2... | collective-permute-start | bytes 393224 | tf_op jit(solution)/shard_map/ppermute | solution.py:203
  28.5 5.7 %collective-permute-start.6 = (f32[1024,128]{1,0:T(8,128)S(1)}, f32[1024,128]{1,0:T(8,128)S(1)}, u32[]{:S(2)}, u32[]{:S(2)}) collective-permute-start(f32[1024,128]{1,0:T(8,128)S(1)} %constant_dynamic-update-slice_fusion.refs_0_), channel_id=1, source_target_pairs={{1,0},{0,1},{3,2},{2,3},{5,4},{4,5},{7,6},{6,7},{9,8},{8,9},{11,10... | collective-permute-start | bytes 1572872 | tf_op jit(solution)/shard_map/ppermute | solution.py:241
  28.6 16.1 %collective-permute-start.5 = (f32[1024,128]{1,0:T(8,128)S(1)}, f32[1024,128]{1,0:T(8,128)S(1)}, u32[]{:S(2)}, u32[]{:S(2)}) collective-permute-start(f32[1024,128]{1,0:T(8,128)S(1)} %constant_dynamic-update-slice_fusion.refs_0_), channel_id=1, source_target_pairs={{30,0},{143,1},{0,2},{1,3},{2,4},{3,5},{4,6},{5,7},{6,8},{7,9},{8,... | collective-permute-start | bytes 1572872 | tf_op jit(solution)/shard_map/ppermute | solution.py:203
  30.1 18.9 %collective-permute-start.8 = (f32[1024,128]{1,0:T(8,128)S(1)}, f32[1024,128]{1,0:T(8,128)S(1)}, u32[]{:S(2)}, u32[]{:S(2)}) collective-permute-start(f32[1024,128]{1,0:T(8,128)S(1)} %constant_dynamic-update-slice_fusion.refs_0_), channel_id=1, source_target_pairs={{0,31},{2,1},{4,3},{6,5},{8,7},{10,9},{12,11},{14,13},{16,15},{18,... | collective-permute-start | bytes 1572872 | tf_op jit(solution)/shard_map/ppermute | solution.py:221
  44.7 4.3 %collective-permute-start.7 = (f32[1024,128]{1,0:T(8,128)S(1)}, f32[1024,128]{1,0:T(8,128)S(1)}, u32[]{:S(2)}, u32[]{:S(2)}) collective-permute-start(f32[1024,128]{1,0:T(8,128)S(1)} %collective-permute-done.5.refs_0_), channel_id=1, source_target_pairs={{1,0},{3,2},{5,4},{7,6},{9,8},{11,10},{13,12},{15,14},{17,16},{19,... | collective-permute-start | bytes 1572872 | tf_op jit(solution)/shard_map/ppermute | solution.py:221
  88.2 5.8 %collective-permute-start.9 = (f32[1024,128]{1,0:T(8,128)S(1)}, f32[1024,128]{1,0:T(8,128)S(1)}, u32[]{:S(2)}, u32[]{:S(2)}) collective-permute-start(f32[1024,128]{1,0:T(8,128)S(1)} %shard_map.91), channel_id=1, source_target_pairs={{0,1},{2,3},{4,5},{6,7},{8,9},{10,11},{12,13},{14,15},{16,17},{18,... | collective-permute-start | bytes 1572872 | tf_op jit(solution)/shard_map/ppermute | solution.py:221
  89.6 18.1 %collective-permute-start.11 = (f32[1024,128]{1,0:T(8,128)S(1)}, f32[1024,128]{1,0:T(8,128)S(1)}, u32[]{:S(2)}, u32[]{:S(2)}) collective-permute-start(f32[1024,128]{1,0:T(8,128)S(1)} %shard_map.91), channel_id=1, source_target_pairs={{1,2},{3,4},{5,6},{7,8},{9,10},{11,12},{13,14},{15,16},{17,18},{19... | collective-permute-start | bytes 1572872 | tf_op jit(solution)/shard_map/ppermute | solution.py:221
  94.1 15.0 %collective-permute-start.10 = (f32[1024,128]{1,0:T(8,128)S(1)}, f32[1024,128]{1,0:T(8,128)S(1)}, u32[]{:S(2)}, u32[]{:S(2)}) collective-permute-start(f32[1024,128]{1,0:T(8,128)S(1)} %add.37), channel_id=1, source_target_pairs={{0,30},{1,143},{2,0},{3,1},{4,2},{5,3},{6,4},{7,5},{8,6},{9,7},{10... | collective-permute-start | bytes 1572872 | tf_op jit(solution)/shard_map/ppermute | solution.py:209
  98.5 10.7 %collective-permute-start.12 = (f32[1024,128]{1,0:T(8,128)S(1)}, f32[1024,128]{1,0:T(8,128)S(1)}, u32[]{:S(2)}, u32[]{:S(2)}) collective-permute-start(f32[1024,128]{1,0:T(8,128)S(1)} %shard_map.92), channel_id=1, source_target_pairs={{1,0},{0,1},{3,2},{2,3},{5,4},{4,5},{7,6},{6,7},{9,8},{8,9},{11,10... | collective-permute-start | bytes 1572872 | tf_op jit(solution)/shard_map/ppermute | solution.py:265
  109.2 8.0 %collective-permute-start.14 = (f32[256,128]{1,0:T(8,128)S(1)}, f32[256,128]{1,0:T(8,128)S(1)}, u32[]{:S(2)}, u32[]{:S(2)}) collective-permute-start(f32[256,128]{1,0:T(8,128)S(1)} %get-tuple-element.20), channel_id=1, source_target_pairs={{0,64},{32,96},{64,0},{96,32},{128,192},{160,224},{192,128},{224,1... | collective-permute-start | bytes 393224 | tf_op jit(solution)/shard_map/ppermute | solution.py:271
  109.4 8.8 %collective-permute-start.16 = (f32[256,128]{1,0:T(8,128)S(1)}, f32[256,128]{1,0:T(8,128)S(1)}, u32[]{:S(2)}, u32[]{:S(2)}) collective-permute-start(f32[256,128]{1,0:T(8,128)S(1)} %get-tuple-element.22), channel_id=1, source_target_pairs={{0,160},{32,128},{64,224},{96,192},{128,32},{160,0},{192,96},{224,... | collective-permute-start | bytes 393224 | tf_op jit(solution)/shard_map/ppermute | solution.py:271
  113.4 12.9 %collective-permute-start.18 = (f32[256,128]{1,0:T(8,128)S(1)}, f32[256,128]{1,0:T(8,128)S(1)}, u32[]{:S(2)}, u32[]{:S(2)}) collective-permute-start(f32[256,128]{1,0:T(8,128)S(1)} %get-tuple-element.21), channel_id=1, source_target_pairs={{0,224},{32,192},{64,160},{96,128},{128,96},{160,64},{192,32},{224... | collective-permute-start | bytes 393224 | tf_op jit(solution)/shard_map/ppermute | solution.py:271
  114.9 11.4 %collective-permute-start.13 = (f32[256,128]{1,0:T(8,128)S(1)}, f32[256,128]{1,0:T(8,128)S(1)}, u32[]{:S(2)}, u32[]{:S(2)}) collective-permute-start(f32[256,128]{1,0:T(8,128)S(1)} %get-tuple-element.23), channel_id=1, source_target_pairs={{0,2},{1,3},{2,4},{3,5},{4,6},{5,7},{6,8},{7,9},{8,10},{9,11},{10,... | collective-permute-start | bytes 393224 | tf_op jit(solution)/shard_map/ppermute | solution.py:209
  117.2 11.0 %collective-permute-start.15 = (f32[256,128]{1,0:T(8,128)S(1)}, f32[256,128]{1,0:T(8,128)S(1)}, u32[]{:S(2)}, u32[]{:S(2)}) collective-permute-start(f32[256,128]{1,0:T(8,128)S(1)} %collective-permute-done.14), channel_id=1, source_target_pairs={{0,10},{1,11},{2,12},{3,13},{4,14},{5,15},{6,16},{7,17},{8,18},{9,... | collective-permute-start | bytes 393224 | tf_op jit(solution)/shard_map/ppermute | solution.py:209
  118.2 13.9 %collective-permute-start.17 = (f32[256,128]{1,0:T(8,128)S(1)}, f32[256,128]{1,0:T(8,128)S(1)}, u32[]{:S(2)}, u32[]{:S(2)}) collective-permute-start(f32[256,128]{1,0:T(8,128)S(1)} %collective-permute-done.16), channel_id=1, source_target_pairs={{0,22},{1,23},{2,24},{3,25},{4,26},{5,27},{6,28},{7,29},{8,30},{9,... | collective-permute-start | bytes 393224 | tf_op jit(solution)/shard_map/ppermute | solution.py:209
  126.3 8.6 %collective-permute-start.19 = (f32[256,128]{1,0:T(8,128)S(1)}, f32[256,128]{1,0:T(8,128)S(1)}, u32[]{:S(2)}, u32[]{:S(2)}) collective-permute-start(f32[256,128]{1,0:T(8,128)S(1)} %collective-permute-done.18), channel_id=1, source_target_pairs={{0,30},{1,31},{2,0},{3,1},{4,2},{5,3},{6,4},{7,5},{8,6},{9,7},{10,... | collective-permute-start | bytes 393224 | tf_op jit(solution)/shard_map/ppermute | solution.py:209
  134.9 5.2 %collective-permute-start.20 = (f32[128,128]{1,0:T(8,128)S(1)}, f32[128,128]{1,0:T(8,128)S(1)}, u32[]{:S(2)}, u32[]{:S(2)}) collective-permute-start(f32[128,128]{1,0:T(8,128)S(1)} %split.9), channel_id=1, source_target_pairs={{32,0},{0,32},{96,64},{64,96},{160,128},{128,160},{224,192},{192,2... | collective-permute-start | bytes 196616 | tf_op jit(solution)/shard_map/ppermute | solution.py:276

commit v5 on v4

--- a/solution.py
+++ b/solution.py
@@ -9,9 +9,9 @@
 
 F32 = jnp.float32
 BF16 = jnp.bfloat16
-HIGHEST = lax.Precision.HIGHEST
 SIDE = 128
 CHUNK = 16
+LIMIT = 48
 NEAR, FAR, OUTER, LOWEST, CORE = 0, 2, 3, 2, 4
 
 
@@ -43,18 +43,36 @@
     return copy, chunks
 
 
-def multiply(part, section, copy, chunks, info, source, target, transposed, held, split, total):
+def multiply(left_of, part, section, chunks, info, source, target, split, total):
     @pl.loop(0, chunks)
     def _(chunk):
+        for left, number in left_of(part, chunk):
+            right = split[info[source + section, number]]
+            product = jnp.dot(left, right, preferred_element_type=F32)
+            row = info[target + section, number] * SIDE
+            total[pl.ds(pl.multiple_of(row, SIDE), SIDE), :] += product
+
+
+def fetched(parts, first, info, tiles, held, sems, transposed):
+    copy, chunks = tile_copies(parts, first, info, tiles, held, sems)
+
+    def left_of(part, chunk):
         copy(part, chunk).wait()
         for slot in range(CHUNK):
             number = chunk * CHUNK + slot
             tile = held[part, number]
-            left = jnp.concatenate(halves(tile.T if transposed else tile), axis=1)
-            right = split[info[source + section, number]]
-            product = jnp.dot(left, right, preferred_element_type=F32)
-            row = info[target + section, number] * SIDE
-            total[pl.ds(pl.multiple_of(row, SIDE), SIDE), :] += product
+            yield jnp.concatenate(halves(tile.T if transposed else tile), axis=1), number
+
+    return left_of, chunks
+
+
+def prepared(tiles):
+    def left_of(part, chunk):
+        for slot in range(CHUNK):
+            number = chunk * CHUNK + slot
+            yield tiles[number], number
+
+    return left_of, tiles.shape[0] // CHUNK
 
 
 def folded(total, nodes):
@@ -62,12 +80,26 @@
     return total[live, :SIDE] + total[live, SIDE:]
 
 
+def prepare_body(parts, first, transposed, info, tiles, *refs):
+    outs, (held, sems) = refs[:parts], refs[parts:]
+    left_of, chunks = fetched(parts, first, info, tiles, held, sems, transposed)
+    for part in range(parts):
+
+        @pl.loop(0, chunks)
+        def _(chunk, part=part):
+            for left, number in left_of(part, chunk):
+                outs[part][number] = left
+
+
 def forward_body(n_in, has_start, choose, first, info, *refs):
     panels, tiles = refs[:n_in], refs[n_in]
-    out, split, total, held, sems = refs[-5:]
+    out, split, total = refs[n_in + 1 + int(has_start) :][:3]
     nodes, parts = out.shape[0], n_in - int(choose)
     sections = info.shape[0] // 4
-    copy, chunks = tile_copies(parts, first, info, tiles, held, sems)
+    if tiles.dtype == F32:
+        left_of, chunks = fetched(parts, first, info, tiles, *refs[-2:], False)
+    else:
+        left_of, chunks = prepared(tiles)
     total[...] = jnp.zeros_like(total)
     for part in range(parts):
         for block in range(nodes // SIDE):
@@ -77,8 +109,7 @@
                 value = jnp.where(info[0, CORE] == 0, value, panels[parts][at, :])
             store_split(split, block, value)
         multiply(
-            part, info[0, first + part], copy, chunks, info, 1 + sections, 1, False,
-            held, split, total,
+            left_of, part, info[0, first + part], chunks, info, 1 + sections, 1, split, total
         )
     value = folded(total, nodes)
     out[...] = value + refs[n_in + 1][...] if has_start else value
@@ -86,70 +117,102 @@
 
 def backward_body(parts, first, info, panel, tiles, *refs):
     outs = refs[:parts]
-    split, total, held, sems = refs[parts:]
+    split, total = refs[parts : parts + 2]
     nodes = panel.shape[0]
     sections = info.shape[0] // 4
-    copy, chunks = tile_copies(parts, first, info, tiles, held, sems)
+    if tiles.dtype == F32:
+        left_of, chunks = fetched(parts, first, info, tiles, *refs[-2:], True)
+    else:
+        left_of, chunks = prepared(tiles)
     for block in range(nodes // SIDE):
         store_split(split, block, panel[pl.ds(block * SIDE, SIDE), :])
     for part in range(parts):
         total[...] = jnp.zeros_like(total)
         multiply(
-            part, info[0, first + part], copy, chunks, info, 1 + 2 * sections, 1 + 3 * sections,
-            True, held, split, total,
+            left_of, part, info[0, first + part], chunks, info, 1 + 2 * sections,
+            1 + 3 * sections, split, total,
         )
         outs[part][...] = folded(total, nodes)
 
 
-def tile_call(body, parts, info, panels, tiles, extra, n_out, cost):
-    slots, (nodes, features) = tiles.shape[1], panels[0].shape
+def local_call(body, parts, slots, info, panels, tiles, extra, outs, scratch):
     whole = pl.BlockSpec(memory_space=pltpu.VMEM)
+    raw = tiles.dtype == F32
+    if raw:
+        scratch = scratch + [
+            pltpu.VMEM((parts, slots, SIDE, SIDE), F32),
+            pltpu.SemaphoreType.DMA((parts, slots // CHUNK)),
+        ]
     return pl.pallas_call(
         body,
         in_specs=[pl.BlockSpec(memory_space=pltpu.SMEM)]
         + [whole] * len(panels)
-        + [pl.BlockSpec(memory_space=pltpu.HBM)]
+        + [pl.BlockSpec(memory_space=pltpu.HBM) if raw else whole]
         + [whole] * len(extra),
-        out_specs=[whole] * n_out,
-        scratch_shapes=[
-            pltpu.VMEM((nodes // SIDE, 2 * SIDE, 2 * SIDE), BF16),
-            pltpu.VMEM((nodes + SIDE, 2 * features), F32),
-            pltpu.VMEM((parts, slots, SIDE, SIDE), F32),
-            pltpu.SemaphoreType.DMA((parts, slots // CHUNK)),
-        ],
-        out_shape=[jax.ShapeDtypeStruct((nodes, features), F32)] * n_out,
-        compiler_params=pltpu.CompilerParams(vmem_limit_bytes=50 << 20),
+        out_specs=[whole] * len(outs),
+        scratch_shapes=scratch,
+        out_shape=outs,
+        compiler_params=pltpu.CompilerParams(vmem_limit_bytes=LIMIT << 20),
         cost_estimate=pl.CostEstimate(
-            flops=cost * parts * slots * SIDE * SIDE * features,
+            flops=32 * parts * slots * SIDE**3,
             bytes_accessed=4 * parts * slots * SIDE * SIDE,
             transcendentals=0,
         ),
     )(info, *panels, tiles, *extra)
 
 
+def tile_call(body, parts, info, panels, tiles, extra, n_out):
+    nodes, features = panels[0].shape
+    return local_call(
+        body, parts, tiles.shape[-3], info, panels, tiles, extra,
+        [jax.ShapeDtypeStruct((nodes, features), F32)] * n_out,
+        [
+            pltpu.VMEM((nodes // SIDE, 2 * SIDE, 2 * SIDE), BF16),
+            pltpu.VMEM((nodes + SIDE, 2 * features), F32),
+        ],
+    )
+
+
+def prepare(parts, first, transposed, info, tiles):
+    slots = tiles.shape[1]
+    body = functools.partial(prepare_body, parts, first, transposed)
+    shape = jax.ShapeDtypeStruct((slots, SIDE, 2 * SIDE), BF16)
+    return local_call(body, parts, slots, info, [], tiles, [], [shape] * parts, [])
+
+
 def forward_tiles(first, info, panels, tiles, start, choose):
     extra = [] if start is None else [start]
     body = functools.partial(forward_body, len(panels), start is not None, choose, first)
-    return tile_call(body, len(panels) - int(choose), info, panels, tiles, extra, 1, 32)[0]
-
-
-def backward_tiles(first, info, panel, tiles, parts, cost=32):
+    return tile_call(body, len(panels) - int(choose), info, panels, tiles, extra, 1)[0]
+
+
+def backward_tiles(first, info, panel, tiles, parts):
     body = functools.partial(backward_body, parts, first)
-    return tile_call(body, parts, info, [panel], tiles, [], parts, cost)
+    return tile_call(body, parts, info, [panel], tiles, [], parts)
+
+
+def widened(value):
+    both = jnp.concatenate(halves(value), axis=1)
+    return jnp.concatenate([both, both], axis=0)
+
+
+def split_dot(left, right):
+    wide = jnp.dot(
+        jnp.concatenate(halves(left), axis=1), widened(right), preferred_element_type=F32
+    )
+    middle = right.shape[1]
+    return wide[:, :middle] + wide[:, middle:]
 
 
 def dense_body(partials, weight, cotangent, hidden, spread):
     propagated = partials[0]
     for index in range(1, partials.shape[0]):
         propagated = propagated + partials[index]
-    preact = jnp.dot(propagated, weight[...], precision=HIGHEST, preferred_element_type=F32)
+    preact = split_dot(propagated, weight[...])
     gate = 1.0 / (1.0 + jnp.exp(-preact))
     hidden[...] = preact * gate
     grad_pre = cotangent[...] * gate * (1.0 + preact * (1.0 - gate))
-    grad = lax.dot_general(
-        grad_pre, weight[...], (((1,), (1,)), ((), ())),
-        precision=HIGHEST, preferred_element_type=F32,
-    )
+    grad = split_dot(grad_pre, weight[...].T)
     for index in range(spread.shape[0]):
         spread[index] = grad
 
@@ -230,28 +293,32 @@
         jnp.concatenate([own, own]), lax.ppermute(own, "rep", twin), (nodes, 0)
     )
     pair, info = lax.optimization_barrier((pair, info))
+    low_tiles, rest_tiles = prepare(2, FAR, False, info, tiles)
     base = jnp.concatenate(
         [
             joint(pair, lambda g, r, k=k: (g + sections * r + 2, r ^ (r >> 2) ^ (2 * k)))
             for k in range(replicas // 2)
         ]
     )
+    base, low_tiles, rest_tiles = lax.optimization_barrier((base, low_tiles, rest_tiles))
     lower = joint(base, below)
     upper = along(base, -1, evens)
     beside = lax.ppermute(base, "blk", swap)
     partial_sum = forward_tiles(NEAR, info, [base, beside], tiles, None, False)
     lower, partial_sum = lax.optimization_barrier((lower, partial_sum))
     lower_beside = along(lower, -1, odds)
-    partial_sum = forward_tiles(FAR, info, [lower], tiles, partial_sum, False)
+    partial_sum = forward_tiles(FAR, info, [lower], low_tiles, partial_sum, False)
     partial_sum = forward_tiles(
-        OUTER, info, [lower_beside, upper], tiles, partial_sum, True
-    )
+        OUTER, info, [lower_beside, upper], rest_tiles, partial_sum, True
+    )
+    late_info, partial_sum = lax.optimization_barrier((info, partial_sum))
+    (outer_tiles,) = prepare(1, OUTER, True, late_info, tiles)
     partials = lax.all_to_all(
         partial_sum.reshape(replicas, -1, own.shape[-1]), "rep", 0, 0, tiled=True
     )
     hidden, spread = dense(partials, weight, cotangent[0])
     grad_panel = lax.all_to_all(spread, "rep", 0, 0, tiled=True).reshape(base.shape)
-    (outer,) = backward_tiles(OUTER, info, grad_panel, tiles, 1)
+    (outer,) = backward_tiles(OUTER, info, grad_panel, outer_tiles, 1)
     outer_in = along(outer, 1, evens)
     to_lower = along(outer, 1, odds)
     (lowest,) = backward_tiles(LOWEST, info, grad_panel, tiles, 1)

time: 143 us -> 139 us (0.972)
  blocking collectives: 30.5 us -> 16.1 us
  starting transfers between devices: 44.6 us -> 51.6 us
  Pallas kernels: 25 us -> 27.4 us
    all_to_all x1 -> x0, blocking collectives: 13.9 us -> none  [shards(): lax.all_to_all(spread, 'rep', 0, 0, tiled=True).reshape(base.shape)]
    all_to_all x0 -> x1, starting transfers between devices: none -> 6.11 us  [shards(): lax.all_to_all(spread, 'rep', 0, 0, tiled=True).reshape(base.shape)]
    all_to_all x0 -> x1, waiting for transfers between devices: none -> 4.63 us  [shards(): lax.all_to_all(spread, 'rep', 0, 0, tiled=True).reshape(base.shape)]
    ppermute x5, waiting for transfers between devices: 15.4 us -> 12.3 us  [joint(): lax.ppermute(block, ('rep', 'blk'), [(device(*source(g, r)), device(g, r)...]
    pallas_call x7 -> x9, Pallas kernels: 22.4 us -> 25.1 us  [local_call(): pl.pallas_call(body, in_specs=[pl.BlockSpec(memory_space=pltpu.SMEM)] + [...]
  transfers between devices with their start and end apart: 21 -> 22, of which waited for: 12 -> 14; matrix products, arithmetic and copies ran while one was open for 2% -> 2% of each run, Pallas kernels for 12% -> 15%
where the time goes in v5:
time: 139 us; the launch traced here: 137 us
  starting transfers between devices  51.6 us (37%)
  waiting for transfers between devices  37.5 us (27%)
  Pallas kernels  27.4 us (20%)
  blocking collectives  16.1 us (12%)
  other arithmetic  2.62 us (2%)
    pallas_call x9, Pallas kernels, local_call(): pl.pallas_call(body, in_specs=[pl.BlockSpec(memory_space=pltpu.SMEM)] + [...  25.1 us
    all_to_all x1, blocking collectives, shards(): lax.all_to_all(partial_sum.reshape(replicas, -1, own.shape[-1]), 'rep', 0...  16.1 us
    ppermute x5, starting transfers between devices, joint(): lax.ppermute(block, ('rep', 'blk'), [(device(*source(g, r)), device(g, r)...  15.9 us
    ppermute x5, waiting for transfers between devices, joint(): lax.ppermute(block, ('rep', 'blk'), [(device(*source(g, r)), device(g, r)...  12.3 us
    ppermute x5, waiting for transfers between devices, back(): lax.ppermute(block, ('rep', 'blk'), [(device(g, r), device(*target(g, r))...  10.2 us
    ppermute x4, starting transfers between devices, along(): lax.ppermute(block, 'blk', [(g, (g + distance) % groups) for g in ids])  7.87 us
    ppermute x3, waiting for transfers between devices, shards(): part = lax.ppermute(part, 'rep', [(r, r ^ across) for r in range(replicas)])  6.32 us
    ppermute x1, starting transfers between devices, shards(): total = received + lax.ppermute(other, 'blk', swap)  6.12 us
  transfers between devices with their start and end apart: 22, of which 14 were waited for; matrix products, arithmetic and copies ran while one was open for 2% of the time, Pallas kernels for 15%

profile of v5, /device:TPU:26, one launch (start us, length us, event | category | flops | bytes accessed | tf_op | source)
XLA Modules:
  0.0 137.0 jit_solution(1913655317205597842)
XLA Ops:
  5.2 4.6 %collective-permute-start.1 = (f32[256,128]{1,0:T(8,128)S(1)}, f32[256,128]{1,0:T(8,128)S(1)}, u32[]{:S(2)}, u32[]{:S(2)}) collective-permute-start(f32[256,128]{1,0:T(8,128)S(1)} %constant_dynamic-update-slice_fusion), channel_id=1, source_target_pairs={{2,0},{3,1},{4,2},{5,3},{6,4},{7,5},{8,6},{9,7},{10,8},{11,9},{12,... | collective-permute-start | bytes 393224 | tf_op jit(solution)/shard_map/ppermute | solution.py:266
  9.8 5.5 %collective-permute-start.2 = (f32[256,128]{1,0:T(8,128)S(1)}, f32[256,128]{1,0:T(8,128)S(1)}, u32[]{:S(2)}, u32[]{:S(2)}) collective-permute-start(f32[256,128]{1,0:T(8,128)S(1)} %constant_dynamic-update-slice_fusion), channel_id=1, source_target_pairs={{66,0},{67,1},{68,2},{69,3},{70,4},{71,5},{72,6},{73,7},{74,8},{75... | collective-permute-start | bytes 393224 | tf_op jit(solution)/shard_map/ppermute | solution.py:266
  16.9 2.5 %collective-permute-start.4 = (f32[256,128]{1,0:T(8,128)S(1)}, f32[256,128]{1,0:T(8,128)S(1)}, u32[]{:S(2)}, u32[]{:S(2)}) collective-permute-start(f32[256,128]{1,0:T(8,128)S(1)} %constant_dynamic-update-slice_fusion), channel_id=1, source_target_pairs={{194,0},{195,1},{196,2},{197,3},{198,4},{199,5},{200,6},{201,7},{2... | collective-permute-start | bytes 393224 | tf_op jit(solution)/shard_map/ppermute | solution.py:266
  19.5 3.1 %shard_map.86 = (bf16[32,128,256]{2,1,0:T(8,128)(2,1)S(1)}, bf16[32,128,256]{2,1,0:T(8,128)(2,1)S(1)}) custom-call(s32[17,32]{1,0:T(8,128)S(1)} %concatenate.10.info, f32[4,32,128,128]{3,2,1,0:T(8,128)} %bitcast.21), custom_call_target="tpu_custom_call" | custom-call | flops 4294967296 | bytes 4194304 | tf_op jit(solution)/shard_map/pallas_call | solution.py:146
  22.6 2.3 %collective-permute-done.3 = f32[256,128]{1,0:T(8,128)S(1)} collective-permute-done((f32[256,128]{1,0:T(8,128)S(1)}, f32[256,128]{1,0:T(8,128)S(1)}, u32[]{:S(2)}, u32[]{:S(2)}) %collective-permute-start.3) | collective-permute-done | bytes 131104 | tf_op jit(solution)/shard_map/ppermute | solution.py:266
  24.9 3.6 %collective-permute-done.4 = f32[256,128]{1,0:T(8,128)S(1)} collective-permute-done((f32[256,128]{1,0:T(8,128)S(1)}, f32[256,128]{1,0:T(8,128)S(1)}, u32[]{:S(2)}, u32[]{:S(2)}) %collective-permute-start.4) | collective-permute-done | bytes 131104 | tf_op jit(solution)/shard_map/ppermute | solution.py:266
  30.2 4.0 %collective-permute-start.8 = (f32[1024,128]{1,0:T(8,128)S(1)}, f32[1024,128]{1,0:T(8,128)S(1)}, u32[]{:S(2)}, u32[]{:S(2)}) collective-permute-start(f32[1024,128]{1,0:T(8,128)S(1)} %pad_maximum_fusion.refs_0_), channel_id=1, source_target_pairs={{0,31},{2,1},{4,3},{6,5},{8,7},{10,9},{12,11},{14,13},{16,15},{18,... | collective-permute-start | bytes 1572872 | tf_op jit(solution)/shard_map/ppermute | solution.py:284
  34.2 4.1 %shard_map.87.refs_2_ = f32[1024,128]{1,0:T(8,128)S(1)} custom-call(s32[17,32]{1,0:T(8,128)S(1)} %concatenate.10.info, f32[1024,128]{1,0:T(8,128)S(1)} %pad_maximum_fusion.refs_0_, f32[1024,128]{1,0:T(8,128)S(1)} %collective-permute-done.6.refs_1_, f32[4,32,128,128]{3,2,1,0:T(8,128)} %bitcast.22), custom_call_target="tpu_custom_call" | custom-call | flops 4294967296 | bytes 4194304 | tf_op jit(solution)/shard_map/pallas_call | solution.py:146
  38.3 6.4 %collective-permute-done.5.refs_0_ = f32[1024,128]{1,0:T(8,128)S(1)} collective-permute-done((f32[1024,128]{1,0:T(8,128)S(1)}, f32[1024,128]{1,0:T(8,128)S(1)}, u32[]{:S(2)}, u32[]{:S(2)}) %collective-permute-start.5) | collective-permute-done | bytes 524320 | tf_op jit(solution)/shard_map/ppermute | solution.py:266
  50.5 16.1 %all_to_all.10.partials = f32[8,128,128]{2,1,0:T(8,128)} all-to-all(f32[8,128,128]{2,1,0:T(8,128)S(1)} %bitcast.20), channel_id=1, replica_groups=mesh['rep'=8,'blk'=32] {'rep'}, dimensions={0} | all-to-all | bytes 1048576 | tf_op jit(solution)/shard_map/all_to_all | solution.py:316
  66.6 2.3 %shard_map.90 = (f32[128,256]{1,0:T(8,128)}, f32[8,128,128]{2,1,0:T(8,128)}) custom-call(f32[8,128,128]{2,1,0:T(8,128)} %all_to_all.10.partials, f32[128,256]{1,0:T(8,128)} %weight.1, f32[128,256]{1,0:T(8,128)} %bitcast.27), custom_call_target="tpu_custom_call" | custom-call | tf_op jit(solution)/shard_map/pallas_call | solution.py:221
  68.9 6.1 %all-to-all-start.1 = ((f32[8,128,128]{2,1,0:T(8,128)}), f32[8,128,128]{2,1,0:T(8,128)S(1)}, u32[]{:S(2)}, u32[]{:S(2)}) async-start(f32[8,128,128]{2,1,0:T(8,128)} %get-tuple-element.29), calls=%async_computation.1 | async-start | bytes 1048576 | tf_op jit(solution)/shard_map/all_to_all | solution.py:320
  75.0 2.7 %shard_map.92.tiles = bf16[32,128,256]{2,1,0:T(8,128)(2,1)S(1)} custom-call(s32[17,32]{1,0:T(8,128)S(1)} %concatenate.10.info, f32[4,32,128,128]{3,2,1,0:T(8,128)} %bitcast.23), custom_call_target="tpu_custom_call" | custom-call | flops 2147483648 | bytes 2097152 | tf_op jit(solution)/shard_map/pallas_call | solution.py:146
  77.7 4.6 %all-to-all-done.1 = f32[8,128,128]{2,1,0:T(8,128)S(1)} async-done(((f32[8,128,128]{2,1,0:T(8,128)}), f32[8,128,128]{2,1,0:T(8,128)S(1)}, u32[]{:S(2)}, u32[]{:S(2)}) %all-to-all-start.1) | async-done | bytes 524320 | tf_op jit(solution)/shard_map/all_to_all | solution.py:320
  87.0 3.1 %shard_map.91 = f32[1024,128]{1,0:T(8,128)S(1)} custom-call(s32[17,32]{1,0:T(8,128)S(1)} %concatenate.10.info, f32[1024,128]{1,0:T(8,128)S(1)} %bitcast.17, f32[4,32,128,128]{3,2,1,0:T(8,128)} %bitcast.24), custom_call_target="tpu_custom_call" | custom-call | flops 2147483648 | bytes 2097152 | tf_op jit(solution)/shard_map/pallas_call | solution.py:146
  91.5 3.1 %shard_map.94 = f32[1024,128]{1,0:T(8,128)S(1)} custom-call(s32[17,32]{1,0:T(8,128)S(1)} %concatenate.10.info, f32[1024,128]{1,0:T(8,128)S(1)} %bitcast.18, f32[4,32,128,128]{3,2,1,0:T(8,128)} %bitcast.25), custom_call_target="tpu_custom_call" | custom-call | flops 2147483648 | bytes 2097152 | tf_op jit(solution)/shard_map/pallas_call | solution.py:146
  94.6 6.1 %collective-permute-start.12 = (f32[1024,128]{1,0:T(8,128)S(1)}, f32[1024,128]{1,0:T(8,128)S(1)}, u32[]{:S(2)}, u32[]{:S(2)}) collective-permute-start(f32[1024,128]{1,0:T(8,128)S(1)} %shard_map.94), channel_id=1, source_target_pairs={{1,0},{0,1},{3,2},{2,3},{5,4},{4,5},{7,6},{6,7},{9,8},{8,9},{11,10... | collective-permute-start | bytes 1572872 | tf_op jit(solution)/shard_map/ppermute | solution.py:332
  100.7 3.1 %shard_map.95 = f32[1024,128]{1,0:T(8,128)S(1)} custom-call(s32[17,32]{1,0:T(8,128)S(1)} %concatenate.10.info, f32[1024,128]{1,0:T(8,128)S(1)} %bitcast.19, f32[4,32,128,128]{3,2,1,0:T(8,128)} %bitcast.26), custom_call_target="tpu_custom_call" | custom-call | flops 2147483648 | bytes 2097152 | tf_op jit(solution)/shard_map/pallas_call | solution.py:146
  105.4 4.1 %collective-permute-start.16 = (f32[256,128]{1,0:T(8,128)S(1)}, f32[256,128]{1,0:T(8,128)S(1)}, u32[]{:S(2)}, u32[]{:S(2)}) collective-permute-start(f32[256,128]{1,0:T(8,128)S(1)} %get-tuple-element.36), channel_id=1, source_target_pairs={{0,160},{32,128},{64,224},{96,192},{128,32},{160,0},{192,96},{224,... | collective-permute-start | bytes 393224 | tf_op jit(solution)/shard_map/ppermute | solution.py:338
  114.3 4.0 %collective-permute-start.17 = (f32[256,128]{1,0:T(8,128)S(1)}, f32[256,128]{1,0:T(8,128)S(1)}, u32[]{:S(2)}, u32[]{:S(2)}) collective-permute-start(f32[256,128]{1,0:T(8,128)S(1)} %collective-permute-done.16), channel_id=1, source_target_pairs={{0,22},{1,23},{2,24},{3,25},{4,26},{5,27},{6,28},{7,29},{8,30},{9,... | collective-permute-start | bytes 393224 | tf_op jit(solution)/shard_map/ppermute | solution.py:272
  118.3 3.0 %collective-permute-done.18 = f32[256,128]{1,0:T(8,128)S(1)} collective-permute-done((f32[256,128]{1,0:T(8,128)S(1)}, f32[256,128]{1,0:T(8,128)S(1)}, u32[]{:S(2)}, u32[]{:S(2)}) %collective-permute-start.18) | collective-permute-done | bytes 131104 | tf_op jit(solution)/shard_map/ppermute | solution.py:338
  121.3 3.2 %collective-permute-done.15 = f32[256,128]{1,0:T(8,128)S(1)} collective-permute-done((f32[256,128]{1,0:T(8,128)S(1)}, f32[256,128]{1,0:T(8,128)S(1)}, u32[]{:S(2)}, u32[]{:S(2)}) %collective-permute-start.15) | collective-permute-done | bytes 131104 | tf_op jit(solution)/shard_map/ppermute | solution.py:272
  124.5 4.3 %collective-permute-done.17 = f32[256,128]{1,0:T(8,128)S(1)} collective-permute-done((f32[256,128]{1,0:T(8,128)S(1)}, f32[256,128]{1,0:T(8,128)S(1)}, u32[]{:S(2)}, u32[]{:S(2)}) %collective-permute-start.17) | collective-permute-done | bytes 131104 | tf_op jit(solution)/shard_map/ppermute | solution.py:272
  130.2 3.9 %collective-permute-start.20 = (f32[128,128]{1,0:T(8,128)S(1)}, f32[128,128]{1,0:T(8,128)S(1)}, u32[]{:S(2)}, u32[]{:S(2)}) collective-permute-start(f32[128,128]{1,0:T(8,128)S(1)} %split.9), channel_id=1, source_target_pairs={{32,0},{0,32},{96,64},{64,96},{160,128},{128,160},{224,192},{192,2... | collective-permute-start | bytes 196616 | tf_op jit(solution)/shard_map/ppermute | solution.py:343
  (45 shorter events, 30.3 us)
Async XLA Ops:
  0.6 4.6 %collective-permute-start = (f32[128,128]{1,0:T(8,128)}, f32[128,128]{1,0:T(8,128)S(1)}, u32[]{:S(2)}, u32[]{:S(2)}) collective-permute-start(f32[128,128]{1,0:T(8,128)} %bitcast.28), channel_id=1, source_target_pairs={{32,0},{0,32},{96,64},{64,96},{160,128},{128,160},{224,192},{192,2... | collective-permute-start | bytes 196616 | tf_op jit(solution)/shard_map/ppermute | solution.py:293
  5.2 17.4 %collective-permute-start.1 = (f32[256,128]{1,0:T(8,128)S(1)}, f32[256,128]{1,0:T(8,128)S(1)}, u32[]{:S(2)}, u32[]{:S(2)}) collective-permute-start(f32[256,128]{1,0:T(8,128)S(1)} %constant_dynamic-update-slice_fusion), channel_id=1, source_target_pairs={{2,0},{3,1},{4,2},{5,3},{6,4},{7,5},{8,6},{9,7},{10,8},{11,9},{12,... | collective-permute-start | bytes 393224 | tf_op jit(solution)/shard_map/ppermute | solution.py:266
  9.8 12.8 %collective-permute-start.2 = (f32[256,128]{1,0:T(8,128)S(1)}, f32[256,128]{1,0:T(8,128)S(1)}, u32[]{:S(2)}, u32[]{:S(2)}) collective-permute-start(f32[256,128]{1,0:T(8,128)S(1)} %constant_dynamic-update-slice_fusion), channel_id=1, source_target_pairs={{66,0},{67,1},{68,2},{69,3},{70,4},{71,5},{72,6},{73,7},{74,8},{75... | collective-permute-start | bytes 393224 | tf_op jit(solution)/shard_map/ppermute | solution.py:266
  15.3 9.6 %collective-permute-start.3 = (f32[256,128]{1,0:T(8,128)S(1)}, f32[256,128]{1,0:T(8,128)S(1)}, u32[]{:S(2)}, u32[]{:S(2)}) collective-permute-start(f32[256,128]{1,0:T(8,128)S(1)} %constant_dynamic-update-slice_fusion), channel_id=1, source_target_pairs={{130,0},{131,1},{132,2},{133,3},{134,4},{135,5},{136,6},{137,7},{1... | collective-permute-start | bytes 393224 | tf_op jit(solution)/shard_map/ppermute | solution.py:266
  16.9 11.5 %collective-permute-start.4 = (f32[256,128]{1,0:T(8,128)S(1)}, f32[256,128]{1,0:T(8,128)S(1)}, u32[]{:S(2)}, u32[]{:S(2)}) collective-permute-start(f32[256,128]{1,0:T(8,128)S(1)} %constant_dynamic-update-slice_fusion), channel_id=1, source_target_pairs={{194,0},{195,1},{196,2},{197,3},{198,4},{199,5},{200,6},{201,7},{2... | collective-permute-start | bytes 393224 | tf_op jit(solution)/shard_map/ppermute | solution.py:266
  28.5 5.7 %collective-permute-start.6 = (f32[1024,128]{1,0:T(8,128)S(1)}, f32[1024,128]{1,0:T(8,128)S(1)}, u32[]{:S(2)}, u32[]{:S(2)}) collective-permute-start(f32[1024,128]{1,0:T(8,128)S(1)} %pad_maximum_fusion.refs_0_), channel_id=1, source_target_pairs={{1,0},{0,1},{3,2},{2,3},{5,4},{4,5},{7,6},{6,7},{9,8},{8,9},{11,10... | collective-permute-start | bytes 1572872 | tf_op jit(solution)/shard_map/ppermute | solution.py:306
  28.6 16.1 %collective-permute-start.5 = (f32[1024,128]{1,0:T(8,128)S(1)}, f32[1024,128]{1,0:T(8,128)S(1)}, u32[]{:S(2)}, u32[]{:S(2)}) collective-permute-start(f32[1024,128]{1,0:T(8,128)S(1)} %pad_maximum_fusion.refs_0_), channel_id=1, source_target_pairs={{30,0},{143,1},{0,2},{1,3},{2,4},{3,5},{4,6},{5,7},{6,8},{7,9},{8,... | collective-permute-start | bytes 1572872 | tf_op jit(solution)/shard_map/ppermute | solution.py:266
  30.2 17.8 %collective-permute-start.8 = (f32[1024,128]{1,0:T(8,128)S(1)}, f32[1024,128]{1,0:T(8,128)S(1)}, u32[]{:S(2)}, u32[]{:S(2)}) collective-permute-start(f32[1024,128]{1,0:T(8,128)S(1)} %pad_maximum_fusion.refs_0_), channel_id=1, source_target_pairs={{0,31},{2,1},{4,3},{6,5},{8,7},{10,9},{12,11},{14,13},{16,15},{18,... | collective-permute-start | bytes 1572872 | tf_op jit(solution)/shard_map/ppermute | solution.py:284
  44.7 3.8 %collective-permute-start.7 = (f32[1024,128]{1,0:T(8,128)S(1)}, f32[1024,128]{1,0:T(8,128)S(1)}, u32[]{:S(2)}, u32[]{:S(2)}) collective-permute-start(f32[1024,128]{1,0:T(8,128)S(1)} %collective-permute-done.5.refs_0_), channel_id=1, source_target_pairs={{1,0},{3,2},{5,4},{7,6},{9,8},{11,10},{13,12},{15,14},{17,16},{19,... | collective-permute-start | bytes 1572872 | tf_op jit(solution)/shard_map/ppermute | solution.py:284
  68.9 13.4 %all-to-all-start.1 = ((f32[8,128,128]{2,1,0:T(8,128)}), f32[8,128,128]{2,1,0:T(8,128)S(1)}, u32[]{:S(2)}, u32[]{:S(2)}) async-start(f32[8,128,128]{2,1,0:T(8,128)} %get-tuple-element.29), calls=%async_computation.1 | async-start | bytes 1048576 | tf_op jit(solution)/shard_map/all_to_all | solution.py:320
  84.3 5.7 %collective-permute-start.9 = (f32[1024,128]{1,0:T(8,128)S(1)}, f32[1024,128]{1,0:T(8,128)S(1)}, u32[]{:S(2)}, u32[]{:S(2)}) collective-permute-start(f32[1024,128]{1,0:T(8,128)S(1)} %shard_map.93), channel_id=1, source_target_pairs={{0,1},{2,3},{4,5},{6,7},{8,9},{10,11},{12,13},{14,15},{16,17},{18,... | collective-permute-start | bytes 1572872 | tf_op jit(solution)/shard_map/ppermute | solution.py:284
  85.7 18.1 %collective-permute-start.11 = (f32[1024,128]{1,0:T(8,128)S(1)}, f32[1024,128]{1,0:T(8,128)S(1)}, u32[]{:S(2)}, u32[]{:S(2)}) collective-permute-start(f32[1024,128]{1,0:T(8,128)S(1)} %shard_map.93), channel_id=1, source_target_pairs={{1,2},{3,4},{5,6},{7,8},{9,10},{11,12},{13,14},{15,16},{17,18},{19... | collective-permute-start | bytes 1572872 | tf_op jit(solution)/shard_map/ppermute | solution.py:284
  90.1 15.0 %collective-permute-start.10 = (f32[1024,128]{1,0:T(8,128)S(1)}, f32[1024,128]{1,0:T(8,128)S(1)}, u32[]{:S(2)}, u32[]{:S(2)}) collective-permute-start(f32[1024,128]{1,0:T(8,128)S(1)} %add.37), channel_id=1, source_target_pairs={{0,30},{1,143},{2,0},{3,1},{4,2},{5,3},{6,4},{7,5},{8,6},{9,7},{10... | collective-permute-start | bytes 1572872 | tf_op jit(solution)/shard_map/ppermute | solution.py:272
  94.6 10.6 %collective-permute-start.12 = (f32[1024,128]{1,0:T(8,128)S(1)}, f32[1024,128]{1,0:T(8,128)S(1)}, u32[]{:S(2)}, u32[]{:S(2)}) collective-permute-start(f32[1024,128]{1,0:T(8,128)S(1)} %shard_map.94), channel_id=1, source_target_pairs={{1,0},{0,1},{3,2},{2,3},{5,4},{4,5},{7,6},{6,7},{9,8},{8,9},{11,10... | collective-permute-start | bytes 1572872 | tf_op jit(solution)/shard_map/ppermute | solution.py:332
  105.3 7.9 %collective-permute-start.14 = (f32[256,128]{1,0:T(8,128)S(1)}, f32[256,128]{1,0:T(8,128)S(1)}, u32[]{:S(2)}, u32[]{:S(2)}) collective-permute-start(f32[256,128]{1,0:T(8,128)S(1)} %get-tuple-element.34), channel_id=1, source_target_pairs={{0,64},{32,96},{64,0},{96,32},{128,192},{160,224},{192,128},{224,1... | collective-permute-start | bytes 393224 | tf_op jit(solution)/shard_map/ppermute | solution.py:338
  105.4 8.9 %collective-permute-start.16 = (f32[256,128]{1,0:T(8,128)S(1)}, f32[256,128]{1,0:T(8,128)S(1)}, u32[]{:S(2)}, u32[]{:S(2)}) collective-permute-start(f32[256,128]{1,0:T(8,128)S(1)} %get-tuple-element.36), channel_id=1, source_target_pairs={{0,160},{32,128},{64,224},{96,192},{128,32},{160,0},{192,96},{224,... | collective-permute-start | bytes 393224 | tf_op jit(solution)/shard_map/ppermute | solution.py:338
  109.5 11.8 %collective-permute-start.18 = (f32[256,128]{1,0:T(8,128)S(1)}, f32[256,128]{1,0:T(8,128)S(1)}, u32[]{:S(2)}, u32[]{:S(2)}) collective-permute-start(f32[256,128]{1,0:T(8,128)S(1)} %get-tuple-element.35), channel_id=1, source_target_pairs={{0,224},{32,192},{64,160},{96,128},{128,96},{160,64},{192,32},{224... | collective-permute-start | bytes 393224 | tf_op jit(solution)/shard_map/ppermute | solution.py:338
  111.0 10.3 %collective-permute-start.13 = (f32[256,128]{1,0:T(8,128)S(1)}, f32[256,128]{1,0:T(8,128)S(1)}, u32[]{:S(2)}, u32[]{:S(2)}) collective-permute-start(f32[256,128]{1,0:T(8,128)S(1)} %get-tuple-element.37), channel_id=1, source_target_pairs={{0,2},{1,3},{2,4},{3,5},{4,6},{5,7},{6,8},{7,9},{8,10},{9,11},{10,... | collective-permute-start | bytes 393224 | tf_op jit(solution)/shard_map/ppermute | solution.py:272
  113.2 11.3 %collective-permute-start.15 = (f32[256,128]{1,0:T(8,128)S(1)}, f32[256,128]{1,0:T(8,128)S(1)}, u32[]{:S(2)}, u32[]{:S(2)}) collective-permute-start(f32[256,128]{1,0:T(8,128)S(1)} %collective-permute-done.14), channel_id=1, source_target_pairs={{0,10},{1,11},{2,12},{3,13},{4,14},{5,15},{6,16},{7,17},{8,18},{9,... | collective-permute-start | bytes 393224 | tf_op jit(solution)/shard_map/ppermute | solution.py:272
  114.3 14.6 %collective-permute-start.17 = (f32[256,128]{1,0:T(8,128)S(1)}, f32[256,128]{1,0:T(8,128)S(1)}, u32[]{:S(2)}, u32[]{:S(2)}) collective-permute-start(f32[256,128]{1,0:T(8,128)S(1)} %collective-permute-done.16), channel_id=1, source_target_pairs={{0,22},{1,23},{2,24},{3,25},{4,26},{5,27},{6,28},{7,29},{8,30},{9,... | collective-permute-start | bytes 393224 | tf_op jit(solution)/shard_map/ppermute | solution.py:272
  121.3 8.9 %collective-permute-start.19 = (f32[256,128]{1,0:T(8,128)S(1)}, f32[256,128]{1,0:T(8,128)S(1)}, u32[]{:S(2)}, u32[]{:S(2)}) collective-permute-start(f32[256,128]{1,0:T(8,128)S(1)} %collective-permute-done.18), channel_id=1, source_target_pairs={{0,30},{1,31},{2,0},{3,1},{4,2},{5,3},{6,4},{7,5},{8,6},{9,7},{10,... | collective-permute-start | bytes 393224 | tf_op jit(solution)/shard_map/ppermute | solution.py:272
  130.2 6.1 %collective-permute-start.20 = (f32[128,128]{1,0:T(8,128)S(1)}, f32[128,128]{1,0:T(8,128)S(1)}, u32[]{:S(2)}, u32[]{:S(2)}) collective-permute-start(f32[128,128]{1,0:T(8,128)S(1)} %split.9), channel_id=1, source_target_pairs={{32,0},{0,32},{96,64},{64,96},{160,128},{128,160},{224,192},{192,2... | collective-permute-start | bytes 196616 | tf_op jit(solution)/shard_map/ppermute | solution.py:343

commit v6 on v5

--- a/solution.py
+++ b/solution.py
@@ -11,7 +11,7 @@
 BF16 = jnp.bfloat16
 SIDE = 128
 CHUNK = 16
-LIMIT = 48
+LIMIT, DENSE_LIMIT = 48, 16
 NEAR, FAR, OUTER, LOWEST, CORE = 0, 2, 3, 2, 4
 
 
@@ -226,6 +226,7 @@
         ],
         in_specs=[pl.BlockSpec(memory_space=pltpu.VMEM)] * 3,
         out_specs=[pl.BlockSpec(memory_space=pltpu.VMEM)] * 2,
+        compiler_params=pltpu.CompilerParams(vmem_limit_bytes=DENSE_LIMIT << 20),
     )(partials, weight, cotangent)
 
 
@@ -320,10 +321,11 @@
     grad_panel = lax.all_to_all(spread, "rep", 0, 0, tiled=True).reshape(base.shape)
     (outer,) = backward_tiles(OUTER, info, grad_panel, outer_tiles, 1)
     outer_in = along(outer, 1, evens)
-    to_lower = along(outer, 1, odds)
     (lowest,) = backward_tiles(LOWEST, info, grad_panel, tiles, 1)
     combined = lowest + outer_in
     from_upper = back(combined, below)
+    outer, combined = lax.optimization_barrier((outer, combined))
+    to_lower = along(outer, 1, odds)
     late_panel, _ = lax.optimization_barrier((grad_panel, combined))
     (other,) = backward_tiles(NEAR + 1, info, late_panel, tiles, 1)
     late_panel, other = lax.optimization_barrier((late_panel, other))

time: 139 us -> 138 us (level)
  transfers between devices with their start and end apart: 22 -> 22, of which waited for: 14 -> 14; matrix products, arithmetic and copies ran while one was open for 2% -> 2% of each run, Pallas kernels for 15% -> 16%
where the time goes in v6:
time: 138 us; the launch traced here: 136 us
  starting transfers between devices  51.1 us (37%)
  waiting for transfers between devices  38 us (28%)
  Pallas kernels  26.4 us (19%)
  blocking collectives  16 us (12%)
  other arithmetic  2.64 us (2%)
    pallas_call x9, Pallas kernels, local_call(): pl.pallas_call(body, in_specs=[pl.BlockSpec(memory_space=pltpu.SMEM)] + [...  25.2 us
    all_to_all x1, blocking collectives, shards(): lax.all_to_all(partial_sum.reshape(replicas, -1, own.shape[-1]), 'rep', 0...  16 us
    ppermute x5, starting transfers between devices, joint(): lax.ppermute(block, ('rep', 'blk'), [(device(*source(g, r)), device(g, r)...  15.9 us
    ppermute x5, waiting for transfers between devices, joint(): lax.ppermute(block, ('rep', 'blk'), [(device(*source(g, r)), device(g, r)...  12.3 us
    ppermute x5, waiting for transfers between devices, back(): lax.ppermute(block, ('rep', 'blk'), [(device(g, r), device(*target(g, r))...  9.94 us
    ppermute x4, starting transfers between devices, along(): lax.ppermute(block, 'blk', [(g, (g + distance) % groups) for g in ids])  7.87 us
    ppermute x3, waiting for transfers between devices, shards(): part = lax.ppermute(part, 'rep', [(r, r ^ across) for r in range(replicas)])  7.13 us
    ppermute x1, starting transfers between devices, shards(): total = received + lax.ppermute(other, 'blk', swap)  6.15 us
  transfers between devices with their start and end apart: 22, of which 14 were waited for; matrix products, arithmetic and copies ran while one was open for 2% of the time, Pallas kernels for 16%

profile of v6, /device:TPU:26, one launch (start us, length us, event | category | flops | bytes accessed | tf_op | source)
XLA Modules:
  0.0 135.9 jit_solution(9216725874931649591)
XLA Ops:
  5.2 4.6 %collective-permute-start.1 = (f32[256,128]{1,0:T(8,128)S(1)}, f32[256,128]{1,0:T(8,128)S(1)}, u32[]{:S(2)}, u32[]{:S(2)}) collective-permute-start(f32[256,128]{1,0:T(8,128)S(1)} %constant_dynamic-update-slice_fusion), channel_id=1, source_target_pairs={{2,0},{3,1},{4,2},{5,3},{6,4},{7,5},{8,6},{9,7},{10,8},{11,9},{12,... | collective-permute-start | bytes 393224 | tf_op jit(solution)/shard_map/ppermute | solution.py:267
  9.8 5.5 %collective-permute-start.2 = (f32[256,128]{1,0:T(8,128)S(1)}, f32[256,128]{1,0:T(8,128)S(1)}, u32[]{:S(2)}, u32[]{:S(2)}) collective-permute-start(f32[256,128]{1,0:T(8,128)S(1)} %constant_dynamic-update-slice_fusion), channel_id=1, source_target_pairs={{66,0},{67,1},{68,2},{69,3},{70,4},{71,5},{72,6},{73,7},{74,8},{75... | collective-permute-start | bytes 393224 | tf_op jit(solution)/shard_map/ppermute | solution.py:267
  16.9 2.5 %collective-permute-start.4 = (f32[256,128]{1,0:T(8,128)S(1)}, f32[256,128]{1,0:T(8,128)S(1)}, u32[]{:S(2)}, u32[]{:S(2)}) collective-permute-start(f32[256,128]{1,0:T(8,128)S(1)} %constant_dynamic-update-slice_fusion), channel_id=1, source_target_pairs={{194,0},{195,1},{196,2},{197,3},{198,4},{199,5},{200,6},{201,7},{2... | collective-permute-start | bytes 393224 | tf_op jit(solution)/shard_map/ppermute | solution.py:267
  19.5 3.1 %shard_map.86 = (bf16[32,128,256]{2,1,0:T(8,128)(2,1)S(1)}, bf16[32,128,256]{2,1,0:T(8,128)(2,1)S(1)}) custom-call(s32[17,32]{1,0:T(8,128)S(1)} %concatenate.10.info, f32[4,32,128,128]{3,2,1,0:T(8,128)} %bitcast.22), custom_call_target="tpu_custom_call" | custom-call | flops 4294967296 | bytes 4194304 | tf_op jit(solution)/shard_map/pallas_call | solution.py:146
  22.6 2.3 %collective-permute-done.3 = f32[256,128]{1,0:T(8,128)S(1)} collective-permute-done((f32[256,128]{1,0:T(8,128)S(1)}, f32[256,128]{1,0:T(8,128)S(1)}, u32[]{:S(2)}, u32[]{:S(2)}) %collective-permute-start.3) | collective-permute-done | bytes 131104 | tf_op jit(solution)/shard_map/ppermute | solution.py:267
  24.9 3.6 %collective-permute-done.4 = f32[256,128]{1,0:T(8,128)S(1)} collective-permute-done((f32[256,128]{1,0:T(8,128)S(1)}, f32[256,128]{1,0:T(8,128)S(1)}, u32[]{:S(2)}, u32[]{:S(2)}) %collective-permute-start.4) | collective-permute-done | bytes 131104 | tf_op jit(solution)/shard_map/ppermute | solution.py:267
  30.2 4.0 %collective-permute-start.8 = (f32[1024,128]{1,0:T(8,128)S(1)}, f32[1024,128]{1,0:T(8,128)S(1)}, u32[]{:S(2)}, u32[]{:S(2)}) collective-permute-start(f32[1024,128]{1,0:T(8,128)S(1)} %pad_maximum_fusion.refs_0_), channel_id=1, source_target_pairs={{0,31},{2,1},{4,3},{6,5},{8,7},{10,9},{12,11},{14,13},{16,15},{18,... | collective-permute-start | bytes 1572872 | tf_op jit(solution)/shard_map/ppermute | solution.py:285
  34.2 4.1 %shard_map.87.refs_2_ = f32[1024,128]{1,0:T(8,128)S(1)} custom-call(s32[17,32]{1,0:T(8,128)S(1)} %concatenate.10.info, f32[1024,128]{1,0:T(8,128)S(1)} %pad_maximum_fusion.refs_0_, f32[1024,128]{1,0:T(8,128)S(1)} %collective-permute-done.6.refs_1_, f32[4,32,128,128]{3,2,1,0:T(8,128)} %bitcast.23), custom_call_target="tpu_custom_call" | custom-call | flops 4294967296 | bytes 4194304 | tf_op jit(solution)/shard_map/pallas_call | solution.py:146
  38.3 6.4 %collective-permute-done.5.refs_0_ = f32[1024,128]{1,0:T(8,128)S(1)} collective-permute-done((f32[1024,128]{1,0:T(8,128)S(1)}, f32[1024,128]{1,0:T(8,128)S(1)}, u32[]{:S(2)}, u32[]{:S(2)}) %collective-permute-start.5) | collective-permute-done | bytes 524320 | tf_op jit(solution)/shard_map/ppermute | solution.py:267
  50.6 16.0 %all_to_all.10.partials = f32[8,128,128]{2,1,0:T(8,128)S(1)} all-to-all(f32[8,128,128]{2,1,0:T(8,128)S(1)} %bitcast.20), channel_id=1, replica_groups=mesh['rep'=8,'blk'=32] {'rep'}, dimensions={0} | all-to-all | bytes 1048576 | tf_op jit(solution)/shard_map/all_to_all | solution.py:317
  67.8 6.1 %all-to-all-start.1 = ((f32[8,128,128]{2,1,0:T(8,128)}), f32[8,128,128]{2,1,0:T(8,128)S(1)}, u32[]{:S(2)}, u32[]{:S(2)}) async-start(f32[8,128,128]{2,1,0:T(8,128)} %get-tuple-element.29), calls=%async_computation.1 | async-start | bytes 1048576 | tf_op jit(solution)/shard_map/all_to_all | solution.py:321
  73.9 2.7 %shard_map.94.tiles = bf16[32,128,256]{2,1,0:T(8,128)(2,1)S(1)} custom-call(s32[17,32]{1,0:T(8,128)S(1)} %concatenate.10.info, f32[4,32,128,128]{3,2,1,0:T(8,128)} %bitcast.24), custom_call_target="tpu_custom_call" | custom-call | flops 2147483648 | bytes 2097152 | tf_op jit(solution)/shard_map/pallas_call | solution.py:146
  76.6 4.6 %all-to-all-done.1 = f32[8,128,128]{2,1,0:T(8,128)S(1)} async-done(((f32[8,128,128]{2,1,0:T(8,128)}), f32[8,128,128]{2,1,0:T(8,128)S(1)}, u32[]{:S(2)}, u32[]{:S(2)}) %all-to-all-start.1) | async-done | bytes 524320 | tf_op jit(solution)/shard_map/all_to_all | solution.py:321
  84.5 3.1 %shard_map.93 = f32[1024,128]{1,0:T(8,128)S(1)} custom-call(s32[17,32]{1,0:T(8,128)S(1)} %concatenate.10.info, f32[1024,128]{1,0:T(8,128)S(1)} %bitcast.17, f32[4,32,128,128]{3,2,1,0:T(8,128)} %bitcast.25), custom_call_target="tpu_custom_call" | custom-call | flops 2147483648 | bytes 2097152 | tf_op jit(solution)/shard_map/pallas_call | solution.py:146
  90.3 3.1 %shard_map.91 = f32[1024,128]{1,0:T(8,128)S(1)} custom-call(s32[17,32]{1,0:T(8,128)S(1)} %concatenate.10.info, f32[1024,128]{1,0:T(8,128)S(1)} %bitcast.18, f32[4,32,128,128]{3,2,1,0:T(8,128)} %bitcast.26), custom_call_target="tpu_custom_call" | custom-call | flops 2147483648 | bytes 2097152 | tf_op jit(solution)/shard_map/pallas_call | solution.py:146
  93.4 6.1 %collective-permute-start.12 = (f32[1024,128]{1,0:T(8,128)S(1)}, f32[1024,128]{1,0:T(8,128)S(1)}, u32[]{:S(2)}, u32[]{:S(2)}) collective-permute-start(f32[1024,128]{1,0:T(8,128)S(1)} %shard_map.91), channel_id=1, source_target_pairs={{1,0},{0,1},{3,2},{2,3},{5,4},{4,5},{7,6},{6,7},{9,8},{8,9},{11,10... | collective-permute-start | bytes 1572872 | tf_op jit(solution)/shard_map/ppermute | solution.py:334
  99.5 3.1 %shard_map.92 = f32[1024,128]{1,0:T(8,128)S(1)} custom-call(s32[17,32]{1,0:T(8,128)S(1)} %concatenate.10.info, f32[1024,128]{1,0:T(8,128)S(1)} %bitcast.19, f32[4,32,128,128]{3,2,1,0:T(8,128)} %bitcast.27), custom_call_target="tpu_custom_call" | custom-call | flops 2147483648 | bytes 2097152 | tf_op jit(solution)/shard_map/pallas_call | solution.py:146
  104.3 4.1 %collective-permute-start.16 = (f32[256,128]{1,0:T(8,128)S(1)}, f32[256,128]{1,0:T(8,128)S(1)}, u32[]{:S(2)}, u32[]{:S(2)}) collective-permute-start(f32[256,128]{1,0:T(8,128)S(1)} %get-tuple-element.36), channel_id=1, source_target_pairs={{0,160},{32,128},{64,224},{96,192},{128,32},{160,0},{192,96},{224,... | collective-permute-start | bytes 393224 | tf_op jit(solution)/shard_map/ppermute | solution.py:340
  109.9 2.3 %collective-permute-done.14 = f32[256,128]{1,0:T(8,128)S(1)} collective-permute-done((f32[256,128]{1,0:T(8,128)S(1)}, f32[256,128]{1,0:T(8,128)S(1)}, u32[]{:S(2)}, u32[]{:S(2)}) %collective-permute-start.14) | collective-permute-done | bytes 131104 | tf_op jit(solution)/shard_map/ppermute | solution.py:340
  113.2 4.0 %collective-permute-start.17 = (f32[256,128]{1,0:T(8,128)S(1)}, f32[256,128]{1,0:T(8,128)S(1)}, u32[]{:S(2)}, u32[]{:S(2)}) collective-permute-start(f32[256,128]{1,0:T(8,128)S(1)} %collective-permute-done.16), channel_id=1, source_target_pairs={{0,22},{1,23},{2,24},{3,25},{4,26},{5,27},{6,28},{7,29},{8,30},{9,... | collective-permute-start | bytes 393224 | tf_op jit(solution)/shard_map/ppermute | solution.py:273
  117.2 3.8 %collective-permute-done.18 = f32[256,128]{1,0:T(8,128)S(1)} collective-permute-done((f32[256,128]{1,0:T(8,128)S(1)}, f32[256,128]{1,0:T(8,128)S(1)}, u32[]{:S(2)}, u32[]{:S(2)}) %collective-permute-start.18) | collective-permute-done | bytes 131104 | tf_op jit(solution)/shard_map/ppermute | solution.py:340
  123.1 4.0 %collective-permute-done.17 = f32[256,128]{1,0:T(8,128)S(1)} collective-permute-done((f32[256,128]{1,0:T(8,128)S(1)}, f32[256,128]{1,0:T(8,128)S(1)}, u32[]{:S(2)}, u32[]{:S(2)}) %collective-permute-start.17) | collective-permute-done | bytes 131104 | tf_op jit(solution)/shard_map/ppermute | solution.py:273
  127.1 2.5 %collective-permute-done.19 = f32[256,128]{1,0:T(8,128)S(1)} collective-permute-done((f32[256,128]{1,0:T(8,128)S(1)}, f32[256,128]{1,0:T(8,128)S(1)}, u32[]{:S(2)}, u32[]{:S(2)}) %collective-permute-start.19) | collective-permute-done | bytes 131104 | tf_op jit(solution)/shard_map/ppermute | solution.py:273
  129.7 3.3 %collective-permute-start.20 = (f32[128,128]{1,0:T(8,128)S(1)}, f32[128,128]{1,0:T(8,128)S(1)}, u32[]{:S(2)}, u32[]{:S(2)}) collective-permute-start(f32[128,128]{1,0:T(8,128)S(1)} %split.9), channel_id=1, source_target_pairs={{32,0},{0,32},{96,64},{64,96},{160,128},{128,160},{224,192},{192,2... | collective-permute-start | bytes 196616 | tf_op jit(solution)/shard_map/ppermute | solution.py:345
  (49 shorter events, 30.1 us)
Async XLA Ops:
  0.6 4.6 %collective-permute-start = (f32[128,128]{1,0:T(8,128)}, f32[128,128]{1,0:T(8,128)S(1)}, u32[]{:S(2)}, u32[]{:S(2)}) collective-permute-start(f32[128,128]{1,0:T(8,128)} %bitcast.28), channel_id=1, source_target_pairs={{32,0},{0,32},{96,64},{64,96},{160,128},{128,160},{224,192},{192,2... | collective-permute-start | bytes 196616 | tf_op jit(solution)/shard_map/ppermute | solution.py:294
  5.2 17.4 %collective-permute-start.1 = (f32[256,128]{1,0:T(8,128)S(1)}, f32[256,128]{1,0:T(8,128)S(1)}, u32[]{:S(2)}, u32[]{:S(2)}) collective-permute-start(f32[256,128]{1,0:T(8,128)S(1)} %constant_dynamic-update-slice_fusion), channel_id=1, source_target_pairs={{2,0},{3,1},{4,2},{5,3},{6,4},{7,5},{8,6},{9,7},{10,8},{11,9},{12,... | collective-permute-start | bytes 393224 | tf_op jit(solution)/shard_map/ppermute | solution.py:267
  9.8 12.8 %collective-permute-start.2 = (f32[256,128]{1,0:T(8,128)S(1)}, f32[256,128]{1,0:T(8,128)S(1)}, u32[]{:S(2)}, u32[]{:S(2)}) collective-permute-start(f32[256,128]{1,0:T(8,128)S(1)} %constant_dynamic-update-slice_fusion), channel_id=1, source_target_pairs={{66,0},{67,1},{68,2},{69,3},{70,4},{71,5},{72,6},{73,7},{74,8},{75... | collective-permute-start | bytes 393224 | tf_op jit(solution)/shard_map/ppermute | solution.py:267
  15.3 9.6 %collective-permute-start.3 = (f32[256,128]{1,0:T(8,128)S(1)}, f32[256,128]{1,0:T(8,128)S(1)}, u32[]{:S(2)}, u32[]{:S(2)}) collective-permute-start(f32[256,128]{1,0:T(8,128)S(1)} %constant_dynamic-update-slice_fusion), channel_id=1, source_target_pairs={{130,0},{131,1},{132,2},{133,3},{134,4},{135,5},{136,6},{137,7},{1... | collective-permute-start | bytes 393224 | tf_op jit(solution)/shard_map/ppermute | solution.py:267
  16.9 11.5 %collective-permute-start.4 = (f32[256,128]{1,0:T(8,128)S(1)}, f32[256,128]{1,0:T(8,128)S(1)}, u32[]{:S(2)}, u32[]{:S(2)}) collective-permute-start(f32[256,128]{1,0:T(8,128)S(1)} %constant_dynamic-update-slice_fusion), channel_id=1, source_target_pairs={{194,0},{195,1},{196,2},{197,3},{198,4},{199,5},{200,6},{201,7},{2... | collective-permute-start | bytes 393224 | tf_op jit(solution)/shard_map/ppermute | solution.py:267
  28.5 5.7 %collective-permute-start.6 = (f32[1024,128]{1,0:T(8,128)S(1)}, f32[1024,128]{1,0:T(8,128)S(1)}, u32[]{:S(2)}, u32[]{:S(2)}) collective-permute-start(f32[1024,128]{1,0:T(8,128)S(1)} %pad_maximum_fusion.refs_0_), channel_id=1, source_target_pairs={{1,0},{0,1},{3,2},{2,3},{5,4},{4,5},{7,6},{6,7},{9,8},{8,9},{11,10... | collective-permute-start | bytes 1572872 | tf_op jit(solution)/shard_map/ppermute | solution.py:307
  28.6 16.1 %collective-permute-start.5 = (f32[1024,128]{1,0:T(8,128)S(1)}, f32[1024,128]{1,0:T(8,128)S(1)}, u32[]{:S(2)}, u32[]{:S(2)}) collective-permute-start(f32[1024,128]{1,0:T(8,128)S(1)} %pad_maximum_fusion.refs_0_), channel_id=1, source_target_pairs={{30,0},{143,1},{0,2},{1,3},{2,4},{3,5},{4,6},{5,7},{6,8},{7,9},{8,... | collective-permute-start | bytes 1572872 | tf_op jit(solution)/shard_map/ppermute | solution.py:267
  30.2 17.9 %collective-permute-start.8 = (f32[1024,128]{1,0:T(8,128)S(1)}, f32[1024,128]{1,0:T(8,128)S(1)}, u32[]{:S(2)}, u32[]{:S(2)}) collective-permute-start(f32[1024,128]{1,0:T(8,128)S(1)} %pad_maximum_fusion.refs_0_), channel_id=1, source_target_pairs={{0,31},{2,1},{4,3},{6,5},{8,7},{10,9},{12,11},{14,13},{16,15},{18,... | collective-permute-start | bytes 1572872 | tf_op jit(solution)/shard_map/ppermute | solution.py:285
  44.7 3.8 %collective-permute-start.7 = (f32[1024,128]{1,0:T(8,128)S(1)}, f32[1024,128]{1,0:T(8,128)S(1)}, u32[]{:S(2)}, u32[]{:S(2)}) collective-permute-start(f32[1024,128]{1,0:T(8,128)S(1)} %collective-permute-done.5.refs_0_), channel_id=1, source_target_pairs={{1,0},{3,2},{5,4},{7,6},{9,8},{11,10},{13,12},{15,14},{17,16},{19,... | collective-permute-start | bytes 1572872 | tf_op jit(solution)/shard_map/ppermute | solution.py:285
  48.1 18.5 %copy-start = (f32[128,256]{1,0:T(8,128)S(1)}, f32[128,256]{1,0:T(8,128)}, u32[]{:S(2)}) copy-start(f32[128,256]{1,0:T(8,128)} %weight.1) | copy-start | bytes 393220
  48.1 18.5 %copy-start.1 = (f32[1,128,256]{2,1,0:T(8,128)S(1)}, f32[1,128,256]{2,1,0:T(8,128)}, u32[]{:S(2)}) copy-start(f32[1,128,256]{2,1,0:T(8,128)} %param.9) | copy-start | bytes 393220
  67.8 13.4 %all-to-all-start.1 = ((f32[8,128,128]{2,1,0:T(8,128)}), f32[8,128,128]{2,1,0:T(8,128)S(1)}, u32[]{:S(2)}, u32[]{:S(2)}) async-start(f32[8,128,128]{2,1,0:T(8,128)} %get-tuple-element.29), calls=%async_computation.1 | async-start | bytes 1048576 | tf_op jit(solution)/shard_map/all_to_all | solution.py:321
  83.2 4.4 %collective-permute-start.9 = (f32[1024,128]{1,0:T(8,128)S(1)}, f32[1024,128]{1,0:T(8,128)S(1)}, u32[]{:S(2)}, u32[]{:S(2)}) collective-permute-start(f32[1024,128]{1,0:T(8,128)S(1)} %shard_map.95), channel_id=1, source_target_pairs={{0,1},{2,3},{4,5},{6,7},{8,9},{10,11},{12,13},{14,15},{16,17},{18,... | collective-permute-start | bytes 1572872 | tf_op jit(solution)/shard_map/ppermute | solution.py:285
  87.7 14.9 %collective-permute-start.11 = (f32[1024,128]{1,0:T(8,128)S(1)}, f32[1024,128]{1,0:T(8,128)S(1)}, u32[]{:S(2)}, u32[]{:S(2)}) collective-permute-start(f32[1024,128]{1,0:T(8,128)S(1)} %shard_map.95), channel_id=1, source_target_pairs={{1,2},{3,4},{5,6},{7,8},{9,10},{11,12},{13,14},{15,16},{17,18},{19... | collective-permute-start | bytes 1572872 | tf_op jit(solution)/shard_map/ppermute | solution.py:285
  89.0 15.0 %collective-permute-start.10 = (f32[1024,128]{1,0:T(8,128)S(1)}, f32[1024,128]{1,0:T(8,128)S(1)}, u32[]{:S(2)}, u32[]{:S(2)}) collective-permute-start(f32[1024,128]{1,0:T(8,128)S(1)} %add.37), channel_id=1, source_target_pairs={{0,30},{1,143},{2,0},{3,1},{4,2},{5,3},{6,4},{7,5},{8,6},{9,7},{10... | collective-permute-start | bytes 1572872 | tf_op jit(solution)/shard_map/ppermute | solution.py:273
  93.4 10.7 %collective-permute-start.12 = (f32[1024,128]{1,0:T(8,128)S(1)}, f32[1024,128]{1,0:T(8,128)S(1)}, u32[]{:S(2)}, u32[]{:S(2)}) collective-permute-start(f32[1024,128]{1,0:T(8,128)S(1)} %shard_map.91), channel_id=1, source_target_pairs={{1,0},{0,1},{3,2},{2,3},{5,4},{4,5},{7,6},{6,7},{9,8},{8,9},{11,10... | collective-permute-start | bytes 1572872 | tf_op jit(solution)/shard_map/ppermute | solution.py:334
  104.2 8.0 %collective-permute-start.14 = (f32[256,128]{1,0:T(8,128)S(1)}, f32[256,128]{1,0:T(8,128)S(1)}, u32[]{:S(2)}, u32[]{:S(2)}) collective-permute-start(f32[256,128]{1,0:T(8,128)S(1)} %get-tuple-element.34), channel_id=1, source_target_pairs={{0,64},{32,96},{64,0},{96,32},{128,192},{160,224},{192,128},{224,1... | collective-permute-start | bytes 393224 | tf_op jit(solution)/shard_map/ppermute | solution.py:340
  104.3 8.8 %collective-permute-start.16 = (f32[256,128]{1,0:T(8,128)S(1)}, f32[256,128]{1,0:T(8,128)S(1)}, u32[]{:S(2)}, u32[]{:S(2)}) collective-permute-start(f32[256,128]{1,0:T(8,128)S(1)} %get-tuple-element.36), channel_id=1, source_target_pairs={{0,160},{32,128},{64,224},{96,192},{128,32},{160,0},{192,96},{224,... | collective-permute-start | bytes 393224 | tf_op jit(solution)/shard_map/ppermute | solution.py:340
  108.4 12.7 %collective-permute-start.18 = (f32[256,128]{1,0:T(8,128)S(1)}, f32[256,128]{1,0:T(8,128)S(1)}, u32[]{:S(2)}, u32[]{:S(2)}) collective-permute-start(f32[256,128]{1,0:T(8,128)S(1)} %get-tuple-element.35), channel_id=1, source_target_pairs={{0,224},{32,192},{64,160},{96,128},{128,96},{160,64},{192,32},{224... | collective-permute-start | bytes 393224 | tf_op jit(solution)/shard_map/ppermute | solution.py:340
  109.9 11.2 %collective-permute-start.13 = (f32[256,128]{1,0:T(8,128)S(1)}, f32[256,128]{1,0:T(8,128)S(1)}, u32[]{:S(2)}, u32[]{:S(2)}) collective-permute-start(f32[256,128]{1,0:T(8,128)S(1)} %get-tuple-element.37), channel_id=1, source_target_pairs={{0,2},{1,3},{2,4},{3,5},{4,6},{5,7},{6,8},{7,9},{8,10},{9,11},{10,... | collective-permute-start | bytes 393224 | tf_op jit(solution)/shard_map/ppermute | solution.py:273
  112.2 11.0 %collective-permute-start.15 = (f32[256,128]{1,0:T(8,128)S(1)}, f32[256,128]{1,0:T(8,128)S(1)}, u32[]{:S(2)}, u32[]{:S(2)}) collective-permute-start(f32[256,128]{1,0:T(8,128)S(1)} %collective-permute-done.14), channel_id=1, source_target_pairs={{0,10},{1,11},{2,12},{3,13},{4,14},{5,15},{6,16},{7,17},{8,18},{9,... | collective-permute-start | bytes 393224 | tf_op jit(solution)/shard_map/ppermute | solution.py:273
  113.2 14.0 %collective-permute-start.17 = (f32[256,128]{1,0:T(8,128)S(1)}, f32[256,128]{1,0:T(8,128)S(1)}, u32[]{:S(2)}, u32[]{:S(2)}) collective-permute-start(f32[256,128]{1,0:T(8,128)S(1)} %collective-permute-done.16), channel_id=1, source_target_pairs={{0,22},{1,23},{2,24},{3,25},{4,26},{5,27},{6,28},{7,29},{8,30},{9,... | collective-permute-start | bytes 393224 | tf_op jit(solution)/shard_map/ppermute | solution.py:273
  121.0 8.6 %collective-permute-start.19 = (f32[256,128]{1,0:T(8,128)S(1)}, f32[256,128]{1,0:T(8,128)S(1)}, u32[]{:S(2)}, u32[]{:S(2)}) collective-permute-start(f32[256,128]{1,0:T(8,128)S(1)} %collective-permute-done.18), channel_id=1, source_target_pairs={{0,30},{1,31},{2,0},{3,1},{4,2},{5,3},{6,4},{7,5},{8,6},{9,7},{10,... | collective-permute-start | bytes 393224 | tf_op jit(solution)/shard_map/ppermute | solution.py:273
  129.7 5.6 %collective-permute-start.20 = (f32[128,128]{1,0:T(8,128)S(1)}, f32[128,128]{1,0:T(8,128)S(1)}, u32[]{:S(2)}, u32[]{:S(2)}) collective-permute-start(f32[128,128]{1,0:T(8,128)S(1)} %split.9), channel_id=1, source_target_pairs={{32,0},{0,32},{96,64},{64,96},{160,128},{128,160},{224,192},{192,2... | collective-permute-start | bytes 196616 | tf_op jit(solution)/shard_map/ppermute | solution.py:345

commit v7 on v6

--- a/solution.py
+++ b/solution.py
@@ -269,10 +269,10 @@
             [(device(*source(g, r)), device(g, r)) for r in range(replicas) for g in range(groups)],
         )
 
-    def back(block, target):
+    def back(block, target, ids=range(groups)):
         return lax.ppermute(
             block, ("rep", "blk"),
-            [(device(g, r), device(*target(g, r))) for r in range(replicas) for g in range(groups)],
+            [(device(g, r), device(*target(g, r))) for r in range(replicas) for g in ids],
         )
 
     def below(group, replica):
@@ -313,24 +313,25 @@
         OUTER, info, [lower_beside, upper], rest_tiles, partial_sum, True
     )
     late_info, partial_sum = lax.optimization_barrier((info, partial_sum))
-    (outer_tiles,) = prepare(1, OUTER, True, late_info, tiles)
+    (lowest_tiles,) = prepare(1, LOWEST, True, late_info, tiles)
     partials = lax.all_to_all(
         partial_sum.reshape(replicas, -1, own.shape[-1]), "rep", 0, 0, tiled=True
     )
     hidden, spread = dense(partials, weight, cotangent[0])
     grad_panel = lax.all_to_all(spread, "rep", 0, 0, tiled=True).reshape(base.shape)
-    (outer,) = backward_tiles(OUTER, info, grad_panel, outer_tiles, 1)
-    outer_in = along(outer, 1, evens)
-    (lowest,) = backward_tiles(LOWEST, info, grad_panel, tiles, 1)
-    combined = lowest + outer_in
-    from_upper = back(combined, below)
+    (lowest,) = backward_tiles(LOWEST, info, grad_panel, lowest_tiles, 1)
+    from_even = back(lowest, below, evens)
+    next_panel, lowest = lax.optimization_barrier((grad_panel, lowest))
+    (outer,) = backward_tiles(OUTER, info, next_panel, tiles, 1)
+    combined = lowest + along(outer, 1, evens)
+    from_odd = back(combined, below, odds)
     outer, combined = lax.optimization_barrier((outer, combined))
     to_lower = along(outer, 1, odds)
     late_panel, _ = lax.optimization_barrier((grad_panel, combined))
     (other,) = backward_tiles(NEAR + 1, info, late_panel, tiles, 1)
     late_panel, other = lax.optimization_barrier((late_panel, other))
     (mine,) = backward_tiles(NEAR, info, late_panel, tiles, 1)
-    received = lax.optimization_barrier(mine + from_upper + to_lower)
+    received = lax.optimization_barrier(mine + from_even + to_lower + from_odd)
     total = received + lax.ppermute(other, "blk", swap)
     parts = total.reshape(replicas // 2, -1, own.shape[-1])
     pair_sum = 0.0

time: 138 us -> 141 us (1.022)
  starting transfers between devices: 51.1 us -> 57.2 us
  waiting for transfers between devices: 38 us -> 34.9 us
    ppermute x3, waiting for transfers between devices: 7.13 us -> 3.79 us  [shards(): part = lax.ppermute(part, 'rep', [(r, r ^ across) for r in range(replicas)])]
    ppermute x5 -> x6, starting transfers between devices: 5.37 us -> 7.77 us  [back(): lax.ppermute(block, ('rep', 'blk'), [(device(g, r), device(*target(g, r))...]
    ppermute x1, starting transfers between devices: 3.32 us -> 5.71 us  [shards(): feature_grad = kept + lax.ppermute(sent, 'rep', twin)]
    ppermute x5 -> x6, waiting for transfers between devices: 9.94 us -> 10.2 us  [back(): lax.ppermute(block, ('rep', 'blk'), [(device(g, r), device(*target(g, r))...]
  transfers between devices with their start and end apart: 22 -> 23, of which waited for: 14 -> 12; matrix products, arithmetic and copies ran while one was open for 2% -> 2% of each run, Pallas kernels for 16% -> 13%
where the time goes in v7:
time: 141 us; the launch traced here: 139 us
  starting transfers between devices  57.2 us (41%)
  waiting for transfers between devices  34.9 us (25%)
  Pallas kernels  26.4 us (19%)
  blocking collectives  16 us (11%)
  other arithmetic  2.72 us (2%)
    pallas_call x9, Pallas kernels, local_call(): pl.pallas_call(body, in_specs=[pl.BlockSpec(memory_space=pltpu.SMEM)] + [...  25.2 us
    all_to_all x1, blocking collectives, shards(): lax.all_to_all(partial_sum.reshape(replicas, -1, own.shape[-1]), 'rep', 0...  16 us
    ppermute x5, starting transfers between devices, joint(): lax.ppermute(block, ('rep', 'blk'), [(device(*source(g, r)), device(g, r)...  15.9 us
    ppermute x5, waiting for transfers between devices, joint(): lax.ppermute(block, ('rep', 'blk'), [(device(*source(g, r)), device(g, r)...  12.3 us
    ppermute x6, waiting for transfers between devices, back(): lax.ppermute(block, ('rep', 'blk'), [(device(g, r), device(*target(g, r))...  10.2 us
    ppermute x4, starting transfers between devices, along(): lax.ppermute(block, 'blk', [(g, (g + distance) % groups) for g in ids])  7.87 us
    ppermute x6, starting transfers between devices, back(): lax.ppermute(block, ('rep', 'blk'), [(device(g, r), device(*target(g, r))...  7.77 us
    ppermute x1, starting transfers between devices, shards(): total = received + lax.ppermute(other, 'blk', swap)  7.44 us
  transfers between devices with their start and end apart: 23, of which 12 were waited for; matrix products, arithmetic and copies ran while one was open for 2% of the time, Pallas kernels for 13%

profile of v7, /device:TPU:26, one launch (start us, length us, event | category | flops | bytes accessed | tf_op | source)
XLA Modules:
  0.0 139.0 jit_solution(2144027014911915464)
XLA Ops:
  5.2 4.6 %collective-permute-start.1 = (f32[256,128]{1,0:T(8,128)S(1)}, f32[256,128]{1,0:T(8,128)S(1)}, u32[]{:S(2)}, u32[]{:S(2)}) collective-permute-start(f32[256,128]{1,0:T(8,128)S(1)} %constant_dynamic-update-slice_fusion), channel_id=1, source_target_pairs={{2,0},{3,1},{4,2},{5,3},{6,4},{7,5},{8,6},{9,7},{10,8},{11,9},{12,... | collective-permute-start | bytes 393224 | tf_op jit(solution)/shard_map/ppermute | solution.py:267
  9.8 5.5 %collective-permute-start.2 = (f32[256,128]{1,0:T(8,128)S(1)}, f32[256,128]{1,0:T(8,128)S(1)}, u32[]{:S(2)}, u32[]{:S(2)}) collective-permute-start(f32[256,128]{1,0:T(8,128)S(1)} %constant_dynamic-update-slice_fusion), channel_id=1, source_target_pairs={{66,0},{67,1},{68,2},{69,3},{70,4},{71,5},{72,6},{73,7},{74,8},{75... | collective-permute-start | bytes 393224 | tf_op jit(solution)/shard_map/ppermute | solution.py:267
  16.9 2.5 %collective-permute-start.4 = (f32[256,128]{1,0:T(8,128)S(1)}, f32[256,128]{1,0:T(8,128)S(1)}, u32[]{:S(2)}, u32[]{:S(2)}) collective-permute-start(f32[256,128]{1,0:T(8,128)S(1)} %constant_dynamic-update-slice_fusion), channel_id=1, source_target_pairs={{194,0},{195,1},{196,2},{197,3},{198,4},{199,5},{200,6},{201,7},{2... | collective-permute-start | bytes 393224 | tf_op jit(solution)/shard_map/ppermute | solution.py:267
  19.5 3.1 %shard_map.86 = (bf16[32,128,256]{2,1,0:T(8,128)(2,1)S(1)}, bf16[32,128,256]{2,1,0:T(8,128)(2,1)S(1)}) custom-call(s32[17,32]{1,0:T(8,128)S(1)} %concatenate.10.info, f32[4,32,128,128]{3,2,1,0:T(8,128)} %bitcast.22), custom_call_target="tpu_custom_call" | custom-call | flops 4294967296 | bytes 4194304 | tf_op jit(solution)/shard_map/pallas_call | solution.py:146
  22.6 2.3 %collective-permute-done.3 = f32[256,128]{1,0:T(8,128)S(1)} collective-permute-done((f32[256,128]{1,0:T(8,128)S(1)}, f32[256,128]{1,0:T(8,128)S(1)}, u32[]{:S(2)}, u32[]{:S(2)}) %collective-permute-start.3) | collective-permute-done | bytes 131104 | tf_op jit(solution)/shard_map/ppermute | solution.py:267
  24.9 3.6 %collective-permute-done.4 = f32[256,128]{1,0:T(8,128)S(1)} collective-permute-done((f32[256,128]{1,0:T(8,128)S(1)}, f32[256,128]{1,0:T(8,128)S(1)}, u32[]{:S(2)}, u32[]{:S(2)}) %collective-permute-start.4) | collective-permute-done | bytes 131104 | tf_op jit(solution)/shard_map/ppermute | solution.py:267
  30.2 4.0 %collective-permute-start.8 = (f32[1024,128]{1,0:T(8,128)S(1)}, f32[1024,128]{1,0:T(8,128)S(1)}, u32[]{:S(2)}, u32[]{:S(2)}) collective-permute-start(f32[1024,128]{1,0:T(8,128)S(1)} %pad_maximum_fusion.refs_0_), channel_id=1, source_target_pairs={{0,31},{2,1},{4,3},{6,5},{8,7},{10,9},{12,11},{14,13},{16,15},{18,... | collective-permute-start | bytes 1572872 | tf_op jit(solution)/shard_map/ppermute | solution.py:285
  34.2 4.1 %shard_map.87.refs_2_ = f32[1024,128]{1,0:T(8,128)S(1)} custom-call(s32[17,32]{1,0:T(8,128)S(1)} %concatenate.10.info, f32[1024,128]{1,0:T(8,128)S(1)} %pad_maximum_fusion.refs_0_, f32[1024,128]{1,0:T(8,128)S(1)} %collective-permute-done.6.refs_1_, f32[4,32,128,128]{3,2,1,0:T(8,128)} %bitcast.23), custom_call_target="tpu_custom_call" | custom-call | flops 4294967296 | bytes 4194304 | tf_op jit(solution)/shard_map/pallas_call | solution.py:146
  38.3 6.4 %collective-permute-done.5.refs_0_ = f32[1024,128]{1,0:T(8,128)S(1)} collective-permute-done((f32[1024,128]{1,0:T(8,128)S(1)}, f32[1024,128]{1,0:T(8,128)S(1)}, u32[]{:S(2)}, u32[]{:S(2)}) %collective-permute-start.5) | collective-permute-done | bytes 524320 | tf_op jit(solution)/shard_map/ppermute | solution.py:267
  50.6 16.0 %all_to_all.10.partials = f32[8,128,128]{2,1,0:T(8,128)S(1)} all-to-all(f32[8,128,128]{2,1,0:T(8,128)S(1)} %bitcast.20), channel_id=1, replica_groups=mesh['rep'=8,'blk'=32] {'rep'}, dimensions={0} | all-to-all | bytes 1048576 | tf_op jit(solution)/shard_map/all_to_all | solution.py:317
  67.8 6.1 %all-to-all-start.1 = ((f32[8,128,128]{2,1,0:T(8,128)}), f32[8,128,128]{2,1,0:T(8,128)S(1)}, u32[]{:S(2)}, u32[]{:S(2)}) async-start(f32[8,128,128]{2,1,0:T(8,128)} %get-tuple-element.31), calls=%async_computation.1 | async-start | bytes 1048576 | tf_op jit(solution)/shard_map/all_to_all | solution.py:321
  73.9 2.7 %shard_map.93.tiles = bf16[32,128,256]{2,1,0:T(8,128)(2,1)S(1)} custom-call(s32[17,32]{1,0:T(8,128)S(1)} %concatenate.10.info, f32[4,32,128,128]{3,2,1,0:T(8,128)} %bitcast.24), custom_call_target="tpu_custom_call" | custom-call | flops 2147483648 | bytes 2097152 | tf_op jit(solution)/shard_map/pallas_call | solution.py:146
  76.6 4.6 %all-to-all-done.1 = f32[8,128,128]{2,1,0:T(8,128)S(1)} async-done(((f32[8,128,128]{2,1,0:T(8,128)}), f32[8,128,128]{2,1,0:T(8,128)S(1)}, u32[]{:S(2)}, u32[]{:S(2)}) %all-to-all-start.1) | async-done | bytes 524320 | tf_op jit(solution)/shard_map/all_to_all | solution.py:321
  83.2 3.1 %shard_map.95 = f32[1024,128]{1,0:T(8,128)S(1)} custom-call(s32[17,32]{1,0:T(8,128)S(1)} %concatenate.10.info, f32[1024,128]{1,0:T(8,128)S(1)} %bitcast.17, f32[4,32,128,128]{3,2,1,0:T(8,128)} %bitcast.25), custom_call_target="tpu_custom_call" | custom-call | flops 2147483648 | bytes 2097152 | tf_op jit(solution)/shard_map/pallas_call | solution.py:146
  87.6 3.0 %collective-permute-start.9 = (f32[1024,128]{1,0:T(8,128)S(1)}, f32[1024,128]{1,0:T(8,128)S(1)}, u32[]{:S(2)}, u32[]{:S(2)}) collective-permute-start(f32[1024,128]{1,0:T(8,128)S(1)} %shard_map.94), channel_id=1, source_target_pairs={{0,30},{2,0},{4,2},{6,4},{8,6},{10,8},{12,10},{14,12},{16,14},{18,... | collective-permute-start | bytes 1572872 | tf_op jit(solution)/shard_map/ppermute | solution.py:273
  92.9 3.1 %shard_map.91 = f32[1024,128]{1,0:T(8,128)S(1)} custom-call(s32[17,32]{1,0:T(8,128)S(1)} %concatenate.10.info, f32[1024,128]{1,0:T(8,128)S(1)} %bitcast.18, f32[4,32,128,128]{3,2,1,0:T(8,128)} %bitcast.26), custom_call_target="tpu_custom_call" | custom-call | flops 2147483648 | bytes 2097152 | tf_op jit(solution)/shard_map/pallas_call | solution.py:146
  95.9 7.4 %collective-permute-start.13 = (f32[1024,128]{1,0:T(8,128)S(1)}, f32[1024,128]{1,0:T(8,128)S(1)}, u32[]{:S(2)}, u32[]{:S(2)}) collective-permute-start(f32[1024,128]{1,0:T(8,128)S(1)} %shard_map.91), channel_id=1, source_target_pairs={{1,0},{0,1},{3,2},{2,3},{5,4},{4,5},{7,6},{6,7},{9,8},{8,9},{11,10... | collective-permute-start | bytes 1572872 | tf_op jit(solution)/shard_map/ppermute | solution.py:335
  103.4 3.1 %shard_map.92 = f32[1024,128]{1,0:T(8,128)S(1)} custom-call(s32[17,32]{1,0:T(8,128)S(1)} %concatenate.10.info, f32[1024,128]{1,0:T(8,128)S(1)} %bitcast.19, f32[4,32,128,128]{3,2,1,0:T(8,128)} %bitcast.27), custom_call_target="tpu_custom_call" | custom-call | flops 2147483648 | bytes 2097152 | tf_op jit(solution)/shard_map/pallas_call | solution.py:146
  107.7 2.6 %collective-permute-start.17 = (f32[256,128]{1,0:T(8,128)S(1)}, f32[256,128]{1,0:T(8,128)S(1)}, u32[]{:S(2)}, u32[]{:S(2)}) collective-permute-start(f32[256,128]{1,0:T(8,128)S(1)} %get-tuple-element.40), channel_id=1, source_target_pairs={{0,160},{32,128},{64,224},{96,192},{128,32},{160,0},{192,96},{224,... | collective-permute-start | bytes 393224 | tf_op jit(solution)/shard_map/ppermute | solution.py:341
  112.7 2.4 %collective-permute-done.15 = f32[256,128]{1,0:T(8,128)S(1)} collective-permute-done((f32[256,128]{1,0:T(8,128)S(1)}, f32[256,128]{1,0:T(8,128)S(1)}, u32[]{:S(2)}, u32[]{:S(2)}) %collective-permute-start.15) | collective-permute-done | bytes 131104 | tf_op jit(solution)/shard_map/ppermute | solution.py:341
  116.5 3.6 %collective-permute-start.18 = (f32[256,128]{1,0:T(8,128)S(1)}, f32[256,128]{1,0:T(8,128)S(1)}, u32[]{:S(2)}, u32[]{:S(2)}) collective-permute-start(f32[256,128]{1,0:T(8,128)S(1)} %collective-permute-done.17), channel_id=1, source_target_pairs={{0,22},{1,23},{2,24},{3,25},{4,26},{5,27},{6,28},{7,29},{8,30},{9,... | collective-permute-start | bytes 393224 | tf_op jit(solution)/shard_map/ppermute | solution.py:273
  120.1 6.0 %collective-permute-done.16 = f32[256,128]{1,0:T(8,128)S(1)} collective-permute-done((f32[256,128]{1,0:T(8,128)S(1)}, f32[256,128]{1,0:T(8,128)S(1)}, u32[]{:S(2)}, u32[]{:S(2)}) %collective-permute-start.16) | collective-permute-done | bytes 131104 | tf_op jit(solution)/shard_map/ppermute | solution.py:273
  127.8 2.5 %collective-permute-done.20 = f32[256,128]{1,0:T(8,128)S(1)} collective-permute-done((f32[256,128]{1,0:T(8,128)S(1)}, f32[256,128]{1,0:T(8,128)S(1)}, u32[]{:S(2)}, u32[]{:S(2)}) %collective-permute-start.20) | collective-permute-done | bytes 131104 | tf_op jit(solution)/shard_map/ppermute | solution.py:273
  130.4 5.7 %collective-permute-start.21 = (f32[128,128]{1,0:T(8,128)S(1)}, f32[128,128]{1,0:T(8,128)S(1)}, u32[]{:S(2)}, u32[]{:S(2)}) collective-permute-start(f32[128,128]{1,0:T(8,128)S(1)} %split.9), channel_id=1, source_target_pairs={{32,0},{0,32},{96,64},{64,96},{160,128},{128,160},{224,192},{192,2... | collective-permute-start | bytes 196616 | tf_op jit(solution)/shard_map/ppermute | solution.py:346
  (51 shorter events, 30.2 us)
Async XLA Ops:
  0.6 4.6 %collective-permute-start = (f32[128,128]{1,0:T(8,128)}, f32[128,128]{1,0:T(8,128)S(1)}, u32[]{:S(2)}, u32[]{:S(2)}) collective-permute-start(f32[128,128]{1,0:T(8,128)} %bitcast.28), channel_id=1, source_target_pairs={{32,0},{0,32},{96,64},{64,96},{160,128},{128,160},{224,192},{192,2... | collective-permute-start | bytes 196616 | tf_op jit(solution)/shard_map/ppermute | solution.py:294
  5.2 17.4 %collective-permute-start.1 = (f32[256,128]{1,0:T(8,128)S(1)}, f32[256,128]{1,0:T(8,128)S(1)}, u32[]{:S(2)}, u32[]{:S(2)}) collective-permute-start(f32[256,128]{1,0:T(8,128)S(1)} %constant_dynamic-update-slice_fusion), channel_id=1, source_target_pairs={{2,0},{3,1},{4,2},{5,3},{6,4},{7,5},{8,6},{9,7},{10,8},{11,9},{12,... | collective-permute-start | bytes 393224 | tf_op jit(solution)/shard_map/ppermute | solution.py:267
  9.8 12.8 %collective-permute-start.2 = (f32[256,128]{1,0:T(8,128)S(1)}, f32[256,128]{1,0:T(8,128)S(1)}, u32[]{:S(2)}, u32[]{:S(2)}) collective-permute-start(f32[256,128]{1,0:T(8,128)S(1)} %constant_dynamic-update-slice_fusion), channel_id=1, source_target_pairs={{66,0},{67,1},{68,2},{69,3},{70,4},{71,5},{72,6},{73,7},{74,8},{75... | collective-permute-start | bytes 393224 | tf_op jit(solution)/shard_map/ppermute | solution.py:267
  15.3 9.6 %collective-permute-start.3 = (f32[256,128]{1,0:T(8,128)S(1)}, f32[256,128]{1,0:T(8,128)S(1)}, u32[]{:S(2)}, u32[]{:S(2)}) collective-permute-start(f32[256,128]{1,0:T(8,128)S(1)} %constant_dynamic-update-slice_fusion), channel_id=1, source_target_pairs={{130,0},{131,1},{132,2},{133,3},{134,4},{135,5},{136,6},{137,7},{1... | collective-permute-start | bytes 393224 | tf_op jit(solution)/shard_map/ppermute | solution.py:267
  16.9 11.5 %collective-permute-start.4 = (f32[256,128]{1,0:T(8,128)S(1)}, f32[256,128]{1,0:T(8,128)S(1)}, u32[]{:S(2)}, u32[]{:S(2)}) collective-permute-start(f32[256,128]{1,0:T(8,128)S(1)} %constant_dynamic-update-slice_fusion), channel_id=1, source_target_pairs={{194,0},{195,1},{196,2},{197,3},{198,4},{199,5},{200,6},{201,7},{2... | collective-permute-start | bytes 393224 | tf_op jit(solution)/shard_map/ppermute | solution.py:267
  28.5 5.7 %collective-permute-start.6 = (f32[1024,128]{1,0:T(8,128)S(1)}, f32[1024,128]{1,0:T(8,128)S(1)}, u32[]{:S(2)}, u32[]{:S(2)}) collective-permute-start(f32[1024,128]{1,0:T(8,128)S(1)} %pad_maximum_fusion.refs_0_), channel_id=1, source_target_pairs={{1,0},{0,1},{3,2},{2,3},{5,4},{4,5},{7,6},{6,7},{9,8},{8,9},{11,10... | collective-permute-start | bytes 1572872 | tf_op jit(solution)/shard_map/ppermute | solution.py:307
  28.6 16.1 %collective-permute-start.5 = (f32[1024,128]{1,0:T(8,128)S(1)}, f32[1024,128]{1,0:T(8,128)S(1)}, u32[]{:S(2)}, u32[]{:S(2)}) collective-permute-start(f32[1024,128]{1,0:T(8,128)S(1)} %pad_maximum_fusion.refs_0_), channel_id=1, source_target_pairs={{30,0},{143,1},{0,2},{1,3},{2,4},{3,5},{4,6},{5,7},{6,8},{7,9},{8,... | collective-permute-start | bytes 1572872 | tf_op jit(solution)/shard_map/ppermute | solution.py:267
  30.2 17.9 %collective-permute-start.8 = (f32[1024,128]{1,0:T(8,128)S(1)}, f32[1024,128]{1,0:T(8,128)S(1)}, u32[]{:S(2)}, u32[]{:S(2)}) collective-permute-start(f32[1024,128]{1,0:T(8,128)S(1)} %pad_maximum_fusion.refs_0_), channel_id=1, source_target_pairs={{0,31},{2,1},{4,3},{6,5},{8,7},{10,9},{12,11},{14,13},{16,15},{18,... | collective-permute-start | bytes 1572872 | tf_op jit(solution)/shard_map/ppermute | solution.py:285
  44.7 3.8 %collective-permute-start.7 = (f32[1024,128]{1,0:T(8,128)S(1)}, f32[1024,128]{1,0:T(8,128)S(1)}, u32[]{:S(2)}, u32[]{:S(2)}) collective-permute-start(f32[1024,128]{1,0:T(8,128)S(1)} %collective-permute-done.5.refs_0_), channel_id=1, source_target_pairs={{1,0},{3,2},{5,4},{7,6},{9,8},{11,10},{13,12},{15,14},{17,16},{19,... | collective-permute-start | bytes 1572872 | tf_op jit(solution)/shard_map/ppermute | solution.py:285
  48.1 18.5 %copy-start = (f32[128,256]{1,0:T(8,128)S(1)}, f32[128,256]{1,0:T(8,128)}, u32[]{:S(2)}) copy-start(f32[128,256]{1,0:T(8,128)} %weight.1) | copy-start | bytes 393220
  67.8 13.4 %all-to-all-start.1 = ((f32[8,128,128]{2,1,0:T(8,128)}), f32[8,128,128]{2,1,0:T(8,128)S(1)}, u32[]{:S(2)}, u32[]{:S(2)}) async-start(f32[8,128,128]{2,1,0:T(8,128)} %get-tuple-element.31), calls=%async_computation.1 | async-start | bytes 1048576 | tf_op jit(solution)/shard_map/all_to_all | solution.py:321
  86.2 4.4 %collective-permute-start.10 = (f32[1024,128]{1,0:T(8,128)S(1)}, f32[1024,128]{1,0:T(8,128)S(1)}, u32[]{:S(2)}, u32[]{:S(2)}) collective-permute-start(f32[1024,128]{1,0:T(8,128)S(1)} %shard_map.95), channel_id=1, source_target_pairs={{0,1},{2,3},{4,5},{6,7},{8,9},{10,11},{12,13},{14,15},{16,17},{18,... | collective-permute-start | bytes 1572872 | tf_op jit(solution)/shard_map/ppermute | solution.py:285
  87.6 18.9 %collective-permute-start.9 = (f32[1024,128]{1,0:T(8,128)S(1)}, f32[1024,128]{1,0:T(8,128)S(1)}, u32[]{:S(2)}, u32[]{:S(2)}) collective-permute-start(f32[1024,128]{1,0:T(8,128)S(1)} %shard_map.94), channel_id=1, source_target_pairs={{0,30},{2,0},{4,2},{6,4},{8,6},{10,8},{12,10},{14,12},{16,14},{18,... | collective-permute-start | bytes 1572872 | tf_op jit(solution)/shard_map/ppermute | solution.py:273
  90.7 15.8 %collective-permute-start.11 = (f32[1024,128]{1,0:T(8,128)S(1)}, f32[1024,128]{1,0:T(8,128)S(1)}, u32[]{:S(2)}, u32[]{:S(2)}) collective-permute-start(f32[1024,128]{1,0:T(8,128)S(1)} %shard_map.95), channel_id=1, source_target_pairs={{1,2},{3,4},{5,6},{7,8},{9,10},{11,12},{13,14},{15,16},{17,18},{19... | collective-permute-start | bytes 1572872 | tf_op jit(solution)/shard_map/ppermute | solution.py:285
  92.0 14.5 %collective-permute-start.12 = (f32[1024,128]{1,0:T(8,128)S(1)}, f32[1024,128]{1,0:T(8,128)S(1)}, u32[]{:S(2)}, u32[]{:S(2)}) collective-permute-start(f32[1024,128]{1,0:T(8,128)S(1)} %add.41), channel_id=1, source_target_pairs={{1,143},{3,1},{5,3},{7,5},{9,7},{11,9},{13,11},{15,13},{17,159},{1... | collective-permute-start | bytes 1572872 | tf_op jit(solution)/shard_map/ppermute | solution.py:273
  95.9 10.7 %collective-permute-start.13 = (f32[1024,128]{1,0:T(8,128)S(1)}, f32[1024,128]{1,0:T(8,128)S(1)}, u32[]{:S(2)}, u32[]{:S(2)}) collective-permute-start(f32[1024,128]{1,0:T(8,128)S(1)} %shard_map.91), channel_id=1, source_target_pairs={{1,0},{0,1},{3,2},{2,3},{5,4},{4,5},{7,6},{6,7},{9,8},{8,9},{11,10... | collective-permute-start | bytes 1572872 | tf_op jit(solution)/shard_map/ppermute | solution.py:335
  106.8 8.3 %collective-permute-start.15 = (f32[256,128]{1,0:T(8,128)S(1)}, f32[256,128]{1,0:T(8,128)S(1)}, u32[]{:S(2)}, u32[]{:S(2)}) collective-permute-start(f32[256,128]{1,0:T(8,128)S(1)} %get-tuple-element.38), channel_id=1, source_target_pairs={{0,64},{32,96},{64,0},{96,32},{128,192},{160,224},{192,128},{224,1... | collective-permute-start | bytes 393224 | tf_op jit(solution)/shard_map/ppermute | solution.py:341
  107.7 8.8 %collective-permute-start.17 = (f32[256,128]{1,0:T(8,128)S(1)}, f32[256,128]{1,0:T(8,128)S(1)}, u32[]{:S(2)}, u32[]{:S(2)}) collective-permute-start(f32[256,128]{1,0:T(8,128)S(1)} %get-tuple-element.40), channel_id=1, source_target_pairs={{0,160},{32,128},{64,224},{96,192},{128,32},{160,0},{192,96},{224,... | collective-permute-start | bytes 393224 | tf_op jit(solution)/shard_map/ppermute | solution.py:341
  110.3 9.8 %collective-permute-start.19 = (f32[256,128]{1,0:T(8,128)S(1)}, f32[256,128]{1,0:T(8,128)S(1)}, u32[]{:S(2)}, u32[]{:S(2)}) collective-permute-start(f32[256,128]{1,0:T(8,128)S(1)} %get-tuple-element.39), channel_id=1, source_target_pairs={{0,224},{32,192},{64,160},{96,128},{128,96},{160,64},{192,32},{224... | collective-permute-start | bytes 393224 | tf_op jit(solution)/shard_map/ppermute | solution.py:341
  112.5 7.7 %collective-permute-start.14 = (f32[256,128]{1,0:T(8,128)S(1)}, f32[256,128]{1,0:T(8,128)S(1)}, u32[]{:S(2)}, u32[]{:S(2)}) collective-permute-start(f32[256,128]{1,0:T(8,128)S(1)} %get-tuple-element.41), channel_id=1, source_target_pairs={{0,2},{1,3},{2,4},{3,5},{4,6},{5,7},{6,8},{7,9},{8,10},{9,11},{10,... | collective-permute-start | bytes 393224 | tf_op jit(solution)/shard_map/ppermute | solution.py:273
  115.1 11.0 %collective-permute-start.16 = (f32[256,128]{1,0:T(8,128)S(1)}, f32[256,128]{1,0:T(8,128)S(1)}, u32[]{:S(2)}, u32[]{:S(2)}) collective-permute-start(f32[256,128]{1,0:T(8,128)S(1)} %collective-permute-done.15), channel_id=1, source_target_pairs={{0,10},{1,11},{2,12},{3,13},{4,14},{5,15},{6,16},{7,17},{8,18},{9,... | collective-permute-start | bytes 393224 | tf_op jit(solution)/shard_map/ppermute | solution.py:273
  116.5 11.3 %collective-permute-start.18 = (f32[256,128]{1,0:T(8,128)S(1)}, f32[256,128]{1,0:T(8,128)S(1)}, u32[]{:S(2)}, u32[]{:S(2)}) collective-permute-start(f32[256,128]{1,0:T(8,128)S(1)} %collective-permute-done.17), channel_id=1, source_target_pairs={{0,22},{1,23},{2,24},{3,25},{4,26},{5,27},{6,28},{7,29},{8,30},{9,... | collective-permute-start | bytes 393224 | tf_op jit(solution)/shard_map/ppermute | solution.py:273
  120.1 10.2 %collective-permute-start.20 = (f32[256,128]{1,0:T(8,128)S(1)}, f32[256,128]{1,0:T(8,128)S(1)}, u32[]{:S(2)}, u32[]{:S(2)}) collective-permute-start(f32[256,128]{1,0:T(8,128)S(1)} %collective-permute-done.19), channel_id=1, source_target_pairs={{0,30},{1,31},{2,0},{3,1},{4,2},{5,3},{6,4},{7,5},{8,6},{9,7},{10,... | collective-permute-start | bytes 393224 | tf_op jit(solution)/shard_map/ppermute | solution.py:273
  130.4 8.0 %collective-permute-start.21 = (f32[128,128]{1,0:T(8,128)S(1)}, f32[128,128]{1,0:T(8,128)S(1)}, u32[]{:S(2)}, u32[]{:S(2)}) collective-permute-start(f32[128,128]{1,0:T(8,128)S(1)} %split.9), channel_id=1, source_target_pairs={{32,0},{0,32},{96,64},{64,96},{160,128},{128,160},{224,192},{192,2... | collective-permute-start | bytes 196616 | tf_op jit(solution)/shard_map/ppermute | solution.py:346
  (1 other events, 18.5 us)

commit v8 on v6

--- a/solution.py
+++ b/solution.py
@@ -70,7 +70,10 @@
     def left_of(part, chunk):
         for slot in range(CHUNK):
             number = chunk * CHUNK + slot
-            yield tiles[number], number
+            tile = tiles[number]
+            if tile.dtype == F32:
+                tile = jnp.concatenate(halves(tile.T), axis=1)
+            yield tile, number
 
     return left_of, tiles.shape[0] // CHUNK
 
@@ -115,12 +118,17 @@
     out[...] = value + refs[n_in + 1][...] if has_start else value
 
 
-def backward_body(parts, first, info, panel, tiles, *refs):
+def backward_body(parts, first, ahead, info, panel, tiles, *refs):
+    if ahead is not None:
+        raw, refs = refs[0], refs[1:]
+        following, sem = refs[parts], refs[-1]
+        fetch = pltpu.make_async_copy(raw.at[info[0, ahead]], following, sem)
+        fetch.start()
     outs = refs[:parts]
-    split, total = refs[parts : parts + 2]
+    split, total = refs[parts + int(ahead is not None) :][:2]
     nodes = panel.shape[0]
     sections = info.shape[0] // 4
-    if tiles.dtype == F32:
+    if len(tiles.shape) == 4:
         left_of, chunks = fetched(parts, first, info, tiles, *refs[-2:], True)
     else:
         left_of, chunks = prepared(tiles)
@@ -133,11 +141,13 @@
             1 + 3 * sections, split, total,
         )
         outs[part][...] = folded(total, nodes)
+    if ahead is not None:
+        fetch.wait()
 
 
 def local_call(body, parts, slots, info, panels, tiles, extra, outs, scratch):
     whole = pl.BlockSpec(memory_space=pltpu.VMEM)
-    raw = tiles.dtype == F32
+    raw = len(tiles.shape) == 4
     if raw:
         scratch = scratch + [
             pltpu.VMEM((parts, slots, SIDE, SIDE), F32),
@@ -148,7 +158,7 @@
         in_specs=[pl.BlockSpec(memory_space=pltpu.SMEM)]
         + [whole] * len(panels)
         + [pl.BlockSpec(memory_space=pltpu.HBM) if raw else whole]
-        + [whole] * len(extra),
+        + [pl.BlockSpec(memory_space=pltpu.HBM) if len(e.shape) == 4 else whole for e in extra],
         out_specs=[whole] * len(outs),
         scratch_shapes=scratch,
         out_shape=outs,
@@ -161,16 +171,18 @@
     )(info, *panels, tiles, *extra)
 
 
-def tile_call(body, parts, info, panels, tiles, extra, n_out):
+def tile_call(body, parts, info, panels, tiles, extra, n_out, ahead=None):
     nodes, features = panels[0].shape
-    return local_call(
-        body, parts, tiles.shape[-3], info, panels, tiles, extra,
-        [jax.ShapeDtypeStruct((nodes, features), F32)] * n_out,
-        [
-            pltpu.VMEM((nodes // SIDE, 2 * SIDE, 2 * SIDE), BF16),
-            pltpu.VMEM((nodes + SIDE, 2 * features), F32),
-        ],
-    )
+    slots = tiles.shape[-3]
+    outs = [jax.ShapeDtypeStruct((nodes, features), F32)] * n_out
+    scratch = [
+        pltpu.VMEM((nodes // SIDE, 2 * SIDE, 2 * SIDE), BF16),
+        pltpu.VMEM((nodes + SIDE, 2 * features), F32),
+    ]
+    if ahead is not None:
+        outs = outs + [jax.ShapeDtypeStruct((slots, SIDE, SIDE), F32)]
+        scratch = scratch + [pltpu.SemaphoreType.DMA]
+    return local_call(body, parts, slots, info, panels, tiles, extra, outs, scratch)
 
 
 def prepare(parts, first, transposed, info, tiles):
@@ -186,9 +198,10 @@
     return tile_call(body, len(panels) - int(choose), info, panels, tiles, extra, 1)[0]
 
 
-def backward_tiles(first, info, panel, tiles, parts):
-    body = functools.partial(backward_body, parts, first)
-    return tile_call(body, parts, info, [panel], tiles, [], parts)
+def backward_tiles(first, info, panel, tiles, parts, ahead=None, raw=None):
+    body = functools.partial(backward_body, parts, first, ahead)
+    extra = [] if ahead is None else [raw]
+    return tile_call(body, parts, info, [panel], tiles, extra, parts, ahead)
 
 
 def widened(value):
@@ -319,9 +332,11 @@
     )
     hidden, spread = dense(partials, weight, cotangent[0])
     grad_panel = lax.all_to_all(spread, "rep", 0, 0, tiled=True).reshape(base.shape)
-    (outer,) = backward_tiles(OUTER, info, grad_panel, outer_tiles, 1)
+    outer, lowest_tiles = backward_tiles(
+        OUTER, info, grad_panel, outer_tiles, 1, LOWEST, tiles
+    )
     outer_in = along(outer, 1, evens)
-    (lowest,) = backward_tiles(LOWEST, info, grad_panel, tiles, 1)
+    (lowest,) = backward_tiles(LOWEST, info, grad_panel, lowest_tiles, 1)
     combined = lowest + outer_in
     from_upper = back(combined, below)
     outer, combined = lax.optimization_barrier((outer, combined))

time: 138 us -> 138 us (level)
  starting transfers between devices: 51.1 us -> 48.9 us
  waiting for transfers between devices: 38 us -> 39.7 us
  blocking collectives: 16 us -> 17.6 us
    ppermute x3, waiting for transfers between devices: 7.13 us -> 0.01 us  [shards(): part = lax.ppermute(part, 'rep', [(r, r ^ across) for r in range(replicas)])]
    ppermute x5, waiting for transfers between devices: 9.94 us -> 15.9 us  [back(): lax.ppermute(block, ('rep', 'blk'), [(device(g, r), device(*target(g, r))...]
    ppermute x1, starting transfers between devices: 3.32 us -> 0.09 us  [shards(): feature_grad = kept + lax.ppermute(sent, 'rep', twin)]
    ppermute x5, starting transfers between devices: 5.37 us -> 8.12 us  [back(): lax.ppermute(block, ('rep', 'blk'), [(device(g, r), device(*target(g, r))...]
    ppermute x1, waiting for transfers between devices: 2.25 us -> 4.25 us  [shards(): feature_grad = kept + lax.ppermute(sent, 'rep', twin)]
    all_to_all x1, blocking collectives: 16 us -> 17.6 us  [shards(): lax.all_to_all(partial_sum.reshape(replicas, -1, own.shape[-1]), 'rep', 0...]
  transfers between devices with their start and end apart: 22 -> 22, of which waited for: 14 -> 12; matrix products, arithmetic and copies ran while one was open for 2% -> 2% of each run, Pallas kernels for 16% -> 15%
where the time goes in v8:
time: 138 us; the launch traced here: 136 us
  starting transfers between devices  48.9 us (35%)
  waiting for transfers between devices  39.7 us (29%)
  Pallas kernels  25.8 us (19%)
  blocking collectives  17.6 us (13%)
  other arithmetic  2.66 us (2%)
    pallas_call x9, Pallas kernels, local_call(): pl.pallas_call(body, in_specs=[pl.BlockSpec(memory_space=pltpu.SMEM)] + [...  24.5 us
    all_to_all x1, blocking collectives, shards(): lax.all_to_all(partial_sum.reshape(replicas, -1, own.shape[-1]), 'rep', 0...  17.6 us
    ppermute x5, waiting for transfers between devices, back(): lax.ppermute(block, ('rep', 'blk'), [(device(g, r), device(*target(g, r))...  15.9 us
    ppermute x5, starting transfers between devices, joint(): lax.ppermute(block, ('rep', 'blk'), [(device(*source(g, r)), device(g, r)...  15.3 us
    ppermute x5, waiting for transfers between devices, joint(): lax.ppermute(block, ('rep', 'blk'), [(device(*source(g, r)), device(g, r)...  12.5 us
    ppermute x4, starting transfers between devices, along(): lax.ppermute(block, 'blk', [(g, (g + distance) % groups) for g in ids])  8.61 us
    ppermute x5, starting transfers between devices, back(): lax.ppermute(block, ('rep', 'blk'), [(device(g, r), device(*target(g, r))...  8.12 us
    all_to_all x1, starting transfers between devices, shards(): lax.all_to_all(spread, 'rep', 0, 0, tiled=True).reshape(base.shape)  6.11 us
  transfers between devices with their start and end apart: 22, of which 12 were waited for; matrix products, arithmetic and copies ran while one was open for 2% of the time, Pallas kernels for 15%

profile of v8, /device:TPU:26, one launch (start us, length us, event | category | flops | bytes accessed | tf_op | source)
XLA Modules:
  0.0 136.4 jit_solution(18354057029468694816)
XLA Ops:
  5.2 8.0 %collective-permute-start.4 = (f32[256,128]{1,0:T(8,128)S(1)}, f32[256,128]{1,0:T(8,128)S(1)}, u32[]{:S(2)}, u32[]{:S(2)}) collective-permute-start(f32[256,128]{1,0:T(8,128)S(1)} %constant_dynamic-update-slice_fusion), channel_id=1, source_target_pairs={{194,0},{195,1},{196,2},{197,3},{198,4},{199,5},{200,6},{201,7},{2... | collective-permute-start | bytes 393224 | tf_op jit(solution)/shard_map/ppermute | solution.py:280
  13.2 3.2 %collective-permute-start.2 = (f32[256,128]{1,0:T(8,128)S(1)}, f32[256,128]{1,0:T(8,128)S(1)}, u32[]{:S(2)}, u32[]{:S(2)}) collective-permute-start(f32[256,128]{1,0:T(8,128)S(1)} %constant_dynamic-update-slice_fusion), channel_id=1, source_target_pairs={{66,0},{67,1},{68,2},{69,3},{70,4},{71,5},{72,6},{73,7},{74,8},{75... | collective-permute-start | bytes 393224 | tf_op jit(solution)/shard_map/ppermute | solution.py:280
  16.4 4.0 %collective-permute-start.1 = (f32[256,128]{1,0:T(8,128)S(1)}, f32[256,128]{1,0:T(8,128)S(1)}, u32[]{:S(2)}, u32[]{:S(2)}) collective-permute-start(f32[256,128]{1,0:T(8,128)S(1)} %constant_dynamic-update-slice_fusion), channel_id=1, source_target_pairs={{2,0},{3,1},{4,2},{5,3},{6,4},{7,5},{8,6},{9,7},{10,8},{11,9},{12,... | collective-permute-start | bytes 393224 | tf_op jit(solution)/shard_map/ppermute | solution.py:280
  20.4 3.1 %shard_map.86 = (bf16[32,128,256]{2,1,0:T(8,128)(2,1)S(1)}, bf16[32,128,256]{2,1,0:T(8,128)(2,1)S(1)}) custom-call(s32[17,32]{1,0:T(8,128)S(1)} %concatenate.10.info, f32[4,32,128,128]{3,2,1,0:T(8,128)} %bitcast.22), custom_call_target="tpu_custom_call" | custom-call | flops 4294967296 | bytes 4194304 | tf_op jit(solution)/shard_map/pallas_call | solution.py:156
  25.3 4.2 %collective-permute-done.1 = f32[256,128]{1,0:T(8,128)S(1)} collective-permute-done((f32[256,128]{1,0:T(8,128)S(1)}, f32[256,128]{1,0:T(8,128)S(1)}, u32[]{:S(2)}, u32[]{:S(2)}) %collective-permute-start.1) | collective-permute-done | bytes 131104 | tf_op jit(solution)/shard_map/ppermute | solution.py:280
  29.8 4.7 %collective-permute-start.8 = (f32[1024,128]{1,0:T(8,128)S(1)}, f32[1024,128]{1,0:T(8,128)S(1)}, u32[]{:S(2)}, u32[]{:S(2)}) collective-permute-start(f32[1024,128]{1,0:T(8,128)S(1)} %pad_maximum_fusion.refs_0_), channel_id=1, source_target_pairs={{0,31},{2,1},{4,3},{6,5},{8,7},{10,9},{12,11},{14,13},{16,15},{18,... | collective-permute-start | bytes 1572872 | tf_op jit(solution)/shard_map/ppermute | solution.py:298
  34.5 4.1 %shard_map.87.refs_2_ = f32[1024,128]{1,0:T(8,128)S(1)} custom-call(s32[17,32]{1,0:T(8,128)S(1)} %concatenate.10.info, f32[1024,128]{1,0:T(8,128)S(1)} %pad_maximum_fusion.refs_0_, f32[1024,128]{1,0:T(8,128)S(1)} %collective-permute-done.6.refs_1_, f32[4,32,128,128]{3,2,1,0:T(8,128)} %bitcast.23), custom_call_target="tpu_custom_call" | custom-call | flops 4294967296 | bytes 4194304 | tf_op jit(solution)/shard_map/pallas_call | solution.py:156
  38.6 6.4 %collective-permute-done.5.refs_0_ = f32[1024,128]{1,0:T(8,128)S(1)} collective-permute-done((f32[1024,128]{1,0:T(8,128)S(1)}, f32[1024,128]{1,0:T(8,128)S(1)}, u32[]{:S(2)}, u32[]{:S(2)}) %collective-permute-start.5) | collective-permute-done | bytes 524320 | tf_op jit(solution)/shard_map/ppermute | solution.py:280
  50.9 17.6 %all_to_all.10.partials = f32[8,128,128]{2,1,0:T(8,128)S(1)} all-to-all(f32[8,128,128]{2,1,0:T(8,128)S(1)} %bitcast.20), channel_id=1, replica_groups=mesh['rep'=8,'blk'=32] {'rep'}, dimensions={0} | all-to-all | bytes 1048576 | tf_op jit(solution)/shard_map/all_to_all | solution.py:330
  69.8 6.1 %all-to-all-start.1 = ((f32[8,128,128]{2,1,0:T(8,128)}), f32[8,128,128]{2,1,0:T(8,128)S(1)}, u32[]{:S(2)}, u32[]{:S(2)}) async-start(f32[8,128,128]{2,1,0:T(8,128)} %get-tuple-element.31), calls=%async_computation.1 | async-start | bytes 1048576 | tf_op jit(solution)/shard_map/all_to_all | solution.py:334
  75.9 2.7 %shard_map.93.tiles = bf16[32,128,256]{2,1,0:T(8,128)(2,1)S(1)} custom-call(s32[17,32]{1,0:T(8,128)S(1)} %concatenate.10.info, f32[4,32,128,128]{3,2,1,0:T(8,128)} %bitcast.24), custom_call_target="tpu_custom_call" | custom-call | flops 2147483648 | bytes 2097152 | tf_op jit(solution)/shard_map/pallas_call | solution.py:156
  78.5 4.6 %all-to-all-done.1 = f32[8,128,128]{2,1,0:T(8,128)S(1)} async-done(((f32[8,128,128]{2,1,0:T(8,128)}), f32[8,128,128]{2,1,0:T(8,128)S(1)}, u32[]{:S(2)}, u32[]{:S(2)}) %all-to-all-start.1) | async-done | bytes 524320 | tf_op jit(solution)/shard_map/all_to_all | solution.py:334
  83.1 2.3 %shard_map.94 = (f32[1024,128]{1,0:T(8,128)S(1)}, f32[32,128,128]{2,1,0:T(8,128)S(1)}) custom-call(s32[17,32]{1,0:T(8,128)S(1)} %concatenate.10.info, f32[1024,128]{1,0:T(8,128)S(1)} %bitcast.16, bf16[32,128,256]{2,1,0:T(8,128)(2,1)S(1)} %shard_map.93.tiles, f32[4,32,128,128]{3,2,1,0:T(8,128)} %bitcast.25), custom_call_target="tpu_custom_call" | custom-call | flops 2147483648 | bytes 2097152 | tf_op jit(solution)/shard_map/pallas_call | solution.py:156
  91.3 3.1 %shard_map.91 = f32[1024,128]{1,0:T(8,128)S(1)} custom-call(s32[17,32]{1,0:T(8,128)S(1)} %concatenate.10.info, f32[1024,128]{1,0:T(8,128)S(1)} %bitcast.18, f32[4,32,128,128]{3,2,1,0:T(8,128)} %bitcast.26), custom_call_target="tpu_custom_call" | custom-call | flops 2147483648 | bytes 2097152 | tf_op jit(solution)/shard_map/pallas_call | solution.py:156
  94.4 4.9 %collective-permute-start.12 = (f32[1024,128]{1,0:T(8,128)S(1)}, f32[1024,128]{1,0:T(8,128)S(1)}, u32[]{:S(2)}, u32[]{:S(2)}) collective-permute-start(f32[1024,128]{1,0:T(8,128)S(1)} %shard_map.91), channel_id=1, source_target_pairs={{1,0},{0,1},{3,2},{2,3},{5,4},{4,5},{7,6},{6,7},{9,8},{8,9},{11,10... | collective-permute-start | bytes 1572872 | tf_op jit(solution)/shard_map/ppermute | solution.py:349
  99.3 3.1 %shard_map.92 = f32[1024,128]{1,0:T(8,128)S(1)} custom-call(s32[17,32]{1,0:T(8,128)S(1)} %concatenate.10.info, f32[1024,128]{1,0:T(8,128)S(1)} %bitcast.19, f32[4,32,128,128]{3,2,1,0:T(8,128)} %bitcast.27), custom_call_target="tpu_custom_call" | custom-call | flops 2147483648 | bytes 2097152 | tf_op jit(solution)/shard_map/pallas_call | solution.py:156
  105.6 2.8 %collective-permute-start.18 = (f32[256,128]{1,0:T(8,128)S(1)}, f32[256,128]{1,0:T(8,128)S(1)}, u32[]{:S(2)}, u32[]{:S(2)}) collective-permute-start(f32[256,128]{1,0:T(8,128)S(1)} %get-tuple-element.39), channel_id=1, source_target_pairs={{0,224},{32,192},{64,160},{96,128},{128,96},{160,64},{192,32},{224... | collective-permute-start | bytes 393224 | tf_op jit(solution)/shard_map/ppermute | solution.py:355
  108.3 2.2 %collective-permute-start.16 = (f32[256,128]{1,0:T(8,128)S(1)}, f32[256,128]{1,0:T(8,128)S(1)}, u32[]{:S(2)}, u32[]{:S(2)}) collective-permute-start(f32[256,128]{1,0:T(8,128)S(1)} %get-tuple-element.40), channel_id=1, source_target_pairs={{0,160},{32,128},{64,224},{96,192},{128,32},{160,0},{192,96},{224,... | collective-permute-start | bytes 393224 | tf_op jit(solution)/shard_map/ppermute | solution.py:355
  111.3 3.3 %collective-permute-start.15 = (f32[256,128]{1,0:T(8,128)S(1)}, f32[256,128]{1,0:T(8,128)S(1)}, u32[]{:S(2)}, u32[]{:S(2)}) collective-permute-start(f32[256,128]{1,0:T(8,128)S(1)} %collective-permute-done.14), channel_id=1, source_target_pairs={{0,10},{1,11},{2,12},{3,13},{4,14},{5,15},{6,16},{7,17},{8,18},{9,... | collective-permute-start | bytes 393224 | tf_op jit(solution)/shard_map/ppermute | solution.py:286
  114.6 2.2 %collective-permute-start.19 = (f32[256,128]{1,0:T(8,128)S(1)}, f32[256,128]{1,0:T(8,128)S(1)}, u32[]{:S(2)}, u32[]{:S(2)}) collective-permute-start(f32[256,128]{1,0:T(8,128)S(1)} %collective-permute-done.18), channel_id=1, source_target_pairs={{0,30},{1,31},{2,0},{3,1},{4,2},{5,3},{6,4},{7,5},{8,6},{9,7},{10,... | collective-permute-start | bytes 393224 | tf_op jit(solution)/shard_map/ppermute | solution.py:286
  117.6 6.8 %collective-permute-done.15 = f32[256,128]{1,0:T(8,128)S(1)} collective-permute-done((f32[256,128]{1,0:T(8,128)S(1)}, f32[256,128]{1,0:T(8,128)S(1)}, u32[]{:S(2)}, u32[]{:S(2)}) %collective-permute-start.15) | collective-permute-done | bytes 131104 | tf_op jit(solution)/shard_map/ppermute | solution.py:286
  124.4 3.7 %collective-permute-done.19 = f32[256,128]{1,0:T(8,128)S(1)} collective-permute-done((f32[256,128]{1,0:T(8,128)S(1)}, f32[256,128]{1,0:T(8,128)S(1)}, u32[]{:S(2)}, u32[]{:S(2)}) %collective-permute-start.19) | collective-permute-done | bytes 131104 | tf_op jit(solution)/shard_map/ppermute | solution.py:286
  128.1 3.3 %collective-permute-done.17 = f32[256,128]{1,0:T(8,128)S(1)} collective-permute-done((f32[256,128]{1,0:T(8,128)S(1)}, f32[256,128]{1,0:T(8,128)S(1)}, u32[]{:S(2)}, u32[]{:S(2)}) %collective-permute-start.17) | collective-permute-done | bytes 131104 | tf_op jit(solution)/shard_map/ppermute | solution.py:286
  131.5 4.3 %collective-permute-done.20 = f32[128,128]{1,0:T(8,128)S(1)} collective-permute-done((f32[128,128]{1,0:T(8,128)S(1)}, f32[128,128]{1,0:T(8,128)S(1)}, u32[]{:S(2)}, u32[]{:S(2)}) %collective-permute-start.20) | collective-permute-done | bytes 65568 | tf_op jit(solution)/shard_map/ppermute | solution.py:360
  (49 shorter events, 25.0 us)
Async XLA Ops:
  0.6 4.6 %collective-permute-start = (f32[128,128]{1,0:T(8,128)}, f32[128,128]{1,0:T(8,128)S(1)}, u32[]{:S(2)}, u32[]{:S(2)}) collective-permute-start(f32[128,128]{1,0:T(8,128)} %bitcast.28), channel_id=1, source_target_pairs={{32,0},{0,32},{96,64},{64,96},{160,128},{128,160},{224,192},{192,2... | collective-permute-start | bytes 196616 | tf_op jit(solution)/shard_map/ppermute | solution.py:307
  5.2 18.3 %collective-permute-start.4 = (f32[256,128]{1,0:T(8,128)S(1)}, f32[256,128]{1,0:T(8,128)S(1)}, u32[]{:S(2)}, u32[]{:S(2)}) collective-permute-start(f32[256,128]{1,0:T(8,128)S(1)} %constant_dynamic-update-slice_fusion), channel_id=1, source_target_pairs={{194,0},{195,1},{196,2},{197,3},{198,4},{199,5},{200,6},{201,7},{2... | collective-permute-start | bytes 393224 | tf_op jit(solution)/shard_map/ppermute | solution.py:280
  13.2 12.2 %collective-permute-start.3 = (f32[256,128]{1,0:T(8,128)S(1)}, f32[256,128]{1,0:T(8,128)S(1)}, u32[]{:S(2)}, u32[]{:S(2)}) collective-permute-start(f32[256,128]{1,0:T(8,128)S(1)} %constant_dynamic-update-slice_fusion), channel_id=1, source_target_pairs={{130,0},{131,1},{132,2},{133,3},{134,4},{135,5},{136,6},{137,7},{1... | collective-permute-start | bytes 393224 | tf_op jit(solution)/shard_map/ppermute | solution.py:280
  13.2 12.2 %collective-permute-start.2 = (f32[256,128]{1,0:T(8,128)S(1)}, f32[256,128]{1,0:T(8,128)S(1)}, u32[]{:S(2)}, u32[]{:S(2)}) collective-permute-start(f32[256,128]{1,0:T(8,128)S(1)} %constant_dynamic-update-slice_fusion), channel_id=1, source_target_pairs={{66,0},{67,1},{68,2},{69,3},{70,4},{71,5},{72,6},{73,7},{74,8},{75... | collective-permute-start | bytes 393224 | tf_op jit(solution)/shard_map/ppermute | solution.py:280
  16.4 13.2 %collective-permute-start.1 = (f32[256,128]{1,0:T(8,128)S(1)}, f32[256,128]{1,0:T(8,128)S(1)}, u32[]{:S(2)}, u32[]{:S(2)}) collective-permute-start(f32[256,128]{1,0:T(8,128)S(1)} %constant_dynamic-update-slice_fusion), channel_id=1, source_target_pairs={{2,0},{3,1},{4,2},{5,3},{6,4},{7,5},{8,6},{9,7},{10,8},{11,9},{12,... | collective-permute-start | bytes 393224 | tf_op jit(solution)/shard_map/ppermute | solution.py:280
  29.6 4.9 %collective-permute-start.6 = (f32[1024,128]{1,0:T(8,128)S(1)}, f32[1024,128]{1,0:T(8,128)S(1)}, u32[]{:S(2)}, u32[]{:S(2)}) collective-permute-start(f32[1024,128]{1,0:T(8,128)S(1)} %pad_maximum_fusion.refs_0_), channel_id=1, source_target_pairs={{1,0},{0,1},{3,2},{2,3},{5,4},{4,5},{7,6},{6,7},{9,8},{8,9},{11,10... | collective-permute-start | bytes 1572872 | tf_op jit(solution)/shard_map/ppermute | solution.py:320
  29.7 15.4 %collective-permute-start.5 = (f32[1024,128]{1,0:T(8,128)S(1)}, f32[1024,128]{1,0:T(8,128)S(1)}, u32[]{:S(2)}, u32[]{:S(2)}) collective-permute-start(f32[1024,128]{1,0:T(8,128)S(1)} %pad_maximum_fusion.refs_0_), channel_id=1, source_target_pairs={{30,0},{143,1},{0,2},{1,3},{2,4},{3,5},{4,6},{5,7},{6,8},{7,9},{8,... | collective-permute-start | bytes 1572872 | tf_op jit(solution)/shard_map/ppermute | solution.py:280
  29.8 18.7 %collective-permute-start.8 = (f32[1024,128]{1,0:T(8,128)S(1)}, f32[1024,128]{1,0:T(8,128)S(1)}, u32[]{:S(2)}, u32[]{:S(2)}) collective-permute-start(f32[1024,128]{1,0:T(8,128)S(1)} %pad_maximum_fusion.refs_0_), channel_id=1, source_target_pairs={{0,31},{2,1},{4,3},{6,5},{8,7},{10,9},{12,11},{14,13},{16,15},{18,... | collective-permute-start | bytes 1572872 | tf_op jit(solution)/shard_map/ppermute | solution.py:298
  45.0 3.8 %collective-permute-start.7 = (f32[1024,128]{1,0:T(8,128)S(1)}, f32[1024,128]{1,0:T(8,128)S(1)}, u32[]{:S(2)}, u32[]{:S(2)}) collective-permute-start(f32[1024,128]{1,0:T(8,128)S(1)} %collective-permute-done.5.refs_0_), channel_id=1, source_target_pairs={{1,0},{3,2},{5,4},{7,6},{9,8},{11,10},{13,12},{15,14},{17,16},{19,... | collective-permute-start | bytes 1572872 | tf_op jit(solution)/shard_map/ppermute | solution.py:298
  48.4 20.1 %copy-start = (f32[128,256]{1,0:T(8,128)S(1)}, f32[128,256]{1,0:T(8,128)}, u32[]{:S(2)}) copy-start(f32[128,256]{1,0:T(8,128)} %weight.1) | copy-start | bytes 393220
  48.4 20.1 %copy-start.1 = (f32[1,128,256]{2,1,0:T(8,128)S(1)}, f32[1,128,256]{2,1,0:T(8,128)}, u32[]{:S(2)}) copy-start(f32[1,128,256]{2,1,0:T(8,128)} %param.9) | copy-start | bytes 393220
  69.8 13.4 %all-to-all-start.1 = ((f32[8,128,128]{2,1,0:T(8,128)}), f32[8,128,128]{2,1,0:T(8,128)S(1)}, u32[]{:S(2)}, u32[]{:S(2)}) async-start(f32[8,128,128]{2,1,0:T(8,128)} %get-tuple-element.31), calls=%async_computation.1 | async-start | bytes 1048576 | tf_op jit(solution)/shard_map/all_to_all | solution.py:334
  85.5 3.4 %collective-permute-start.9 = (f32[1024,128]{1,0:T(8,128)S(1)}, f32[1024,128]{1,0:T(8,128)S(1)}, u32[]{:S(2)}, u32[]{:S(2)}) collective-permute-start(f32[1024,128]{1,0:T(8,128)S(1)} %get-tuple-element.36), channel_id=1, source_target_pairs={{0,1},{2,3},{4,5},{6,7},{8,9},{10,11},{12,13},{14,15},{16,17},{18,... | collective-permute-start | bytes 1572872 | tf_op jit(solution)/shard_map/ppermute | solution.py:298
  89.0 14.1 %collective-permute-start.11 = (f32[1024,128]{1,0:T(8,128)S(1)}, f32[1024,128]{1,0:T(8,128)S(1)}, u32[]{:S(2)}, u32[]{:S(2)}) collective-permute-start(f32[1024,128]{1,0:T(8,128)S(1)} %get-tuple-element.36), channel_id=1, source_target_pairs={{1,2},{3,4},{5,6},{7,8},{9,10},{11,12},{13,14},{15,16},{17,18},{19... | collective-permute-start | bytes 1572872 | tf_op jit(solution)/shard_map/ppermute | solution.py:298
  90.3 15.0 %collective-permute-start.10 = (f32[1024,128]{1,0:T(8,128)S(1)}, f32[1024,128]{1,0:T(8,128)S(1)}, u32[]{:S(2)}, u32[]{:S(2)}) collective-permute-start(f32[1024,128]{1,0:T(8,128)S(1)} %add.37), channel_id=1, source_target_pairs={{0,30},{1,143},{2,0},{3,1},{4,2},{5,3},{6,4},{7,5},{8,6},{9,7},{10... | collective-permute-start | bytes 1572872 | tf_op jit(solution)/shard_map/ppermute | solution.py:286
  94.4 10.9 %collective-permute-start.12 = (f32[1024,128]{1,0:T(8,128)S(1)}, f32[1024,128]{1,0:T(8,128)S(1)}, u32[]{:S(2)}, u32[]{:S(2)}) collective-permute-start(f32[1024,128]{1,0:T(8,128)S(1)} %shard_map.91), channel_id=1, source_target_pairs={{1,0},{0,1},{3,2},{2,3},{5,4},{4,5},{7,6},{6,7},{9,8},{8,9},{11,10... | collective-permute-start | bytes 1572872 | tf_op jit(solution)/shard_map/ppermute | solution.py:349
  105.4 5.9 %collective-permute-start.14 = (f32[256,128]{1,0:T(8,128)S(1)}, f32[256,128]{1,0:T(8,128)S(1)}, u32[]{:S(2)}, u32[]{:S(2)}) collective-permute-start(f32[256,128]{1,0:T(8,128)S(1)} %get-tuple-element.38), channel_id=1, source_target_pairs={{0,64},{32,96},{64,0},{96,32},{128,192},{160,224},{192,128},{224,1... | collective-permute-start | bytes 393224 | tf_op jit(solution)/shard_map/ppermute | solution.py:355
  105.6 9.0 %collective-permute-start.18 = (f32[256,128]{1,0:T(8,128)S(1)}, f32[256,128]{1,0:T(8,128)S(1)}, u32[]{:S(2)}, u32[]{:S(2)}) collective-permute-start(f32[256,128]{1,0:T(8,128)S(1)} %get-tuple-element.39), channel_id=1, source_target_pairs={{0,224},{32,192},{64,160},{96,128},{128,96},{160,64},{192,32},{224... | collective-permute-start | bytes 393224 | tf_op jit(solution)/shard_map/ppermute | solution.py:355
  108.3 8.5 %collective-permute-start.16 = (f32[256,128]{1,0:T(8,128)S(1)}, f32[256,128]{1,0:T(8,128)S(1)}, u32[]{:S(2)}, u32[]{:S(2)}) collective-permute-start(f32[256,128]{1,0:T(8,128)S(1)} %get-tuple-element.40), channel_id=1, source_target_pairs={{0,160},{32,128},{64,224},{96,192},{128,32},{160,0},{192,96},{224,... | collective-permute-start | bytes 393224 | tf_op jit(solution)/shard_map/ppermute | solution.py:355
  110.5 7.1 %collective-permute-start.13 = (f32[256,128]{1,0:T(8,128)S(1)}, f32[256,128]{1,0:T(8,128)S(1)}, u32[]{:S(2)}, u32[]{:S(2)}) collective-permute-start(f32[256,128]{1,0:T(8,128)S(1)} %get-tuple-element.41), channel_id=1, source_target_pairs={{0,2},{1,3},{2,4},{3,5},{4,6},{5,7},{6,8},{7,9},{8,10},{9,11},{10,... | collective-permute-start | bytes 393224 | tf_op jit(solution)/shard_map/ppermute | solution.py:286
  111.3 13.0 %collective-permute-start.15 = (f32[256,128]{1,0:T(8,128)S(1)}, f32[256,128]{1,0:T(8,128)S(1)}, u32[]{:S(2)}, u32[]{:S(2)}) collective-permute-start(f32[256,128]{1,0:T(8,128)S(1)} %collective-permute-done.14), channel_id=1, source_target_pairs={{0,10},{1,11},{2,12},{3,13},{4,14},{5,15},{6,16},{7,17},{8,18},{9,... | collective-permute-start | bytes 393224 | tf_op jit(solution)/shard_map/ppermute | solution.py:286
  114.6 13.5 %collective-permute-start.19 = (f32[256,128]{1,0:T(8,128)S(1)}, f32[256,128]{1,0:T(8,128)S(1)}, u32[]{:S(2)}, u32[]{:S(2)}) collective-permute-start(f32[256,128]{1,0:T(8,128)S(1)} %collective-permute-done.18), channel_id=1, source_target_pairs={{0,30},{1,31},{2,0},{3,1},{4,2},{5,3},{6,4},{7,5},{8,6},{9,7},{10,... | collective-permute-start | bytes 393224 | tf_op jit(solution)/shard_map/ppermute | solution.py:286
  116.8 14.6 %collective-permute-start.17 = (f32[256,128]{1,0:T(8,128)S(1)}, f32[256,128]{1,0:T(8,128)S(1)}, u32[]{:S(2)}, u32[]{:S(2)}) collective-permute-start(f32[256,128]{1,0:T(8,128)S(1)} %collective-permute-done.16), channel_id=1, source_target_pairs={{0,22},{1,23},{2,24},{3,25},{4,26},{5,27},{6,28},{7,29},{8,30},{9,... | collective-permute-start | bytes 393224 | tf_op jit(solution)/shard_map/ppermute | solution.py:286
  131.4 4.4 %collective-permute-start.20 = (f32[128,128]{1,0:T(8,128)S(1)}, f32[128,128]{1,0:T(8,128)S(1)}, u32[]{:S(2)}, u32[]{:S(2)}) collective-permute-start(f32[128,128]{1,0:T(8,128)S(1)} %split.9), channel_id=1, source_target_pairs={{32,0},{0,32},{96,64},{64,96},{160,128},{128,160},{224,192},{192,2... | collective-permute-start | bytes 196616 | tf_op jit(solution)/shard_map/ppermute | solution.py:360

commit v9 on v6

--- a/solution.py
+++ b/solution.py
@@ -334,7 +334,7 @@
     total = received + lax.ppermute(other, "blk", swap)
     parts = total.reshape(replicas // 2, -1, own.shape[-1])
     pair_sum = 0.0
-    for k in range(replicas // 2):
+    for k in reversed(range(replicas // 2)):
         part, across = parts[k], (2 * k) ^ (k >> 1)
         if k:
             part = lax.ppermute(part, "rep", [(r, r ^ across) for r in range(replicas)])

time: 138 us -> 140 us (1.014)
  the two profiles are of different devices: /device:TPU:26 before, /device:TPU:64 now
where the time goes in v9:
time: 140 us; the launch traced here: 139 us
  starting transfers between devices  45.9 us (33%)
  waiting for transfers between devices  43.2 us (31%)
  Pallas kernels  26.4 us (19%)
  blocking collectives  19.1 us (14%)
  other arithmetic  2.64 us (2%)
    pallas_call x9, Pallas kernels, local_call(): pl.pallas_call(body, in_specs=[pl.BlockSpec(memory_space=pltpu.SMEM)] + [...  25.2 us
    ppermute x5, starting transfers between devices, joint(): lax.ppermute(block, ('rep', 'blk'), [(device(*source(g, r)), device(g, r)...  20 us
    ppermute x5, waiting for transfers between devices, back(): lax.ppermute(block, ('rep', 'blk'), [(device(g, r), device(*target(g, r))...  19.5 us
    all_to_all x1, blocking collectives, shards(): lax.all_to_all(partial_sum.reshape(replicas, -1, own.shape[-1]), 'rep', 0...  19.1 us
    ppermute x5, starting transfers between devices, back(): lax.ppermute(block, ('rep', 'blk'), [(device(g, r), device(*target(g, r))...  9.53 us
    all_to_all x1, waiting for transfers between devices, shards(): lax.all_to_all(spread, 'rep', 0, 0, tiled=True).reshape(base.shape)  7.21 us
    ppermute x5, waiting for transfers between devices, joint(): lax.ppermute(block, ('rep', 'blk'), [(device(*source(g, r)), device(g, r)...  6.95 us
    ppermute x4, starting transfers between devices, along(): lax.ppermute(block, 'blk', [(g, (g + distance) % groups) for g in ids])  5.21 us
  transfers between devices with their start and end apart: 22, of which 11 were waited for; matrix products, arithmetic and copies ran while one was open for 2% of the time, Pallas kernels for 15%

profile of v9, /device:TPU:64, one launch (start us, length us, event | category | flops | bytes accessed | tf_op | source)
XLA Modules:
  0.0 139.1 jit_solution(17399073913964097024)
XLA Ops:
  5.3 8.4 %collective-permute-start.2 = (f32[256,128]{1,0:T(8,128)S(1)}, f32[256,128]{1,0:T(8,128)S(1)}, u32[]{:S(2)}, u32[]{:S(2)}) collective-permute-start(f32[256,128]{1,0:T(8,128)S(1)} %constant_dynamic-update-slice_fusion), channel_id=1, source_target_pairs={{66,0},{67,1},{68,2},{69,3},{70,4},{71,5},{72,6},{73,7},{74,8},{75... | collective-permute-start | bytes 393224 | tf_op jit(solution)/shard_map/ppermute | solution.py:267
  13.7 4.3 %collective-permute-start.3 = (f32[256,128]{1,0:T(8,128)S(1)}, f32[256,128]{1,0:T(8,128)S(1)}, u32[]{:S(2)}, u32[]{:S(2)}) collective-permute-start(f32[256,128]{1,0:T(8,128)S(1)} %constant_dynamic-update-slice_fusion), channel_id=1, source_target_pairs={{130,0},{131,1},{132,2},{133,3},{134,4},{135,5},{136,6},{137,7},{1... | collective-permute-start | bytes 393224 | tf_op jit(solution)/shard_map/ppermute | solution.py:267
  18.0 3.6 %collective-permute-start.4 = (f32[256,128]{1,0:T(8,128)S(1)}, f32[256,128]{1,0:T(8,128)S(1)}, u32[]{:S(2)}, u32[]{:S(2)}) collective-permute-start(f32[256,128]{1,0:T(8,128)S(1)} %constant_dynamic-update-slice_fusion), channel_id=1, source_target_pairs={{194,0},{195,1},{196,2},{197,3},{198,4},{199,5},{200,6},{201,7},{2... | collective-permute-start | bytes 393224 | tf_op jit(solution)/shard_map/ppermute | solution.py:267
  21.6 3.1 %shard_map.86 = (bf16[32,128,256]{2,1,0:T(8,128)(2,1)S(1)}, bf16[32,128,256]{2,1,0:T(8,128)(2,1)S(1)}) custom-call(s32[17,32]{1,0:T(8,128)S(1)} %concatenate.10.info, f32[4,32,128,128]{3,2,1,0:T(8,128)} %bitcast.22), custom_call_target="tpu_custom_call" | custom-call | flops 4294967296 | bytes 4194304 | tf_op jit(solution)/shard_map/pallas_call | solution.py:146
  25.5 3.6 %collective-permute-start.5 = (f32[1024,128]{1,0:T(8,128)S(1)}, f32[1024,128]{1,0:T(8,128)S(1)}, u32[]{:S(2)}, u32[]{:S(2)}) collective-permute-start(f32[1024,128]{1,0:T(8,128)S(1)} %pad_maximum_fusion.refs_0_), channel_id=1, source_target_pairs={{30,0},{143,1},{0,2},{1,3},{2,4},{3,5},{4,6},{5,7},{6,8},{7,9},{8,... | collective-permute-start | bytes 1572872 | tf_op jit(solution)/shard_map/ppermute | solution.py:267
  30.3 4.1 %shard_map.87.refs_2_ = f32[1024,128]{1,0:T(8,128)S(1)} custom-call(s32[17,32]{1,0:T(8,128)S(1)} %concatenate.10.info, f32[1024,128]{1,0:T(8,128)S(1)} %pad_maximum_fusion.refs_0_, f32[1024,128]{1,0:T(8,128)S(1)} %collective-permute-done.6.refs_1_, f32[4,32,128,128]{3,2,1,0:T(8,128)} %bitcast.23), custom_call_target="tpu_custom_call" | custom-call | flops 4294967296 | bytes 4194304 | tf_op jit(solution)/shard_map/pallas_call | solution.py:146
  34.4 6.4 %collective-permute-done.5.refs_0_ = f32[1024,128]{1,0:T(8,128)S(1)} collective-permute-done((f32[1024,128]{1,0:T(8,128)S(1)}, f32[1024,128]{1,0:T(8,128)S(1)}, u32[]{:S(2)}, u32[]{:S(2)}) %collective-permute-start.5) | collective-permute-done | bytes 524320 | tf_op jit(solution)/shard_map/ppermute | solution.py:267
  42.1 2.1 %shard_map.88.refs_3_ = f32[1024,128]{1,0:T(8,128)S(1)} custom-call(s32[17,32]{1,0:T(8,128)S(1)} %concatenate.10.info, f32[1024,128]{1,0:T(8,128)S(1)} %collective-permute-done.5.refs_0_, bf16[32,128,256]{2,1,0:T(8,128)(2,1)S(1)} %get-tuple-element.25.refs_1_, f32[1024,128]{1,0:T(8,128)S(1)} %shard_map.87.refs_2_), custom_call_target="tpu_custom_call" | custom-call | flops 2147483648 | bytes 2097152 | tf_op jit(solution)/shard_map/pallas_call | solution.py:146
  44.6 2.1 %shard_map.89 = f32[1024,128]{1,0:T(8,128)S(1)} custom-call(s32[17,32]{1,0:T(8,128)S(1)} %concatenate.10.info, f32[1024,128]{1,0:T(8,128)S(1)} %collective-permute-done.7.refs_0_, f32[1024,128]{1,0:T(8,128)S(1)} %collective-permute-done.8.refs_1_, bf16[32,128,256]{2,1,0:T(8,128)(2,1)S(1)} %get-tuple-element.24.refs_2_, f32[1024,128]{1,0:T(8,128)S(1)} %shard_map.88.refs_3_), custom_call_target="tpu_custom_call" | custom-call | flops 2147483648 | bytes 2097152 | tf_op jit(solution)/shard_map/pallas_call | solution.py:146
  46.7 19.1 %all_to_all.10.partials = f32[8,128,128]{2,1,0:T(8,128)S(1)} all-to-all(f32[8,128,128]{2,1,0:T(8,128)S(1)} %bitcast.20), channel_id=1, replica_groups=mesh['rep'=8,'blk'=32] {'rep'}, dimensions={0} | all-to-all | bytes 1048576 | tf_op jit(solution)/shard_map/all_to_all | solution.py:317
  67.0 3.5 %all-to-all-start.1 = ((f32[8,128,128]{2,1,0:T(8,128)}), f32[8,128,128]{2,1,0:T(8,128)S(1)}, u32[]{:S(2)}, u32[]{:S(2)}) async-start(f32[8,128,128]{2,1,0:T(8,128)} %get-tuple-element.29), calls=%async_computation.1 | async-start | bytes 1048576 | tf_op jit(solution)/shard_map/all_to_all | solution.py:321
  70.5 2.7 %shard_map.94.tiles = bf16[32,128,256]{2,1,0:T(8,128)(2,1)S(1)} custom-call(s32[17,32]{1,0:T(8,128)S(1)} %concatenate.10.info, f32[4,32,128,128]{3,2,1,0:T(8,128)} %bitcast.24), custom_call_target="tpu_custom_call" | custom-call | flops 2147483648 | bytes 2097152 | tf_op jit(solution)/shard_map/pallas_call | solution.py:146
  73.2 7.2 %all-to-all-done.1 = f32[8,128,128]{2,1,0:T(8,128)S(1)} async-done(((f32[8,128,128]{2,1,0:T(8,128)}), f32[8,128,128]{2,1,0:T(8,128)S(1)}, u32[]{:S(2)}, u32[]{:S(2)}) %all-to-all-start.1) | async-done | bytes 524320 | tf_op jit(solution)/shard_map/all_to_all | solution.py:321
  83.7 3.1 %shard_map.93 = f32[1024,128]{1,0:T(8,128)S(1)} custom-call(s32[17,32]{1,0:T(8,128)S(1)} %concatenate.10.info, f32[1024,128]{1,0:T(8,128)S(1)} %bitcast.17, f32[4,32,128,128]{3,2,1,0:T(8,128)} %bitcast.25), custom_call_target="tpu_custom_call" | custom-call | flops 2147483648 | bytes 2097152 | tf_op jit(solution)/shard_map/pallas_call | solution.py:146
  88.2 2.0 %collective-permute-start.10 = (f32[1024,128]{1,0:T(8,128)S(1)}, f32[1024,128]{1,0:T(8,128)S(1)}, u32[]{:S(2)}, u32[]{:S(2)}) collective-permute-start(f32[1024,128]{1,0:T(8,128)S(1)} %add.37), channel_id=1, source_target_pairs={{0,30},{1,143},{2,0},{3,1},{4,2},{5,3},{6,4},{7,5},{8,6},{9,7},{10... | collective-permute-start | bytes 1572872 | tf_op jit(solution)/shard_map/ppermute | solution.py:273
  90.2 3.1 %shard_map.91 = f32[1024,128]{1,0:T(8,128)S(1)} custom-call(s32[17,32]{1,0:T(8,128)S(1)} %concatenate.10.info, f32[1024,128]{1,0:T(8,128)S(1)} %bitcast.18, f32[4,32,128,128]{3,2,1,0:T(8,128)} %bitcast.26), custom_call_target="tpu_custom_call" | custom-call | flops 2147483648 | bytes 2097152 | tf_op jit(solution)/shard_map/pallas_call | solution.py:146
  94.1 3.1 %shard_map.92 = f32[1024,128]{1,0:T(8,128)S(1)} custom-call(s32[17,32]{1,0:T(8,128)S(1)} %concatenate.10.info, f32[1024,128]{1,0:T(8,128)S(1)} %bitcast.19, f32[4,32,128,128]{3,2,1,0:T(8,128)} %bitcast.27), custom_call_target="tpu_custom_call" | custom-call | flops 2147483648 | bytes 2097152 | tf_op jit(solution)/shard_map/pallas_call | solution.py:146
  97.4 5.1 %collective-permute-done.10 = f32[1024,128]{1,0:T(8,128)S(1)} collective-permute-done((f32[1024,128]{1,0:T(8,128)S(1)}, f32[1024,128]{1,0:T(8,128)S(1)}, u32[]{:S(2)}, u32[]{:S(2)}) %collective-permute-start.10) | collective-permute-done | bytes 524320 | tf_op jit(solution)/shard_map/ppermute | solution.py:273
  107.9 4.3 %collective-permute-done.13 = f32[256,128]{1,0:T(8,128)S(1)} collective-permute-done((f32[256,128]{1,0:T(8,128)S(1)}, f32[256,128]{1,0:T(8,128)S(1)}, u32[]{:S(2)}, u32[]{:S(2)}) %collective-permute-start.13) | collective-permute-done | bytes 131104 | tf_op jit(solution)/shard_map/ppermute | solution.py:340
  112.2 2.4 %collective-permute-start.14 = (f32[256,128]{1,0:T(8,128)S(1)}, f32[256,128]{1,0:T(8,128)S(1)}, u32[]{:S(2)}, u32[]{:S(2)}) collective-permute-start(f32[256,128]{1,0:T(8,128)S(1)} %collective-permute-done.13), channel_id=1, source_target_pairs={{0,30},{1,31},{2,0},{3,1},{4,2},{5,3},{6,4},{7,5},{8,6},{9,7},{10,... | collective-permute-start | bytes 393224 | tf_op jit(solution)/shard_map/ppermute | solution.py:273
  114.6 4.5 %collective-permute-start.16 = (f32[256,128]{1,0:T(8,128)S(1)}, f32[256,128]{1,0:T(8,128)S(1)}, u32[]{:S(2)}, u32[]{:S(2)}) collective-permute-start(f32[256,128]{1,0:T(8,128)S(1)} %collective-permute-done.15), channel_id=1, source_target_pairs={{0,22},{1,23},{2,24},{3,25},{4,26},{5,27},{6,28},{7,29},{8,30},{9,... | collective-permute-start | bytes 393224 | tf_op jit(solution)/shard_map/ppermute | solution.py:273
  119.6 5.6 %collective-permute-done.16 = f32[256,128]{1,0:T(8,128)S(1)} collective-permute-done((f32[256,128]{1,0:T(8,128)S(1)}, f32[256,128]{1,0:T(8,128)S(1)}, u32[]{:S(2)}, u32[]{:S(2)}) %collective-permute-start.16) | collective-permute-done | bytes 131104 | tf_op jit(solution)/shard_map/ppermute | solution.py:273
  125.2 8.9 %collective-permute-done.18 = f32[256,128]{1,0:T(8,128)S(1)} collective-permute-done((f32[256,128]{1,0:T(8,128)S(1)}, f32[256,128]{1,0:T(8,128)S(1)}, u32[]{:S(2)}, u32[]{:S(2)}) %collective-permute-start.18) | collective-permute-done | bytes 131104 | tf_op jit(solution)/shard_map/ppermute | solution.py:273
  134.2 4.3 %collective-permute-done.20 = f32[128,128]{1,0:T(8,128)S(1)} collective-permute-done((f32[128,128]{1,0:T(8,128)S(1)}, f32[128,128]{1,0:T(8,128)S(1)}, u32[]{:S(2)}, u32[]{:S(2)}) %collective-permute-start.20) | collective-permute-done | bytes 65568 | tf_op jit(solution)/shard_map/ppermute | solution.py:345
  (49 shorter events, 22.0 us)
Async XLA Ops:
  0.6 4.6 %collective-permute-start = (f32[128,128]{1,0:T(8,128)}, f32[128,128]{1,0:T(8,128)S(1)}, u32[]{:S(2)}, u32[]{:S(2)}) collective-permute-start(f32[128,128]{1,0:T(8,128)} %bitcast.28), channel_id=1, source_target_pairs={{32,0},{0,32},{96,64},{64,96},{160,128},{128,160},{224,192},{192,2... | collective-permute-start | bytes 196616 | tf_op jit(solution)/shard_map/ppermute | solution.py:294
  5.2 19.5 %collective-permute-start.1 = (f32[256,128]{1,0:T(8,128)S(1)}, f32[256,128]{1,0:T(8,128)S(1)}, u32[]{:S(2)}, u32[]{:S(2)}) collective-permute-start(f32[256,128]{1,0:T(8,128)S(1)} %constant_dynamic-update-slice_fusion), channel_id=1, source_target_pairs={{2,0},{3,1},{4,2},{5,3},{6,4},{7,5},{8,6},{9,7},{10,8},{11,9},{12,... | collective-permute-start | bytes 393224 | tf_op jit(solution)/shard_map/ppermute | solution.py:267
  5.3 19.4 %collective-permute-start.2 = (f32[256,128]{1,0:T(8,128)S(1)}, f32[256,128]{1,0:T(8,128)S(1)}, u32[]{:S(2)}, u32[]{:S(2)}) collective-permute-start(f32[256,128]{1,0:T(8,128)S(1)} %constant_dynamic-update-slice_fusion), channel_id=1, source_target_pairs={{66,0},{67,1},{68,2},{69,3},{70,4},{71,5},{72,6},{73,7},{74,8},{75... | collective-permute-start | bytes 393224 | tf_op jit(solution)/shard_map/ppermute | solution.py:267
  13.7 11.0 %collective-permute-start.3 = (f32[256,128]{1,0:T(8,128)S(1)}, f32[256,128]{1,0:T(8,128)S(1)}, u32[]{:S(2)}, u32[]{:S(2)}) collective-permute-start(f32[256,128]{1,0:T(8,128)S(1)} %constant_dynamic-update-slice_fusion), channel_id=1, source_target_pairs={{130,0},{131,1},{132,2},{133,3},{134,4},{135,5},{136,6},{137,7},{1... | collective-permute-start | bytes 393224 | tf_op jit(solution)/shard_map/ppermute | solution.py:267
  18.0 7.3 %collective-permute-start.4 = (f32[256,128]{1,0:T(8,128)S(1)}, f32[256,128]{1,0:T(8,128)S(1)}, u32[]{:S(2)}, u32[]{:S(2)}) collective-permute-start(f32[256,128]{1,0:T(8,128)S(1)} %constant_dynamic-update-slice_fusion), channel_id=1, source_target_pairs={{194,0},{195,1},{196,2},{197,3},{198,4},{199,5},{200,6},{201,7},{2... | collective-permute-start | bytes 393224 | tf_op jit(solution)/shard_map/ppermute | solution.py:267
  25.4 5.0 %collective-permute-start.6 = (f32[1024,128]{1,0:T(8,128)S(1)}, f32[1024,128]{1,0:T(8,128)S(1)}, u32[]{:S(2)}, u32[]{:S(2)}) collective-permute-start(f32[1024,128]{1,0:T(8,128)S(1)} %pad_maximum_fusion.refs_0_), channel_id=1, source_target_pairs={{1,0},{0,1},{3,2},{2,3},{5,4},{4,5},{7,6},{6,7},{9,8},{8,9},{11,10... | collective-permute-start | bytes 1572872 | tf_op jit(solution)/shard_map/ppermute | solution.py:307
  25.5 15.3 %collective-permute-start.5 = (f32[1024,128]{1,0:T(8,128)S(1)}, f32[1024,128]{1,0:T(8,128)S(1)}, u32[]{:S(2)}, u32[]{:S(2)}) collective-permute-start(f32[1024,128]{1,0:T(8,128)S(1)} %pad_maximum_fusion.refs_0_), channel_id=1, source_target_pairs={{30,0},{143,1},{0,2},{1,3},{2,4},{3,5},{4,6},{5,7},{6,8},{7,9},{8,... | collective-permute-start | bytes 1572872 | tf_op jit(solution)/shard_map/ppermute | solution.py:267
  29.0 15.2 %collective-permute-start.8 = (f32[1024,128]{1,0:T(8,128)S(1)}, f32[1024,128]{1,0:T(8,128)S(1)}, u32[]{:S(2)}, u32[]{:S(2)}) collective-permute-start(f32[1024,128]{1,0:T(8,128)S(1)} %pad_maximum_fusion.refs_0_), channel_id=1, source_target_pairs={{0,31},{2,1},{4,3},{6,5},{8,7},{10,9},{12,11},{14,13},{16,15},{18,... | collective-permute-start | bytes 1572872 | tf_op jit(solution)/shard_map/ppermute | solution.py:285
  40.8 3.8 %collective-permute-start.7 = (f32[1024,128]{1,0:T(8,128)S(1)}, f32[1024,128]{1,0:T(8,128)S(1)}, u32[]{:S(2)}, u32[]{:S(2)}) collective-permute-start(f32[1024,128]{1,0:T(8,128)S(1)} %collective-permute-done.5.refs_0_), channel_id=1, source_target_pairs={{1,0},{3,2},{5,4},{7,6},{9,8},{11,10},{13,12},{15,14},{17,16},{19,... | collective-permute-start | bytes 1572872 | tf_op jit(solution)/shard_map/ppermute | solution.py:285
  44.2 21.7 %copy-start = (f32[128,256]{1,0:T(8,128)S(1)}, f32[128,256]{1,0:T(8,128)}, u32[]{:S(2)}) copy-start(f32[128,256]{1,0:T(8,128)} %weight.1) | copy-start | bytes 393220
  44.2 21.6 %copy-start.1 = (f32[1,128,256]{2,1,0:T(8,128)S(1)}, f32[1,128,256]{2,1,0:T(8,128)}, u32[]{:S(2)}) copy-start(f32[1,128,256]{2,1,0:T(8,128)} %param.9) | copy-start | bytes 393220
  67.0 13.4 %all-to-all-start.1 = ((f32[8,128,128]{2,1,0:T(8,128)}), f32[8,128,128]{2,1,0:T(8,128)S(1)}, u32[]{:S(2)}, u32[]{:S(2)}) async-start(f32[8,128,128]{2,1,0:T(8,128)} %get-tuple-element.29), calls=%async_computation.1 | async-start | bytes 1048576 | tf_op jit(solution)/shard_map/all_to_all | solution.py:321
  82.4 4.4 %collective-permute-start.9 = (f32[1024,128]{1,0:T(8,128)S(1)}, f32[1024,128]{1,0:T(8,128)S(1)}, u32[]{:S(2)}, u32[]{:S(2)}) collective-permute-start(f32[1024,128]{1,0:T(8,128)S(1)} %shard_map.95), channel_id=1, source_target_pairs={{0,1},{2,3},{4,5},{6,7},{8,9},{10,11},{12,13},{14,15},{16,17},{18,... | collective-permute-start | bytes 1572872 | tf_op jit(solution)/shard_map/ppermute | solution.py:285
  86.9 10.5 %collective-permute-start.11 = (f32[1024,128]{1,0:T(8,128)S(1)}, f32[1024,128]{1,0:T(8,128)S(1)}, u32[]{:S(2)}, u32[]{:S(2)}) collective-permute-start(f32[1024,128]{1,0:T(8,128)S(1)} %shard_map.95), channel_id=1, source_target_pairs={{1,2},{3,4},{5,6},{7,8},{9,10},{11,12},{13,14},{15,16},{17,18},{19... | collective-permute-start | bytes 1572872 | tf_op jit(solution)/shard_map/ppermute | solution.py:285
  88.2 14.3 %collective-permute-start.10 = (f32[1024,128]{1,0:T(8,128)S(1)}, f32[1024,128]{1,0:T(8,128)S(1)}, u32[]{:S(2)}, u32[]{:S(2)}) collective-permute-start(f32[1024,128]{1,0:T(8,128)S(1)} %add.37), channel_id=1, source_target_pairs={{0,30},{1,143},{2,0},{3,1},{4,2},{5,3},{6,4},{7,5},{8,6},{9,7},{10... | collective-permute-start | bytes 1572872 | tf_op jit(solution)/shard_map/ppermute | solution.py:273
  93.3 9.3 %collective-permute-start.12 = (f32[1024,128]{1,0:T(8,128)S(1)}, f32[1024,128]{1,0:T(8,128)S(1)}, u32[]{:S(2)}, u32[]{:S(2)}) collective-permute-start(f32[1024,128]{1,0:T(8,128)S(1)} %shard_map.91), channel_id=1, source_target_pairs={{1,0},{0,1},{3,2},{2,3},{5,4},{4,5},{7,6},{6,7},{9,8},{8,9},{11,10... | collective-permute-start | bytes 1572872 | tf_op jit(solution)/shard_map/ppermute | solution.py:334
  102.7 9.5 %collective-permute-start.13 = (f32[256,128]{1,0:T(8,128)S(1)}, f32[256,128]{1,0:T(8,128)S(1)}, u32[]{:S(2)}, u32[]{:S(2)}) collective-permute-start(f32[256,128]{1,0:T(8,128)S(1)} %get-tuple-element.37), channel_id=1, source_target_pairs={{0,224},{32,192},{64,160},{96,128},{128,96},{160,64},{192,32},{224... | collective-permute-start | bytes 393224 | tf_op jit(solution)/shard_map/ppermute | solution.py:340
  104.2 10.3 %collective-permute-start.15 = (f32[256,128]{1,0:T(8,128)S(1)}, f32[256,128]{1,0:T(8,128)S(1)}, u32[]{:S(2)}, u32[]{:S(2)}) collective-permute-start(f32[256,128]{1,0:T(8,128)S(1)} %get-tuple-element.34), channel_id=1, source_target_pairs={{0,160},{32,128},{64,224},{96,192},{128,32},{160,0},{192,96},{224,... | collective-permute-start | bytes 393224 | tf_op jit(solution)/shard_map/ppermute | solution.py:340
  105.8 13.2 %collective-permute-start.17 = (f32[256,128]{1,0:T(8,128)S(1)}, f32[256,128]{1,0:T(8,128)S(1)}, u32[]{:S(2)}, u32[]{:S(2)}) collective-permute-start(f32[256,128]{1,0:T(8,128)S(1)} %get-tuple-element.36), channel_id=1, source_target_pairs={{0,64},{32,96},{64,0},{96,32},{128,192},{160,224},{192,128},{224,1... | collective-permute-start | bytes 393224 | tf_op jit(solution)/shard_map/ppermute | solution.py:340
  107.8 11.8 %collective-permute-start.19 = (f32[256,128]{1,0:T(8,128)S(1)}, f32[256,128]{1,0:T(8,128)S(1)}, u32[]{:S(2)}, u32[]{:S(2)}) collective-permute-start(f32[256,128]{1,0:T(8,128)S(1)} %get-tuple-element.35), channel_id=1, source_target_pairs={{0,2},{1,3},{2,4},{3,5},{4,6},{5,7},{6,8},{7,9},{8,10},{9,11},{10,... | collective-permute-start | bytes 393224 | tf_op jit(solution)/shard_map/ppermute | solution.py:273
  112.2 7.5 %collective-permute-start.14 = (f32[256,128]{1,0:T(8,128)S(1)}, f32[256,128]{1,0:T(8,128)S(1)}, u32[]{:S(2)}, u32[]{:S(2)}) collective-permute-start(f32[256,128]{1,0:T(8,128)S(1)} %collective-permute-done.13), channel_id=1, source_target_pairs={{0,30},{1,31},{2,0},{3,1},{4,2},{5,3},{6,4},{7,5},{8,6},{9,7},{10,... | collective-permute-start | bytes 393224 | tf_op jit(solution)/shard_map/ppermute | solution.py:273
  114.6 10.6 %collective-permute-start.16 = (f32[256,128]{1,0:T(8,128)S(1)}, f32[256,128]{1,0:T(8,128)S(1)}, u32[]{:S(2)}, u32[]{:S(2)}) collective-permute-start(f32[256,128]{1,0:T(8,128)S(1)} %collective-permute-done.15), channel_id=1, source_target_pairs={{0,22},{1,23},{2,24},{3,25},{4,26},{5,27},{6,28},{7,29},{8,30},{9,... | collective-permute-start | bytes 393224 | tf_op jit(solution)/shard_map/ppermute | solution.py:273
  119.0 15.0 %collective-permute-start.18 = (f32[256,128]{1,0:T(8,128)S(1)}, f32[256,128]{1,0:T(8,128)S(1)}, u32[]{:S(2)}, u32[]{:S(2)}) collective-permute-start(f32[256,128]{1,0:T(8,128)S(1)} %collective-permute-done.17), channel_id=1, source_target_pairs={{0,10},{1,11},{2,12},{3,13},{4,14},{5,15},{6,16},{7,17},{8,18},{9,... | collective-permute-start | bytes 393224 | tf_op jit(solution)/shard_map/ppermute | solution.py:273
  134.1 4.4 %collective-permute-start.20 = (f32[128,128]{1,0:T(8,128)S(1)}, f32[128,128]{1,0:T(8,128)S(1)}, u32[]{:S(2)}, u32[]{:S(2)}) collective-permute-start(f32[128,128]{1,0:T(8,128)S(1)} %split.9), channel_id=1, source_target_pairs={{32,0},{0,32},{96,64},{64,96},{160,128},{128,160},{224,192},{192,2... | collective-permute-start | bytes 196616 | tf_op jit(solution)/shard_map/ppermute | solution.py:345
